TPU v7x, 128 devices: a whole 4x4x4 slice. The times are simulated.
128 devices in a mesh: row: 8 (over x, core), col: 8 (over y, z_lo), seg: 2 (over z_hi).
Axes of the slice: x: 4, y: 4, z: 4 (z_hi: 2, z_lo: 2; z = z_hi * 2 + z_lo), core: 2. Of those that a mesh axis runs over, the one named last changes fastest.
Arguments:
- traces: float32 [64, 1024, 2000], P('seg', ('row', 'col')), may hold values from -100 to 100
- channel_alive: int32 [1024], P(('row', 'col')), may hold values 0 or 1
Outputs:
- stacks: float32 [1024, 1024, 401], P('row', ('col', 'seg'))
All inputs are finite; a program needn't handle non-finite values. No bound on the sum of `channel_alive` on one device may be relied on, other than what follows from the above.
Results may differ from a plain program's by a relative error of at most 0.0028.
Values may be sent and summed in bfloat16 or wider, within the bound.
No kernel may reach another device: no remote copies, remote signals or barrier semaphores. Data moves between devices by JAX's collectives and lax.ppermute only.
A program may use at most 192 MiB of HBM per device.

v0:
```python
import math

import jax
import jax.numpy as jnp
from jax import lax
from jax.sharding import PartitionSpec as P

NF = 192
F_LO = 8
MAXLAG = 200
SMOOTH = 5


def spread(shard, axis, root):
    mine = lax.axis_index(axis) == root
    return lax.psum(jnp.where(mine, shard, jnp.zeros_like(shard)), axis)


def forward_table(samples):
    times = jnp.arange(samples, dtype=jnp.int32)
    freqs = F_LO + jnp.arange(NF, dtype=jnp.int32)
    phase = jnp.mod(times[:, None] * freqs[None, :], samples).astype(jnp.float32) * (
        2.0 * math.pi / samples
    )
    window_taper = 0.5 - 0.5 * jnp.cos(
        (times.astype(jnp.float32) + 0.5) * (2.0 * math.pi / samples)
    )
    return jnp.concatenate(
        [window_taper[:, None] * jnp.cos(phase), -window_taper[:, None] * jnp.sin(phase)], axis=1
    )


def inverse_table(samples, segments):
    freqs = F_LO + jnp.arange(NF, dtype=jnp.int32)
    shifts = jnp.arange(2 * MAXLAG + 1, dtype=jnp.int32) - MAXLAG
    phase = jnp.mod(freqs[:, None] * shifts[None, :], samples).astype(jnp.float32) * (
        2.0 * math.pi / samples
    )
    scale_factor = 1.0 / math.sqrt(NF * segments)
    return jnp.concatenate([jnp.cos(phase), jnp.sin(phase)], axis=0) * scale_factor


def whiten(real_part, imag_part, alive_mask):
    magnitude = jnp.sqrt(real_part * real_part + imag_part * imag_part)
    index_bins = jnp.arange(NF, dtype=jnp.int32)
    smoothing = (jnp.abs(index_bins[:, None] - index_bins[None, :]) <= SMOOTH).astype(jnp.float32)
    counts = jnp.sum(smoothing, axis=0)
    smooth = jnp.dot(magnitude, smoothing, precision=lax.Precision.HIGHEST) / counts
    water_level = jnp.mean(magnitude, axis=-1, keepdims=True)
    divisor = smooth + 0.05 * water_level + 1e-06
    weight = alive_mask.astype(jnp.float32)[None, :, None] / divisor
    white_real = (real_part * weight).astype(jnp.bfloat16)
    white_imag = (imag_part * weight).astype(jnp.bfloat16)
    return jnp.concatenate([white_real, white_imag], axis=-1)


def cross_spectra(left_spec, right_spec):
    left_real = left_spec[..., :NF]
    left_imag = left_spec[..., NF:]
    stacked_real = jnp.concatenate([left_real, left_imag], axis=0)
    stacked_imag = jnp.concatenate([left_imag, -left_real], axis=0)
    right_both = jnp.concatenate([right_spec[..., :NF], right_spec[..., NF:]], axis=0)
    cross_real = jnp.einsum(
        "sik,sjk->ijk", stacked_real, right_both, preferred_element_type=jnp.float32
    )
    cross_imag = jnp.einsum(
        "sik,sjk->ijk", stacked_imag, right_both, preferred_element_type=jnp.float32
    )
    return jnp.concatenate([cross_real, cross_imag], axis=-1)


def body(traces, channel_alive):
    seg_count, chan_count, samples = traces.shape
    flat_traces = traces.reshape(seg_count * chan_count, samples)
    spectra = jnp.dot(flat_traces, forward_table(samples), precision=lax.Precision.HIGHEST)
    spectra = spectra.reshape(seg_count, chan_count, 2 * NF)
    own_white = whiten(spectra[..., :NF], spectra[..., NF:], channel_alive)
    row_white = lax.all_gather(own_white, "col", axis=1, tiled=True)
    col_white = spread(row_white, "row", lax.axis_index("col"))
    inv_table = inverse_table(samples, seg_count * lax.axis_size("seg"))
    cross_all = cross_spectra(row_white, col_white)
    lagged = jnp.dot(cross_all, inv_table, precision=lax.Precision.HIGHEST)
    stacks = lax.psum_scatter(lagged, "seg", scatter_dimension=1, tiled=True)
    return stacks


def solution(mesh):
    return jax.shard_map(
        body,
        mesh=mesh,
        in_specs=(P("seg", ("row", "col"), None), P(("row", "col"))),
        out_specs=P("row", ("col", "seg"), None),
        check_vma=False,
    )
```

profile of v0, /device:TPU:4, one launch (start us, length us, event | category | flops | bytes accessed | tf_op | source)
XLA Modules:
  0.0 700.9 jit_solution(15009581936183908273)
XLA Ops:
  6.7 0.7 convert_element_type.36
  7.3 8.4 %cosine_multiply_fusion = (f32[2000,192]{1,0:T(8,128)S(1)}, f32[2000,192]{1,0:T(8,128)S(1)}) fusion(s32[192]{0:T(256)S(1)} %iota_add_fusion.1, f32[2000]{0:T(1024)S(1)} %get-tuple-element.18, f32[2000]{0:T(1024)S(1)} %get-tuple-element.19), kind=kLoop, calls=%fused_computation.16 | loop fusion | flops 4224000 | bytes 3088768 | tf_op jit(solution)/shard_map/mul | solution.py:29
  15.7 13.8 %fusion.13 = f32[512,384]{0,1:T(8,128)S(1)} fusion(f32[512,2000]{1,0:T(8,128)} %bitcast.26, f32[2000,192]{1,0:T(8,128)S(1)} %get-tuple-element.17, f32[2000,192]{1,0:T(8,128)S(1)} %get-tuple-element.16), kind=kOutput, calls=%fused_computation.21 | convolution fusion | flops 4719360000 | bytes 7954432 | tf_op jit(solution)/shard_map/dot_general | solution.py:75
  29.8 0.3 fusion.33
  30.2 0.7 multiply_convert_fusion.1
  30.8 0.9 pad_maximum_fusion.3
  31.8 72.9 %all-gather.2.cloned.1.call-done = bf16[32,128,384]{2,1,0:T(8,128)(2,1)} async-done(((bf16[32,16,384]{2,1,0:T(8,128)(2,1)}), bf16[32,128,384]{2,1,0:T(8,128)(2,1)}) %all-gather.2.cloned.1.call-update) | async-done | bytes 3145744 | tf_op jit(solution)/shard_map/all_gather | solution.py:78
  104.7 2.0 broadcast_select_fusion
  106.8 3.0 fusion.28
  109.8 0.8 fusion.39
  110.6 4.1 pad_maximum_fusion.1
  114.7 6.3 copy.9
  121.0 6.4 copy.11
  127.4 46.8 %all-reduce.2.cloned.1.call-done = bf16[32,128,384]{2,1,0:T(8,128)(2,1)} async-done(((bf16[32,128,384]{2,1,0:T(8,128)(2,1)}), bf16[32,128,384]{2,1,0:T(8,128)(2,1)}) %all-reduce.2.cloned.1.call-update) | async-done | bytes 3145744 | tf_op jit(solution)/shard_map/psum | solution.py:16
  174.2 3.5 fusion.40
  177.7 2.7 pad_maximum_fusion
  180.4 7.8 %copy.8 = bf16[64,128,192]{1,0,2:T(8,128)(2,1)S(1)} copy(bf16[64,128,192]{2,1,0:T(8,128)(2,1)} %pad_maximum_fusion) | data formatting | bytes 6291456 | tf_op jit(solution)/shard_map/concatenate | solution.py:62
  188.2 8.6 %fusion.42 = f32[192,128,128]{2,1,0:T(8,128)} fusion(bf16[64,128,192]{1,0,2:T(8,128)(2,1)S(1)} %copy.8, bf16[64,128,192]{1,0,2:T(8,128)(2,1)} %copy.11), kind=kOutput, calls=%fused_computation.62 | convolution fusion | flops 402653184 | bytes 18874368 | tf_op jit(solution)/shard_map/sik,sjk->ijk/dot_general | solution.py:66
  196.8 17.6 %copy.12 = f32[192,128,128]{0,1,2:T(8,128)} copy(f32[192,128,128]{2,1,0:T(8,128)} %fusion.42) | data formatting | bytes 25165824 | tf_op jit(solution)/shard_map/sik,sjk->ijk/dot_general | solution.py:66
  214.4 8.6 %fusion.41 = f32[192,128,128]{2,1,0:T(8,128)} fusion(bf16[64,128,192]{1,0,2:T(8,128)(2,1)S(1)} %copy.8, bf16[64,128,192]{1,0,2:T(8,128)(2,1)} %copy.9), kind=kOutput, calls=%fused_computation.61 | convolution fusion | flops 402653184 | bytes 18874368 | tf_op jit(solution)/shard_map/sik,sjk->ijk/dot_general | solution.py:63
  223.0 17.7 %copy.10 = f32[192,128,128]{0,1,2:T(8,128)} copy(f32[192,128,128]{2,1,0:T(8,128)} %fusion.41) | data formatting | bytes 25165824 | tf_op jit(solution)/shard_map/sik,sjk->ijk/dot_general | solution.py:63
  240.7 60.3 %fusion = f32[128,128,401]{2,1,0:T(8,128)} fusion(f32[128,128,192]{2,1,0:T(8,128)} %bitcast.22, f32[128,128,192]{2,1,0:T(8,128)} %bitcast.23, f32[192,401]{0,1:T(8,128)S(1)} %copy-done.2, f32[192,401]{0,1:T(8,128)S(1)} %copy-done.1), kind=kOutput, calls=%fused_computation | convolution fusion | flops 30281084928 | bytes 52061696 | tf_op jit(solution)/shard_map/dot_general | solution.py:82
  301.0 377.3 %reduce-scatter.2.cloned.1.call-done = f32[128,64,401]{2,1,0:T(8,128)} async-done(((f32[128,128,401]{2,1,0:T(8,128)}), f32[128,64,401]{2,1,0:T(8,128)}) %reduce-scatter.2.cloned.1.call-update) | async-done | bytes 13139984 | tf_op jit(solution)/shard_map/reduce_scatter | solution.py:83
  678.4 16.0 %copy.7 = f32[128,64,401]{0,1,2:T(8,128)} copy(f32[128,64,401]{2,1,0:T(8,128)} %reduce-scatter.2.cloned.1.call-done) | data formatting | bytes 26279936 | tf_op jit(solution)/shard_map/reduce_scatter | solution.py:83
  (18 shorter events, 0.5 us)
Async XLA Ops:
  6.5 98.1 %all-gather.2.cloned.1.call-start = ((), (), s32[]{:S(2)}) async-start(), calls=%async_computation.1 | async-start | bytes 3538944 | tf_op jit(solution)/shard_map/all_gather | solution.py:78
  31.8 142.5 %all-reduce.2.cloned.1.call-start = ((), (), s32[]{:S(2)}) async-start(), calls=%async_computation.2 | async-start | bytes 6291456 | tf_op jit(solution)/shard_map/psum | solution.py:16
  106.7 3.1 copy-start
  106.7 571.7 %reduce-scatter.2.cloned.1.call-start = ((), (), s32[]{:S(2)}) async-start(), calls=%async_computation.3 | async-start | bytes 50331648 | tf_op jit(solution)/shard_map/reduce_scatter | solution.py:83
  223.0 17.8 %copy-start.1 = (f32[192,401]{0,1:T(8,128)S(1)}, f32[192,401]{0,1:T(8,128)}, u32[]{:S(2)}) copy-start(f32[192,401]{0,1:T(8,128)} %get-tuple-element.14) | copy-start | bytes 923908
  223.0 17.8 %copy-start.2 = (f32[192,401]{0,1:T(8,128)S(1)}, f32[192,401]{0,1:T(8,128)}, u32[]{:S(2)}) copy-start(f32[192,401]{0,1:T(8,128)} %get-tuple-element.15) | copy-start | bytes 923908
Sparse Core Ops, SparseCore 0:
  31.9 72.7 all-gather.1
  107.0 67.1 all-reduce.1
  301.2 377.1 reduce-scatter.1
where the time goes:
time: 703 us; the launch traced here: 701 us
  waiting for transfers between devices  497 us (71%)
  matrix products  91.9 us (13%)
  local copies, waits for them, and re-layouts  75.7 us (11%)
  other arithmetic  23 us (3%)
  between operations  13.2 us (2%)
    reduce_scatter x1, waiting for transfers between devices, body(): stacks = lax.psum_scatter(lagged, 'seg', scatter_dimension=1, tiled=True)  377 us
    all_gather x1, waiting for transfers between devices, body(): row_white = lax.all_gather(own_white, 'col', axis=1, tiled=True)  72.9 us
    dot_general x1, matrix products, body(): lagged = jnp.dot(cross_all, inv_table, precision=lax.Precision.HIGHEST)  60.3 us
    psum x1, waiting for transfers between devices, spread(): return lax.psum(jnp.where(mine, shard, jnp.zeros_like(shard)), axis)  46.8 us
    dot_general x1, local copies, waits for them, and re-layouts, cross_spectra(): jnp.einsum('sik,sjk->ijk', stacked_real, right_both, preferred_element_ty...  17.7 us
    dot_general x1, local copies, waits for them, and re-layouts, cross_spectra(): jnp.einsum('sik,sjk->ijk', stacked_imag, right_both, preferred_element_ty...  17.6 us
    reduce_scatter x1, local copies, waits for them, and re-layouts, body(): stacks = lax.psum_scatter(lagged, 'seg', scatter_dimension=1, tiled=True)  16 us
  transfers between devices with their start and end apart: 3, of which 3 were waited for; matrix products, arithmetic and copies ran while one was open for 3% of the time, Pallas kernels for 0%

commit v1 on v0

v1 whole, which is shorter than its diff:
```python
import functools
import math

import jax
import jax.numpy as jnp
import ml_dtypes
import numpy as np
from jax import lax
from jax.experimental import pallas as pl
from jax.experimental.pallas import tpu as pltpu
from jax.sharding import PartitionSpec as P

NT = 2000
NF = 192
F_LO = 8
MAXLAG = 200
LAGS = 2 * MAXLAG + 1
SMOOTH = 5
SEGS = 64
PAIRS = NF // 2
CH = 16
SEG_DEV = 32
AXES = ("row", "col", "seg")
XROWS = 104
LAG_ROWS = 416
VMEM = 60 * 2**20
BF16 = jnp.bfloat16
F32 = jnp.float32


def split_bf16(table, terms):
    rest = np.asarray(table, np.float64)
    parts = []
    for _ in range(terms):
        part = rest.astype(np.float32).astype(ml_dtypes.bfloat16)
        parts.append(part)
        rest = rest - part.astype(np.float64)
    return np.stack(parts)


def forward_table():
    times = np.arange(NT)
    window_taper = 0.5 - 0.5 * np.cos((times + 0.5) * (2.0 * np.pi / NT))
    rows = []
    for reim in range(2):
        for kpar in range(2):
            freqs = F_LO + 2 * np.arange(PAIRS) + kpar
            phase = np.mod(freqs[:, None] * times[None, :], NT) * (2.0 * np.pi / NT)
            wave = np.cos(phase) if reim == 0 else -np.sin(phase)
            rows.append(wave * window_taper[None, :])
    return np.concatenate(rows, axis=0)


def inverse_table():
    shifts = np.arange(LAGS) - MAXLAG
    cols = []
    for kpar in range(2):
        for reim in range(2):
            freqs = F_LO + 2 * np.arange(PAIRS) + kpar
            phase = np.mod(freqs[None, :] * shifts[:, None], NT) * (2.0 * np.pi / NT)
            cols.append(np.cos(phase) if reim == 0 else np.sin(phase))
    table = np.concatenate(cols, axis=1) / math.sqrt(NF * SEGS)
    table = np.concatenate([table, np.zeros((LAG_ROWS - LAGS, 2 * NF))], axis=0)
    return np.concatenate(list(split_bf16(table, 2)), axis=1)


def smoothing_tables():
    freqs = np.concatenate([2 * np.arange(PAIRS), 2 * np.arange(PAIRS) + 1])
    near = (np.abs(freqs[:, None] - freqs[None, :]) <= SMOOTH).astype(np.float32)
    return near.astype(ml_dtypes.bfloat16), near.sum(axis=1, keepdims=True)


def lane_tables():
    by_channel = np.zeros((512, 512), np.float32)
    by_group = np.zeros((512, 512), np.float32)
    seg, ch = np.meshgrid(np.arange(SEG_DEV), np.arange(CH), indexing="ij")
    by_channel[seg * CH + ch, ch * SEG_DEV + seg] = 1
    grp, sub, seg = np.meshgrid(np.arange(4), np.arange(4), np.arange(32), indexing="ij")
    by_group[grp * 128 + sub * 32 + seg, sub * 128 + grp * 32 + seg] = 1
    rows = np.zeros((128, 128), np.float32)
    ch, pair = np.meshgrid(np.arange(CH), np.arange(8), indexing="ij")
    rows[pair * CH + ch, ch * 8 + pair] = 1
    as16 = lambda t: t.astype(ml_dtypes.bfloat16)
    return as16(by_channel), as16(by_group), as16(rows)


def flat(x, y, z, core):
    return ((x * 2 + core) * 8 + (y * 2 + z % 2)) * 2 + z // 2


def places():
    return [
        (x, y, z, core)
        for x in range(4) for y in range(4) for z in range(4) for core in range(2)
    ]


def perm_of(move):
    return [(flat(*place), flat(*move(*place))) for place in places()]


def along_first(n):
    return perm_of(
        lambda x, y, z, core: (x, (y + n) % 4, z, core) if core == 0 else (x, y, (z + n) % 4, core)
    )


def along_second(n):
    return perm_of(
        lambda x, y, z, core: (x, (y + n) % 4, z, core) if core == 1 else (x, y, (z + n) % 4, core)
    )


def to_readers():
    return perm_of(
        lambda x, y, z, core: ((x + y + z) % 4, x, 2 * (y // 2) + core, y % 2)
    )


def slot_table():
    offsets, moves = (0, -1, 1, 2), (0, 1, -1, 2)
    table = np.zeros((128, 24), np.int32)
    for x, y, z, core in places():
        row = table[flat(x, y, z, core)]
        first, second = (y, z) if core == 0 else (z, y)
        for arr, n in enumerate(moves):
            for k in range(4):
                pos1, pos2 = (first + offsets[k]) % 4, (second - n) % 4
                ys, zs = (pos1, pos2) if core == 0 else (pos2, pos1)
                row[arr * 4 + k] = (2 * ys + zs % 2) * 2 + zs // 2
        for xs in range(4):
            for c2 in range(2):
                zs = (xs - y - (2 * (z // 2) + c2)) % 4
                row[16 + xs * 2 + c2] = (zs // 2) * 4 + c2 * 2 + zs % 2
    return table


def dot_nt(a, b):
    return lax.dot_general(a, b, (((1,), (1,)), ((), ())), preferred_element_type=F32)


def dot_nn(a, b):
    return jnp.dot(a, b, preferred_element_type=F32)


def split3(value):
    hi = value.astype(BF16)
    rest = value - hi.astype(F32)
    mid = rest.astype(BF16)
    return hi, mid, (rest - mid.astype(F32)).astype(BF16)


def spectra_kernel(
    alive_ref, traces_ref, table_ref, near_ref, counts_ref, chan_ref, group_ref, rows_ref,
    out_ref, white_ref,
):
    step = pl.program_id(0)
    segs = traces_ref.shape[0]
    lanes = segs * CH
    hi, mid, lo = split3(traces_ref[...].reshape(lanes, NT))
    t_hi, t_mid, t_lo = table_ref[0], table_ref[1], table_ref[2]
    spectra = dot_nt(t_lo, hi) + dot_nt(t_hi, lo) + dot_nt(t_mid, mid)
    spectra = spectra + (dot_nt(t_mid, hi) + dot_nt(t_hi, mid))
    spectra = spectra + dot_nt(t_hi, hi)
    real, imag = spectra[:NF], spectra[NF:]
    magnitude = jnp.sqrt(real * real + imag * imag)
    m_hi, m_mid, m_lo = split3(magnitude)
    near = near_ref[...]
    smooth = (dot_nn(near, m_lo) + dot_nn(near, m_mid) + dot_nn(near, m_hi)) / counts_ref[...]
    water = jnp.sum(magnitude, axis=0, keepdims=True) * (1.0 / NF)
    weight = 1.0 / (smooth + 0.05 * water + 1e-6)
    at = pl.ds(pl.multiple_of(step * lanes, 128), lanes)
    white_ref[:NF, at] = (real * weight).astype(BF16)
    white_ref[NF:, at] = (imag * weight).astype(BF16)

    @pl.when(step == pl.num_programs(0) - 1)
    def _():
        by_channel = dot_nn(white_ref[...], chan_ref[...]).astype(BF16)
        alive = [alive_ref[c].astype(F32) for c in range(CH)]
        grouped = []
        for b in range(4):
            lhs = jnp.concatenate(
                [by_channel[g * PAIRS:(g + 1) * PAIRS, 128 * b:128 * b + 128] for g in range(4)],
                axis=1,
            )
            grouped.append(dot_nn(lhs, group_ref[...]))
        for half in range(PAIRS // 16):
            cols = []
            for part in range(2):
                at8 = slice(16 * half + 8 * part, 16 * half + 8 * part + 8)
                cols.append(
                    jnp.concatenate(
                        [
                            grouped[c // 4][at8, 128 * (c % 4):128 * (c % 4) + 128] * alive[c]
                            for c in range(CH)
                        ],
                        axis=0,
                    )
                )
            block = jnp.concatenate(cols, axis=1).astype(BF16)
            block = dot_nn(rows_ref[...], block).astype(BF16)
            for part in range(2):
                at8 = slice(16 * half + 8 * part, 16 * half + 8 * part + 8)
                out_ref[at8] = block[:, 128 * part:128 * part + 128].reshape(8, CH, 128)


def whitened(traces, alive):
    steps = 2
    near, counts = smoothing_tables()
    by_channel, by_group, rows = lane_tables()
    table = split_bf16(forward_table(), 3)
    whole = lambda a: pl.BlockSpec(a.shape, lambda i: (0,) * a.ndim)
    consts = (table, near, counts, by_channel, by_group, rows)
    return pl.pallas_call(
        spectra_kernel,
        grid=(steps,),
        out_shape=jax.ShapeDtypeStruct((PAIRS, CH, 128), BF16),
        in_specs=[
            pl.BlockSpec(memory_space=pltpu.SMEM),
            pl.BlockSpec((SEG_DEV // steps, CH, NT), lambda i: (i, 0, 0)),
        ]
        + [whole(a) for a in consts],
        out_specs=pl.BlockSpec((PAIRS, CH, 128), lambda i: (0, 0, 0)),
        scratch_shapes=[pltpu.VMEM((2 * NF, SEG_DEV * CH), BF16)],
        compiler_params=pltpu.CompilerParams(vmem_limit_bytes=VMEM),
        name="whitened_spectra",
    )(alive, traces, *(jnp.asarray(a) for a in consts))


CHUNKS = 4
PER = PAIRS // CHUNKS
J_STEP = 8


def stack_kernel(slots_ref, *refs):
    parts, second_ref, table_ref, out_ref = refs[:4], refs[4], refs[5], refs[6]
    left, right = refs[7:9]
    cross_refs, sems = refs[9:13], refs[13]
    step = pl.program_id(0)

    def copies(chunk):
        at = pl.ds(chunk * PER, PER)
        found = []
        for n in range(8):
            slot = slots_ref[16 + n]
            found.append((second_ref.at[n, at], right.at[slot, at]))
        for arr, ref in enumerate(parts):
            for k in range(4):
                found.append((ref.at[k, at], left.at[slots_ref[arr * 4 + k], at]))
        return [
            pltpu.make_async_copy(src, dst, sems.at[chunk, n])
            for n, (src, dst) in enumerate(found)
        ]

    @pl.when(step == 0)
    def _():
        pending = [copies(chunk) for chunk in range(CHUNKS)]
        for chunk in pending:
            for copy in chunk:
                copy.start()
        lane = lax.broadcasted_iota(jnp.int32, (CH, 128), 1)
        even = (lane // 32) % 2 == 0
        one, zero = jnp.float32(1), jnp.float32(0)
        sign = jnp.where(lane < 64, -one, one)
        keep0 = jnp.where(even, one, zero).astype(BF16)
        keep1 = jnp.where(even, zero, one).astype(BF16)
        turn0 = (sign * jnp.where(even, one, zero)).astype(BF16)
        turn1 = (sign * jnp.where(even, zero, one)).astype(BF16)

        def cross(p, _):
            first = jnp.concatenate(
                [jnp.concatenate([left[2 * u + h, p] for u in range(8)], axis=0) for h in range(2)],
                axis=1,
            )
            cols = []
            for h in range(2):
                blocks = [right[4 * h + n, p] for n in range(4)]
                swapped = [jnp.concatenate([b[:, 64:], b[:, :64]], axis=1) for b in blocks]
                cols.append(
                    jnp.concatenate(
                        [b * keep0 for b in blocks]
                        + [b * turn0 for b in swapped]
                        + [b * keep1 for b in blocks]
                        + [b * turn1 for b in swapped],
                        axis=0,
                    )
                )
            product = dot_nt(jnp.concatenate(cols, axis=1), first)
            for g in range(4):
                cross_refs[g][pl.ds(p, 64, stride=XROWS), :] = product[64 * g:64 * g + 64]
            return 0

        for chunk in range(CHUNKS):
            for copy in pending[chunk]:
                copy.wait()
            lax.fori_loop(chunk * PER, (chunk + 1) * PER, cross, 0, unroll=UNROLL)

    table = table_ref[...]
    out_rows = out_ref.reshape(LAGS * J_STEP, 128)
    for pair in range(J_STEP // 2):
        cols = []
        for e in range(2):
            j = step * J_STEP + 2 * pair + e
            at = pl.ds(pl.multiple_of(j * XROWS, 8), PAIRS)
            cols.append(jnp.concatenate([ref[at, :].astype(BF16) for ref in cross_refs], axis=0))
        both = jnp.concatenate(cols, axis=1)
        lags = dot_nn(table, jnp.concatenate([both, both], axis=0))
        for e in range(2):
            out_rows[pl.ds(2 * pair + e, LAGS, stride=J_STEP), :] = lags[:LAGS, 128 * e:128 * e + 128]


UNROLL = 12


def stacked(slots, parts, second, table):
    any_spec = pl.BlockSpec(memory_space=pl.ANY)
    return pl.pallas_call(
        stack_kernel,
        grid_spec=pltpu.PrefetchScalarGridSpec(
            num_scalar_prefetch=1,
            grid=(64 // J_STEP,),
            in_specs=[any_spec] * 5 + [pl.BlockSpec(table.shape, lambda u, s: (0, 0))],
            out_specs=pl.BlockSpec((LAGS, J_STEP, 128), lambda u, s: (0, u, 0)),
            scratch_shapes=[
                pltpu.VMEM((16, PAIRS, CH, 128), BF16),
                pltpu.VMEM((8, PAIRS, CH, 128), BF16),
            ]
            + [pltpu.VMEM((64 * XROWS, 128), F32)] * 4
            + [pltpu.SemaphoreType.DMA((CHUNKS, 24))],
        ),
        out_shape=jax.ShapeDtypeStruct((LAGS, 64, 128), F32),
        compiler_params=pltpu.CompilerParams(vmem_limit_bytes=VMEM),
        cost_estimate=pl.CostEstimate(
            flops=2 * 10**10, bytes_accessed=24 * 2**20, transcendentals=0
        ),
        name="stacks",
    )(slots, *parts, second, table)


def body(traces, channel_alive):
    own = whitened(traces, channel_alive)
    device = (lax.axis_index("row") * 8 + lax.axis_index("col")) * 2 + lax.axis_index("seg")
    slots = lax.dynamic_index_in_dim(jnp.asarray(slot_table()), device, 0, keepdims=False)
    send = lambda a, perm: lax.ppermute(a, AXES, perm)
    first = [own] + [send(own, along_first(n)) for n in (1, -1, 2)]
    second = send(own, to_readers())
    *first, second = lax.optimization_barrier((*first, second))
    mine = jnp.stack(first)
    second = lax.all_gather(second, "row", axis=0)
    parts = [mine] + [send(mine, along_second(n)) for n in (1, -1, 2)]
    out = stacked(slots, parts, second, jnp.asarray(inverse_table()))
    return jnp.transpose(out, (2, 1, 0))


def solution(mesh):
    return jax.shard_map(
        body,
        mesh=mesh,
        in_specs=(P("seg", ("row", "col"), None), P(("row", "col"))),
        out_specs=P("row", ("col", "seg"), None),
        check_vma=False,
    )
```

time: 703 us -> 111 us (0.16)
  waiting for transfers between devices: 497 us -> 51.9 us
  matrix products: 91.9 us -> 0 us
  local copies, waits for them, and re-layouts: 75.7 us -> 1.28 us
  Pallas kernels: 0 us -> 29.4 us
  other arithmetic: 23 us -> 1.19 us
  starting transfers between devices: 0.09 us -> 13.4 us
    reduce_scatter x1 -> x0, waiting for transfers between devices: 377 us -> none  [body(): stacks = lax.psum_scatter(lagged, 'seg', scatter_dimension=1, tiled=True)]
    dot_general x5 -> x0, matrix products: 91.9 us -> none  [the longest x1 60.3 us: body(): lagged = jnp.dot(cross_all, inv_table, precision=lax.Precision.HIGHEST)]
    all_gather x1, waiting for transfers between devices: 72.9 us -> 0.01 us  [body(): second = lax.all_gather(second, 'row', axis=0)]
    ppermute x0 -> x7, waiting for transfers between devices: none -> 51.9 us  [body(): send = lambda a, perm: lax.ppermute(a, AXES, perm)]
    psum x1 -> x0, waiting for transfers between devices: 46.8 us -> none  [spread(): return lax.psum(jnp.where(mine, shard, jnp.zeros_like(shard)), axis)]
    dot_general x3 -> x0, local copies, waits for them, and re-layouts: 35.7 us -> none  [the longest x1 17.7 us: cross_spectra(): jnp.einsum('sik,sjk->ijk', stacked_real, right_both, preferred_element_ty...]
    pallas_call x0 -> x2, Pallas kernels: none -> 29.4 us  [the longest x1 18.3 us: stacked(): pl.pallas_call(stack_kernel, grid_spec=pltpu.PrefetchScalarGridSpec(num_s...]
    concatenate x3 -> x0, local copies, waits for them, and re-layouts: 20.6 us -> none  [the longest x1 7.79 us: cross_spectra(): jnp.concatenate([right_spec[..., :NF], right_spec[..., NF:]], axis=0)]
  transfers between devices with their start and end apart: 3 -> 8, of which waited for: 3 -> 6; matrix products, arithmetic and copies ran while one was open for 3% -> 2% of each run, Pallas kernels for 0% -> 0%
where the time goes in v1:
time: 111 us
  waiting for transfers between devices  51.9 us (47%)
  Pallas kernels  29.4 us (26%)
  starting transfers between devices  13.4 us (12%)
  between operations  13.4 us (12%)
  local copies, waits for them, and re-layouts  1.28 us (1%)
  other arithmetic  1.19 us (1%)
    ppermute x7, waiting for transfers between devices, body(): send = lambda a, perm: lax.ppermute(a, AXES, perm)  51.9 us
    pallas_call x1, Pallas kernels, stacked(): pl.pallas_call(stack_kernel, grid_spec=pltpu.PrefetchScalarGridSpec(num_s...  18.3 us
    ppermute x7, starting transfers between devices, body(): send = lambda a, perm: lax.ppermute(a, AXES, perm)  13.4 us
    pallas_call x1, Pallas kernels, whitened(): pl.pallas_call(spectra_kernel, grid=(steps,), out_shape=jax.ShapeDtypeStr...  11.1 us
  transfers between devices with their start and end apart: 8, of which 6 were waited for; matrix products, arithmetic and copies ran while one was open for 2% of the time, Pallas kernels for 0%

profile of v1, /device:TPU:4, one launch (start us, length us, event | category | flops | bytes accessed | tf_op | source)
XLA Modules:
  0.0 110.6 jit_solution(2649665090793464873)
XLA Ops:
  6.5 0.0 all-gather.3.cloned.1.call-start
  6.5 11.1 %whitened_spectra.1 = bf16[96,16,128]{2,1,0:T(8,128)(2,1)} custom-call(s32[16]{0:T(128)} %alive_ref.1, f32[32,16,2000]{2,1,0:T(8,128)} %traces_ref.1, bf16[3,384,2000]{2,1,0:T(8,128)(2,1)} %constant.38.clone.table_ref, bf16[192,192]{1,0:T(8,128)(2,1)} %constant.39.clone.near_ref, f32[192,1]{1,0:T(8,128)} %constant.40.clone.counts_ref, ...), custom_call_target="tpu_custom_call" | custom-call | tf_op jit(solution)/shard_map/whitened_spectra/pallas_call | solution.py:214
  17.6 5.1 %collective-permute-start.3 = (bf16[96,16,128]{2,1,0:T(8,128)(2,1)}, bf16[96,16,128]{2,1,0:T(8,128)(2,1)S(1)}, u32[]{:S(2)}, u32[]{:S(2)}) collective-permute-start(bf16[96,16,128]{2,1,0:T(8,128)(2,1)} %whitened_spectra.1), channel_id=1, source_target_pairs={{0,0},{16,2},{2,32},{18,34},{1,64},{17,66},{3,96},{19,98},{4,48},{... | collective-permute-start | bytes 1179656 | tf_op jit(solution)/shard_map/ppermute | solution.py:344
  22.7 3.9 %collective-permute-start.2 = (bf16[96,16,128]{2,1,0:T(8,128)(2,1)}, bf16[96,16,128]{2,1,0:T(8,128)(2,1)S(1)}, u32[]{:S(2)}, u32[]{:S(2)}) collective-permute-start(bf16[96,16,128]{2,1,0:T(8,128)(2,1)} %whitened_spectra.1), channel_id=1, source_target_pairs={{0,8},{16,17},{2,10},{18,19},{1,9},{17,16},{3,11},{19,18},{4,12},{... | collective-permute-start | bytes 1179656 | tf_op jit(solution)/shard_map/ppermute | solution.py:344
  26.6 0.0 collective-permute-start.1
  26.6 2.0 %collective-permute-start = (bf16[96,16,128]{2,1,0:T(8,128)(2,1)}, bf16[96,16,128]{2,1,0:T(8,128)(2,1)S(1)}, u32[]{:S(2)}, u32[]{:S(2)}) collective-permute-start(bf16[96,16,128]{2,1,0:T(8,128)(2,1)} %whitened_spectra.1), channel_id=1, source_target_pairs={{0,4},{16,18},{2,6},{18,17},{1,5},{17,19},{3,7},{19,16},{4,8},{20,... | collective-permute-start | bytes 1179656 | tf_op jit(solution)/shard_map/ppermute | solution.py:344
  28.7 6.9 %collective-permute-done.3 = bf16[96,16,128]{2,1,0:T(8,128)(2,1)S(1)} collective-permute-done((bf16[96,16,128]{2,1,0:T(8,128)(2,1)}, bf16[96,16,128]{2,1,0:T(8,128)(2,1)S(1)}, u32[]{:S(2)}, u32[]{:S(2)}) %collective-permute-start.3) | collective-permute-done | bytes 393248 | tf_op jit(solution)/shard_map/ppermute | solution.py:344
  35.6 5.6 %collective-permute-done.2 = bf16[96,16,128]{2,1,0:T(8,128)(2,1)S(1)} collective-permute-done((bf16[96,16,128]{2,1,0:T(8,128)(2,1)}, bf16[96,16,128]{2,1,0:T(8,128)(2,1)S(1)}, u32[]{:S(2)}, u32[]{:S(2)}) %collective-permute-start.2) | collective-permute-done | bytes 393248 | tf_op jit(solution)/shard_map/ppermute | solution.py:344
  41.1 0.0 collective-permute-done.1
  41.1 4.1 %collective-permute-done = bf16[96,16,128]{2,1,0:T(8,128)(2,1)S(1)} collective-permute-done((bf16[96,16,128]{2,1,0:T(8,128)(2,1)}, bf16[96,16,128]{2,1,0:T(8,128)(2,1)S(1)}, u32[]{:S(2)}, u32[]{:S(2)}) %collective-permute-start) | collective-permute-done | bytes 393248 | tf_op jit(solution)/shard_map/ppermute | solution.py:344
  45.2 0.0 copy-done.1
  45.2 0.0 all-gather.3.cloned.1.call-update
  45.3 1.2 %pad_maximum_fusion.refs_0_ = bf16[4,96,16,128]{3,2,1,0:T(8,128)(2,1)S(1)} fusion(bf16[1,96,16,128]{3,2,1,0:T(8,128)(2,1)S(1)} %bitcast.9, bf16[1,96,16,128]{3,2,1,0:T(8,128)(2,1)S(1)} %bitcast.10, bf16[1,96,16,128]{3,2,1,0:T(8,128)(2,1)S(1)} %bitcast.11, bf16[1,96,16,128]{3,2,1,0:T(8,128)(2,1)} %bitcast.8), kind=kLoop, calls=%fused_computation | loop fusion | flops 2359296 | bytes 3145728 | tf_op jit(solution)/shard_map/stack | solution.py:348
  46.5 0.0 copy-start
  46.5 0.1 collective-permute-start.6
  46.6 1.5 %collective-permute-start.5 = (bf16[4,96,16,128]{3,2,1,0:T(8,128)(2,1)S(1)}, bf16[4,96,16,128]{3,2,1,0:T(8,128)(2,1)}, u32[]{:S(2)}, u32[]{:S(2)}) collective-permute-start(bf16[4,96,16,128]{3,2,1,0:T(8,128)(2,1)S(1)} %pad_maximum_fusion.refs_0_), channel_id=1, source_target_pairs={{0,3},{16,28},{2,0},{18,30},{1,2},{17,29},{3,1},{19,31},{4,7},{20,... | collective-permute-start | bytes 4718600 | tf_op jit(solution)/shard_map/ppermute | solution.py:344
  48.1 0.8 collective-permute-start.4
  48.8 1.3 %dynamic-slice_bitcast_fusion.slots_ref = s32[24]{0:T(128)} fusion(s32[128,24]{1,0:T(8,128)} %constant.44.clone, s32[]{:T(128)S(6)} %select_n.4), kind=kLoop, calls=%fused_computation.1 | loop fusion | bytes 196 | tf_op jit(solution)/shard_map/jit(dynamic_index_in_dim)/squeeze | solution.py:343
  50.1 18.5 %collective-permute-done.6.refs_3_ = bf16[4,96,16,128]{3,2,1,0:T(8,128)(2,1)S(1)} collective-permute-done((bf16[4,96,16,128]{3,2,1,0:T(8,128)(2,1)S(1)}, bf16[4,96,16,128]{3,2,1,0:T(8,128)(2,1)S(1)}, u32[]{:S(2)}, u32[]{:S(2)}) %collective-permute-start.6) | collective-permute-done | bytes 1572896 | tf_op jit(solution)/shard_map/ppermute | solution.py:344
  68.6 15.7 %collective-permute-done.5.refs_2_ = bf16[4,96,16,128]{3,2,1,0:T(8,128)(2,1)} collective-permute-done((bf16[4,96,16,128]{3,2,1,0:T(8,128)(2,1)S(1)}, bf16[4,96,16,128]{3,2,1,0:T(8,128)(2,1)}, u32[]{:S(2)}, u32[]{:S(2)}) %collective-permute-start.5) | collective-permute-done | bytes 1572896 | tf_op jit(solution)/shard_map/ppermute | solution.py:344
  84.2 1.2 %collective-permute-done.4.refs_1_ = bf16[4,96,16,128]{3,2,1,0:T(8,128)(2,1)} collective-permute-done((bf16[4,96,16,128]{3,2,1,0:T(8,128)(2,1)S(1)}, bf16[4,96,16,128]{3,2,1,0:T(8,128)(2,1)}, u32[]{:S(2)}, u32[]{:S(2)}) %collective-permute-start.4) | collective-permute-done | bytes 1572896 | tf_op jit(solution)/shard_map/ppermute | solution.py:344
  85.4 0.0 copy-done
  85.4 0.0 copy-done.2
  85.4 18.3 %stacks.1 = f32[401,64,128]{2,1,0:T(8,128)} custom-call(s32[24]{0:T(128)} %dynamic-slice_bitcast_fusion.slots_ref, bf16[4,96,16,128]{3,2,1,0:T(8,128)(2,1)} %copy-done, bf16[4,96,16,128]{3,2,1,0:T(8,128)(2,1)} %collective-permute-done.4.refs_1_, bf16[4,96,16,128]{3,2,1,0:T(8,128)(2,1)} %collective-permute-done.5.refs_2_, bf16[4,96,16,128]{3,2,1,0:T(8,128)(2,1)} %copy-done.2, ...), custom_call_target="tpu_custom_call" | custom-call | flops 20000000000 | bytes 25165824 | tf_op jit(solution)/shard_map/stacks/pallas_call | solution.py:317
  (3 shorter events, 0.0 us)
Async XLA Ops:
  6.5 78.9 %all-gather.3.cloned.1.call-start = ((), (), s32[]{:S(2)}) async-start(), calls=%async_computation | async-start | bytes 3538944 | tf_op jit(solution)/shard_map/all_gather | solution.py:349
  17.6 17.9 %collective-permute-start.3 = (bf16[96,16,128]{2,1,0:T(8,128)(2,1)}, bf16[96,16,128]{2,1,0:T(8,128)(2,1)S(1)}, u32[]{:S(2)}, u32[]{:S(2)}) collective-permute-start(bf16[96,16,128]{2,1,0:T(8,128)(2,1)} %whitened_spectra.1), channel_id=1, source_target_pairs={{0,0},{16,2},{2,32},{18,34},{1,64},{17,66},{3,96},{19,98},{4,48},{... | collective-permute-start | bytes 1179656 | tf_op jit(solution)/shard_map/ppermute | solution.py:344
  22.7 18.4 %collective-permute-start.2 = (bf16[96,16,128]{2,1,0:T(8,128)(2,1)}, bf16[96,16,128]{2,1,0:T(8,128)(2,1)S(1)}, u32[]{:S(2)}, u32[]{:S(2)}) collective-permute-start(bf16[96,16,128]{2,1,0:T(8,128)(2,1)} %whitened_spectra.1), channel_id=1, source_target_pairs={{0,8},{16,17},{2,10},{18,19},{1,9},{17,16},{3,11},{19,18},{4,12},{... | collective-permute-start | bytes 1179656 | tf_op jit(solution)/shard_map/ppermute | solution.py:344
  26.6 14.5 %collective-permute-start.1 = (bf16[96,16,128]{2,1,0:T(8,128)(2,1)}, bf16[96,16,128]{2,1,0:T(8,128)(2,1)S(1)}, u32[]{:S(2)}, u32[]{:S(2)}) collective-permute-start(bf16[96,16,128]{2,1,0:T(8,128)(2,1)} %whitened_spectra.1), channel_id=1, source_target_pairs={{0,12},{16,19},{2,14},{18,16},{1,13},{17,18},{3,15},{19,17},{4,0},... | collective-permute-start | bytes 1179656 | tf_op jit(solution)/shard_map/ppermute | solution.py:344
  26.6 18.6 %collective-permute-start = (bf16[96,16,128]{2,1,0:T(8,128)(2,1)}, bf16[96,16,128]{2,1,0:T(8,128)(2,1)S(1)}, u32[]{:S(2)}, u32[]{:S(2)}) collective-permute-start(bf16[96,16,128]{2,1,0:T(8,128)(2,1)} %whitened_spectra.1), channel_id=1, source_target_pairs={{0,4},{16,18},{2,6},{18,17},{1,5},{17,19},{3,7},{19,16},{4,8},{20,... | collective-permute-start | bytes 1179656 | tf_op jit(solution)/shard_map/ppermute | solution.py:344
  35.6 9.7 %copy-start.1 = (bf16[96,16,128]{2,1,0:T(8,128)(2,1)}, bf16[96,16,128]{2,1,0:T(8,128)(2,1)S(1)}, u32[]{:S(2)}) copy-start(bf16[96,16,128]{2,1,0:T(8,128)(2,1)S(1)} %collective-permute-done.3) | copy-start | bytes 1179652
  46.5 39.0 %copy-start = (bf16[4,96,16,128]{3,2,1,0:T(8,128)(2,1)}, bf16[4,96,16,128]{3,2,1,0:T(8,128)(2,1)S(1)}, u32[]{:S(2)}) copy-start(bf16[4,96,16,128]{3,2,1,0:T(8,128)(2,1)S(1)} %pad_maximum_fusion.refs_0_) | copy-start | bytes 4718596
  46.5 22.1 %collective-permute-start.6 = (bf16[4,96,16,128]{3,2,1,0:T(8,128)(2,1)S(1)}, bf16[4,96,16,128]{3,2,1,0:T(8,128)(2,1)S(1)}, u32[]{:S(2)}, u32[]{:S(2)}) collective-permute-start(bf16[4,96,16,128]{3,2,1,0:T(8,128)(2,1)S(1)} %pad_maximum_fusion.refs_0_), channel_id=1, source_target_pairs={{0,1},{16,24},{2,3},{18,26},{1,0},{17,25},{3,2},{19,27},{4,5},{20,... | collective-permute-start | bytes 4718600 | tf_op jit(solution)/shard_map/ppermute | solution.py:344
  46.6 37.7 %collective-permute-start.5 = (bf16[4,96,16,128]{3,2,1,0:T(8,128)(2,1)S(1)}, bf16[4,96,16,128]{3,2,1,0:T(8,128)(2,1)}, u32[]{:S(2)}, u32[]{:S(2)}) collective-permute-start(bf16[4,96,16,128]{3,2,1,0:T(8,128)(2,1)S(1)} %pad_maximum_fusion.refs_0_), channel_id=1, source_target_pairs={{0,3},{16,28},{2,0},{18,30},{1,2},{17,29},{3,1},{19,31},{4,7},{20,... | collective-permute-start | bytes 4718600 | tf_op jit(solution)/shard_map/ppermute | solution.py:344
  48.1 37.4 %collective-permute-start.4 = (bf16[4,96,16,128]{3,2,1,0:T(8,128)(2,1)S(1)}, bf16[4,96,16,128]{3,2,1,0:T(8,128)(2,1)}, u32[]{:S(2)}, u32[]{:S(2)}) collective-permute-start(bf16[4,96,16,128]{3,2,1,0:T(8,128)(2,1)S(1)} %pad_maximum_fusion.refs_0_), channel_id=1, source_target_pairs={{0,2},{16,20},{2,1},{18,22},{1,3},{17,21},{3,0},{19,23},{4,6},{20,... | collective-permute-start | bytes 4718600 | tf_op jit(solution)/shard_map/ppermute | solution.py:344
  68.6 16.9 %copy-start.2 = (bf16[4,96,16,128]{3,2,1,0:T(8,128)(2,1)}, bf16[4,96,16,128]{3,2,1,0:T(8,128)(2,1)S(1)}, u32[]{:S(2)}) copy-start(bf16[4,96,16,128]{3,2,1,0:T(8,128)(2,1)S(1)} %collective-permute-done.6.refs_3_) | copy-start | bytes 4718596
Sparse Core Ops, SparseCore 0:
  45.4 24.6 all-gather.2

commit v2 on v1

--- a/solution.py
+++ b/solution.py
@@ -22,7 +22,8 @@
 SEG_DEV = 32
 AXES = ("row", "col", "seg")
 XROWS = 104
-LAG_ROWS = 416
+LAG_ROWS = 208
+TERMS = 2
 VMEM = 60 * 2**20
 BF16 = jnp.bfloat16
 F32 = jnp.float32
@@ -52,16 +53,17 @@
 
 
 def inverse_table():
-    shifts = np.arange(LAGS) - MAXLAG
-    cols = []
-    for kpar in range(2):
-        for reim in range(2):
+    shifts = np.arange(LAG_ROWS)
+    parts = []
+    for reim in range(2):
+        cols = []
+        for kpar in range(2):
             freqs = F_LO + 2 * np.arange(PAIRS) + kpar
             phase = np.mod(freqs[None, :] * shifts[:, None], NT) * (2.0 * np.pi / NT)
             cols.append(np.cos(phase) if reim == 0 else np.sin(phase))
-    table = np.concatenate(cols, axis=1) / math.sqrt(NF * SEGS)
-    table = np.concatenate([table, np.zeros((LAG_ROWS - LAGS, 2 * NF))], axis=0)
-    return np.concatenate(list(split_bf16(table, 2)), axis=1)
+        table = np.concatenate(cols, axis=1) / math.sqrt(NF * SEGS)
+        parts.append(np.concatenate(list(split_bf16(table, TERMS)), axis=1))
+    return np.concatenate(parts, axis=0)
 
 
 def smoothing_tables():
@@ -113,25 +115,35 @@
 
 def to_readers():
     return perm_of(
-        lambda x, y, z, core: ((x + y + z) % 4, x, 2 * (y // 2) + core, y % 2)
+        lambda x, y, z, core: ((x + y + z + 2 * core) % 4, x, 2 * (y // 2) + core, y % 2)
     )
 
 
+def along_x(n):
+    return perm_of(lambda x, y, z, core: ((x + n) % 4, y, z, core))
+
+
+def other_core():
+    return perm_of(lambda x, y, z, core: (x, y, z, 1 - core))
+
+
 def slot_table():
-    offsets, moves = (0, -1, 1, 2), (0, 1, -1, 2)
+    offsets = (0, -1, 1, 2)
+    first_order = [(k, n) for n in (0, 1, -1) for k in range(4)] + [(k, 2) for k in range(4)]
     table = np.zeros((128, 24), np.int32)
     for x, y, z, core in places():
         row = table[flat(x, y, z, core)]
         first, second = (y, z) if core == 0 else (z, y)
-        for arr, n in enumerate(moves):
+        for at, (k, n) in enumerate(first_order):
+            pos1, pos2 = (first + offsets[k]) % 4, (second - n) % 4
+            ys, zs = (pos1, pos2) if core == 0 else (pos2, pos1)
+            row[at] = (2 * ys + zs % 2) * 2 + zs // 2
+        for other in range(2):
             for k in range(4):
-                pos1, pos2 = (first + offsets[k]) % 4, (second - n) % 4
-                ys, zs = (pos1, pos2) if core == 0 else (pos2, pos1)
-                row[arr * 4 + k] = (2 * ys + zs % 2) * 2 + zs // 2
-        for xs in range(4):
-            for c2 in range(2):
-                zs = (xs - y - (2 * (z // 2) + c2)) % 4
-                row[16 + xs * 2 + c2] = (zs // 2) * 4 + c2 * 2 + zs % 2
+                c2 = core ^ other
+                ys, xs = 2 * (z // 2) + c2, (x + offsets[k]) % 4
+                zs = (xs - y - ys - 2 * (z % 2)) % 4
+                row[16 + other * 4 + k] = (zs // 2) * 4 + c2 * 2 + zs % 2
     return table
 
 
@@ -152,46 +164,64 @@
 
 def spectra_kernel(
     alive_ref, traces_ref, table_ref, near_ref, counts_ref, chan_ref, group_ref, rows_ref,
-    out_ref, white_ref,
+    out_ref, total_ref,
 ):
     step = pl.program_id(0)
-    segs = traces_ref.shape[0]
-    lanes = segs * CH
-    hi, mid, lo = split3(traces_ref[...].reshape(lanes, NT))
-    t_hi, t_mid, t_lo = table_ref[0], table_ref[1], table_ref[2]
-    spectra = dot_nt(t_lo, hi) + dot_nt(t_hi, lo) + dot_nt(t_mid, mid)
-    spectra = spectra + (dot_nt(t_mid, hi) + dot_nt(t_hi, mid))
-    spectra = spectra + dot_nt(t_hi, hi)
-    real, imag = spectra[:NF], spectra[NF:]
-    magnitude = jnp.sqrt(real * real + imag * imag)
-    m_hi, m_mid, m_lo = split3(magnitude)
-    near = near_ref[...]
-    smooth = (dot_nn(near, m_lo) + dot_nn(near, m_mid) + dot_nn(near, m_hi)) / counts_ref[...]
-    water = jnp.sum(magnitude, axis=0, keepdims=True) * (1.0 / NF)
-    weight = 1.0 / (smooth + 0.05 * water + 1e-6)
-    at = pl.ds(pl.multiple_of(step * lanes, 128), lanes)
-    white_ref[:NF, at] = (real * weight).astype(BF16)
-    white_ref[NF:, at] = (imag * weight).astype(BF16)
+    lanes = SEG_DEV * CH
+    width = traces_ref.shape[2]
+    traces = traces_ref[...].reshape(lanes, width)
+    inside = lax.broadcasted_iota(jnp.int32, (1, width), 1) < NT - step * width
+    hi, mid, lo = split3(jnp.where(inside, traces, 0.0))
+    rows = 2 * NF
+    by_hi = dot_nt(table_ref[...], hi)
+    by_mid = dot_nt(table_ref[: 2 * rows], mid)
+    by_lo = dot_nt(table_ref[:rows], lo)
+    small = by_hi[2 * rows :] + by_lo + by_mid[rows:]
+    added = by_hi[:rows] + (by_hi[rows : 2 * rows] + by_mid[:rows] + small)
+
+    @pl.when(step == 0)
+    def _():
+        total_ref[...] = added
+
+    @pl.when(step > 0)
+    def _():
+        total_ref[...] += added
 
     @pl.when(step == pl.num_programs(0) - 1)
     def _():
-        by_channel = dot_nn(white_ref[...], chan_ref[...]).astype(BF16)
+        real, imag = total_ref[:NF], total_ref[NF:]
+        magnitude = jnp.sqrt(real * real + imag * imag)
+        m_hi, m_mid, m_lo = split3(magnitude)
+        near = near_ref[...]
+        smooth = (dot_nn(near, m_lo) + dot_nn(near, m_mid) + dot_nn(near, m_hi)) / counts_ref[...]
+        water = jnp.sum(magnitude, axis=0, keepdims=True) * (1.0 / NF)
+        weight = 1.0 / (smooth + 0.05 * water + 1e-6)
+        white = jnp.concatenate([real * weight, imag * weight], axis=0).astype(BF16)
+        by_channel = dot_nn(white, chan_ref[...]).astype(BF16)
         alive = [alive_ref[c].astype(F32) for c in range(CH)]
-        grouped = []
-        for b in range(4):
-            lhs = jnp.concatenate(
-                [by_channel[g * PAIRS:(g + 1) * PAIRS, 128 * b:128 * b + 128] for g in range(4)],
-                axis=1,
-            )
-            grouped.append(dot_nn(lhs, group_ref[...]))
+        lhs = jnp.concatenate(
+            [
+                jnp.concatenate(
+                    [by_channel[g * PAIRS:(g + 1) * PAIRS, 128 * b:128 * b + 128] for g in range(4)],
+                    axis=1,
+                )
+                for b in range(4)
+            ],
+            axis=0,
+        )
+        grouped = dot_nn(lhs, group_ref[...])
         for half in range(PAIRS // 16):
             cols = []
             for part in range(2):
-                at8 = slice(16 * half + 8 * part, 16 * half + 8 * part + 8)
+                at = 16 * half + 8 * part
                 cols.append(
                     jnp.concatenate(
                         [
-                            grouped[c // 4][at8, 128 * (c % 4):128 * (c % 4) + 128] * alive[c]
+                            grouped[
+                                PAIRS * (c // 4) + at:PAIRS * (c // 4) + at + 8,
+                                128 * (c % 4):128 * (c % 4) + 128,
+                            ]
+                            * alive[c]
                             for c in range(CH)
                         ],
                         axis=0,
@@ -200,31 +230,33 @@
             block = jnp.concatenate(cols, axis=1).astype(BF16)
             block = dot_nn(rows_ref[...], block).astype(BF16)
             for part in range(2):
-                at8 = slice(16 * half + 8 * part, 16 * half + 8 * part + 8)
-                out_ref[at8] = block[:, 128 * part:128 * part + 128].reshape(8, CH, 128)
+                at = 16 * half + 8 * part
+                out_ref[at:at + 8] = block[:, 128 * part:128 * part + 128].reshape(8, CH, 128)
 
 
 def whitened(traces, alive):
-    steps = 2
+    width = 512
     near, counts = smoothing_tables()
     by_channel, by_group, rows = lane_tables()
-    table = split_bf16(forward_table(), 3)
+    table = split_bf16(forward_table(), 3).reshape(6 * NF, NT)
+    table = np.concatenate([table, np.zeros((6 * NF, 4 * width - NT), table.dtype)], axis=1)
     whole = lambda a: pl.BlockSpec(a.shape, lambda i: (0,) * a.ndim)
-    consts = (table, near, counts, by_channel, by_group, rows)
+    consts = (near, counts, by_channel, by_group, rows)
     return pl.pallas_call(
         spectra_kernel,
-        grid=(steps,),
+        grid=(4,),
         out_shape=jax.ShapeDtypeStruct((PAIRS, CH, 128), BF16),
         in_specs=[
             pl.BlockSpec(memory_space=pltpu.SMEM),
-            pl.BlockSpec((SEG_DEV // steps, CH, NT), lambda i: (i, 0, 0)),
+            pl.BlockSpec((SEG_DEV, CH, width), lambda i: (0, 0, i)),
+            pl.BlockSpec((6 * NF, width), lambda i: (0, i)),
         ]
         + [whole(a) for a in consts],
         out_specs=pl.BlockSpec((PAIRS, CH, 128), lambda i: (0, 0, 0)),
-        scratch_shapes=[pltpu.VMEM((2 * NF, SEG_DEV * CH), BF16)],
+        scratch_shapes=[pltpu.VMEM((2 * NF, SEG_DEV * CH), F32)],
         compiler_params=pltpu.CompilerParams(vmem_limit_bytes=VMEM),
         name="whitened_spectra",
-    )(alive, traces, *(jnp.asarray(a) for a in consts))
+    )(alive, traces, *(jnp.asarray(a) for a in (table,) + consts))
 
 
 CHUNKS = 4
@@ -233,20 +265,18 @@
 
 
 def stack_kernel(slots_ref, *refs):
-    parts, second_ref, table_ref, out_ref = refs[:4], refs[4], refs[5], refs[6]
-    left, right = refs[7:9]
-    cross_refs, sems = refs[9:13], refs[13]
+    sources, table_ref, out_ref = refs[:7], refs[7], refs[8]
+    left, right = refs[9:11]
+    cross_refs, sems = refs[11:15], refs[15]
     step = pl.program_id(0)
 
     def copies(chunk):
         at = pl.ds(chunk * PER, PER)
         found = []
-        for n in range(8):
-            slot = slots_ref[16 + n]
-            found.append((second_ref.at[n, at], right.at[slot, at]))
-        for arr, ref in enumerate(parts):
-            for k in range(4):
-                found.append((ref.at[k, at], left.at[slots_ref[arr * 4 + k], at]))
+        for ref in sources:
+            for k in range(ref.shape[0]):
+                to = left if len(found) < 16 else right
+                found.append((ref.at[k, at], to.at[slots_ref[len(found)], at]))
         return [
             pltpu.make_async_copy(src, dst, sems.at[chunk, n])
             for n, (src, dst) in enumerate(found)
@@ -295,31 +325,41 @@
                 copy.wait()
             lax.fori_loop(chunk * PER, (chunk + 1) * PER, cross, 0, unroll=UNROLL)
 
-    table = table_ref[...]
     out_rows = out_ref.reshape(LAGS * J_STEP, 128)
+    turned = 7 - lax.broadcasted_iota(jnp.int32, (LAG_ROWS // 8, 8, 128), 1)
     for pair in range(J_STEP // 2):
-        cols = []
+        halves = []
+        for reim in range(2):
+            cols = []
+            for e in range(2):
+                j = step * J_STEP + 2 * pair + e
+                at = pl.ds(pl.multiple_of(j * XROWS, 8), PAIRS)
+                x = [cross_refs[2 * kpar + reim][at, :].astype(BF16) for kpar in range(2)]
+                cols.append(jnp.concatenate(x * TERMS, axis=0))
+            rows = slice(LAG_ROWS * reim, LAG_ROWS * (reim + 1))
+            halves.append(dot_nn(table_ref[rows, :], jnp.concatenate(cols, axis=1)))
+        later, earlier = halves[0] + halves[1], halves[0] - halves[1]
         for e in range(2):
-            j = step * J_STEP + 2 * pair + e
-            at = pl.ds(pl.multiple_of(j * XROWS, 8), PAIRS)
-            cols.append(jnp.concatenate([ref[at, :].astype(BF16) for ref in cross_refs], axis=0))
-        both = jnp.concatenate(cols, axis=1)
-        lags = dot_nn(table, jnp.concatenate([both, both], axis=0))
-        for e in range(2):
-            out_rows[pl.ds(2 * pair + e, LAGS, stride=J_STEP), :] = lags[:LAGS, 128 * e:128 * e + 128]
-
-
-UNROLL = 12
-
-
-def stacked(slots, parts, second, table):
+            lanes, j = slice(128 * e, 128 * e + 128), 2 * pair + e
+            back = earlier[:, lanes].reshape(LAG_ROWS // 8, 8, 128)
+            back = jnp.take_along_axis(back, turned, axis=1)
+            for v in range(MAXLAG // 8):
+                out_rows[pl.ds((MAXLAG - 7 - 8 * v) * J_STEP + j, 8, stride=J_STEP), :] = back[v]
+            out_rows[pl.ds(j, 1), :] = earlier[MAXLAG:MAXLAG + 1, lanes]
+            out_rows[pl.ds(MAXLAG * J_STEP + j, MAXLAG + 1, stride=J_STEP), :] = later[: MAXLAG + 1, lanes]
+
+
+UNROLL = 24
+
+
+def stacked(slots, sources, table):
     any_spec = pl.BlockSpec(memory_space=pl.ANY)
     return pl.pallas_call(
         stack_kernel,
         grid_spec=pltpu.PrefetchScalarGridSpec(
             num_scalar_prefetch=1,
             grid=(64 // J_STEP,),
-            in_specs=[any_spec] * 5 + [pl.BlockSpec(table.shape, lambda u, s: (0, 0))],
+            in_specs=[any_spec] * len(sources) + [pl.BlockSpec(table.shape, lambda u, s: (0, 0))],
             out_specs=pl.BlockSpec((LAGS, J_STEP, 128), lambda u, s: (0, u, 0)),
             scratch_shapes=[
                 pltpu.VMEM((16, PAIRS, CH, 128), BF16),
@@ -334,7 +374,7 @@
             flops=2 * 10**10, bytes_accessed=24 * 2**20, transcendentals=0
         ),
         name="stacks",
-    )(slots, *parts, second, table)
+    )(slots, *sources, table)
 
 
 def body(traces, channel_alive):
@@ -346,9 +386,14 @@
     second = send(own, to_readers())
     *first, second = lax.optimization_barrier((*first, second))
     mine = jnp.stack(first)
-    second = lax.all_gather(second, "row", axis=0)
-    parts = [mine] + [send(mine, along_second(n)) for n in (1, -1, 2)]
-    out = stacked(slots, parts, second, jnp.asarray(inverse_table()))
+    up, down = send(mine, along_second(1)), send(mine, along_second(-1))
+    seconds = [second] + [send(second, along_x(n)) for n in (1, -1, 2)]
+    up, down, *seconds = lax.optimization_barrier((up, down, *seconds))
+    seconds = jnp.stack(seconds)
+    far_up, far_down = send(up[:2], along_second(1)), send(down[2:], along_second(-1))
+    others = send(seconds, other_core())
+    sources = (mine, up, down, far_up, far_down, seconds, others)
+    out = stacked(slots, sources, jnp.asarray(inverse_table()))
     return jnp.transpose(out, (2, 1, 0))
 
 

time: 111 us -> 94.5 us (0.85)
  between operations: 13.4 us -> 0.1 us
  waiting for transfers between devices: 51.9 us -> 41.3 us
  starting transfers between devices: 13.4 us -> 23.3 us
  Pallas kernels: 29.4 us -> 26.5 us
    ppermute x7 -> x12, waiting for transfers between devices: 51.9 us -> 41.3 us  [body(): send = lambda a, perm: lax.ppermute(a, AXES, perm)]
    ppermute x7 -> x12, starting transfers between devices: 13.4 us -> 23.3 us  [body(): send = lambda a, perm: lax.ppermute(a, AXES, perm)]
    pallas_call x1, Pallas kernels: 18.3 us -> 16.4 us  [stacked(): pl.pallas_call(stack_kernel, grid_spec=pltpu.PrefetchScalarGridSpec(num_s...]
  transfers between devices with their start and end apart: 8 -> 12, of which waited for: 6 -> 9; matrix products, arithmetic and copies ran while one was open for 2% -> 2% of each run, Pallas kernels for 0% -> 0%
where the time goes in v2:
time: 94.5 us; the launch traced here: 94.2 us
  waiting for transfers between devices  41.3 us (44%)
  Pallas kernels  26.5 us (28%)
  starting transfers between devices  23.3 us (25%)
  local copies, waits for them, and re-layouts  1.57 us (2%)
  other arithmetic  1.39 us (1%)
    ppermute x12, waiting for transfers between devices, body(): send = lambda a, perm: lax.ppermute(a, AXES, perm)  41.3 us
    ppermute x12, starting transfers between devices, body(): send = lambda a, perm: lax.ppermute(a, AXES, perm)  23.3 us
    pallas_call x1, Pallas kernels, stacked(): pl.pallas_call(stack_kernel, grid_spec=pltpu.PrefetchScalarGridSpec(num_s...  16.4 us
    pallas_call x1, Pallas kernels, whitened(): pl.pallas_call(spectra_kernel, grid=(4,), out_shape=jax.ShapeDtypeStruct(...  10.1 us
  transfers between devices with their start and end apart: 12, of which 9 were waited for; matrix products, arithmetic and copies ran while one was open for 2% of the time, Pallas kernels for 0%

profile of v2, /device:TPU:4, one launch (start us, length us, event | category | flops | bytes accessed | tf_op | source)
XLA Modules:
  0.0 94.2 jit_solution(6542622325346061271)
XLA Ops:
  0.0 10.1 %whitened_spectra.1 = bf16[96,16,128]{2,1,0:T(8,128)(2,1)} custom-call(s32[16]{0:T(128)} %alive_ref.1, f32[32,16,2000]{2,1,0:T(8,128)} %traces_ref.1, bf16[1152,2048]{1,0:T(8,128)(2,1)} %constant.38.clone.table_ref, bf16[192,192]{1,0:T(8,128)(2,1)} %constant.39.clone.near_ref, f32[192,1]{1,0:T(8,128)} %constant.40.clone.counts_ref, ...), custom_call_target="tpu_custom_call" | custom-call | tf_op jit(solution)/shard_map/whitened_spectra/pallas_call | solution.py:245
  10.1 5.1 %collective-permute-start.3 = (bf16[96,16,128]{2,1,0:T(8,128)(2,1)}, bf16[96,16,128]{2,1,0:T(8,128)(2,1)S(1)}, u32[]{:S(2)}, u32[]{:S(2)}) collective-permute-start(bf16[96,16,128]{2,1,0:T(8,128)(2,1)} %whitened_spectra.1), channel_id=1, source_target_pairs={{0,0},{16,66},{2,32},{18,98},{1,64},{17,2},{3,96},{19,34},{4,48},{... | collective-permute-start | bytes 1179656 | tf_op jit(solution)/shard_map/ppermute | solution.py:384
  15.2 3.9 %collective-permute-start.2 = (bf16[96,16,128]{2,1,0:T(8,128)(2,1)}, bf16[96,16,128]{2,1,0:T(8,128)(2,1)S(1)}, u32[]{:S(2)}, u32[]{:S(2)}) collective-permute-start(bf16[96,16,128]{2,1,0:T(8,128)(2,1)} %whitened_spectra.1), channel_id=1, source_target_pairs={{0,8},{16,17},{2,10},{18,19},{1,9},{17,16},{3,11},{19,18},{4,12},{... | collective-permute-start | bytes 1179656 | tf_op jit(solution)/shard_map/ppermute | solution.py:384
  19.1 2.0 %collective-permute-start = (bf16[96,16,128]{2,1,0:T(8,128)(2,1)}, bf16[96,16,128]{2,1,0:T(8,128)(2,1)S(1)}, u32[]{:S(2)}, u32[]{:S(2)}) collective-permute-start(bf16[96,16,128]{2,1,0:T(8,128)(2,1)} %whitened_spectra.1), channel_id=1, source_target_pairs={{0,4},{16,18},{2,6},{18,17},{1,5},{17,19},{3,7},{19,16},{4,8},{20,... | collective-permute-start | bytes 1179656 | tf_op jit(solution)/shard_map/ppermute | solution.py:384
  21.2 3.2 %collective-permute-done.3 = bf16[96,16,128]{2,1,0:T(8,128)(2,1)S(1)} collective-permute-done((bf16[96,16,128]{2,1,0:T(8,128)(2,1)}, bf16[96,16,128]{2,1,0:T(8,128)(2,1)S(1)}, u32[]{:S(2)}, u32[]{:S(2)}) %collective-permute-start.3) | collective-permute-done | bytes 393248 | tf_op jit(solution)/shard_map/ppermute | solution.py:384
  24.4 5.0 %collective-permute-done.2 = bf16[96,16,128]{2,1,0:T(8,128)(2,1)S(1)} collective-permute-done((bf16[96,16,128]{2,1,0:T(8,128)(2,1)}, bf16[96,16,128]{2,1,0:T(8,128)(2,1)S(1)}, u32[]{:S(2)}, u32[]{:S(2)}) %collective-permute-start.2) | collective-permute-done | bytes 393248 | tf_op jit(solution)/shard_map/ppermute | solution.py:384
  29.4 3.3 %collective-permute-done.1 = bf16[96,16,128]{2,1,0:T(8,128)(2,1)S(1)} collective-permute-done((bf16[96,16,128]{2,1,0:T(8,128)(2,1)}, bf16[96,16,128]{2,1,0:T(8,128)(2,1)S(1)}, u32[]{:S(2)}, u32[]{:S(2)}) %collective-permute-start.1) | collective-permute-done | bytes 393248 | tf_op jit(solution)/shard_map/ppermute | solution.py:384
  32.7 0.8 collective-permute-done
  33.5 1.2 %pad_maximum_fusion.refs_0_ = bf16[4,96,16,128]{3,2,1,0:T(8,128)(2,1)S(1)} fusion(bf16[1,96,16,128]{3,2,1,0:T(8,128)(2,1)S(1)} %bitcast.14, bf16[1,96,16,128]{3,2,1,0:T(8,128)(2,1)S(1)} %bitcast.16, bf16[1,96,16,128]{3,2,1,0:T(8,128)(2,1)S(1)} %bitcast.18, bf16[1,96,16,128]{3,2,1,0:T(8,128)(2,1)} %bitcast.11), kind=kLoop, calls=%fused_computation | loop fusion | flops 2359296 | bytes 3145728 | tf_op jit(solution)/shard_map/stack | solution.py:388
  34.7 2.1 %collective-permute-start.5 = (bf16[4,96,16,128]{3,2,1,0:T(8,128)(2,1)S(1)}, bf16[4,96,16,128]{3,2,1,0:T(8,128)(2,1)S(1)}, u32[]{:S(2)}, u32[]{:S(2)}) collective-permute-start(bf16[4,96,16,128]{3,2,1,0:T(8,128)(2,1)S(1)} %pad_maximum_fusion.refs_0_), channel_id=1, source_target_pairs={{0,3},{16,28},{2,0},{18,30},{1,2},{17,29},{3,1},{19,31},{4,7},{20,... | collective-permute-start | bytes 4718600 | tf_op jit(solution)/shard_map/ppermute | solution.py:384
  36.8 2.9 %collective-permute-start.8 = (bf16[96,16,128]{2,1,0:T(8,128)(2,1)S(1)}, bf16[96,16,128]{2,1,0:T(8,128)(2,1)S(1)}, u32[]{:S(2)}, u32[]{:S(2)}) collective-permute-start(bf16[96,16,128]{2,1,0:T(8,128)(2,1)S(1)} %collective-permute-done.3), channel_id=1, source_target_pairs={{0,64},{16,80},{2,66},{18,82},{1,65},{17,81},{3,67},{19,83},{4,68}... | collective-permute-start | bytes 1179656 | tf_op jit(solution)/shard_map/ppermute | solution.py:384
  39.7 0.7 collective-permute-start.7
  40.5 1.3 %collective-permute-start.6 = (bf16[96,16,128]{2,1,0:T(8,128)(2,1)S(1)}, bf16[96,16,128]{2,1,0:T(8,128)(2,1)S(1)}, u32[]{:S(2)}, u32[]{:S(2)}) collective-permute-start(bf16[96,16,128]{2,1,0:T(8,128)(2,1)S(1)} %collective-permute-done.3), channel_id=1, source_target_pairs={{0,32},{16,48},{2,34},{18,50},{1,33},{17,49},{3,35},{19,51},{4,36}... | collective-permute-start | bytes 1179656 | tf_op jit(solution)/shard_map/ppermute | solution.py:384
  41.8 7.2 %collective-permute-done.8 = bf16[96,16,128]{2,1,0:T(8,128)(2,1)S(1)} collective-permute-done((bf16[96,16,128]{2,1,0:T(8,128)(2,1)S(1)}, bf16[96,16,128]{2,1,0:T(8,128)(2,1)S(1)}, u32[]{:S(2)}, u32[]{:S(2)}) %collective-permute-start.8) | collective-permute-done | bytes 393248 | tf_op jit(solution)/shard_map/ppermute | solution.py:384
  49.0 9.4 %collective-permute-done.7 = bf16[96,16,128]{2,1,0:T(8,128)(2,1)S(1)} collective-permute-done((bf16[96,16,128]{2,1,0:T(8,128)(2,1)S(1)}, bf16[96,16,128]{2,1,0:T(8,128)(2,1)S(1)}, u32[]{:S(2)}, u32[]{:S(2)}) %collective-permute-start.7) | collective-permute-done | bytes 393248 | tf_op jit(solution)/shard_map/ppermute | solution.py:384
  58.4 0.2 collective-permute-done.6
  58.7 0.2 pad_maximum_fusion.1.refs_5_
  58.9 2.6 %collective-permute-start.11 = (bf16[4,96,16,128]{3,2,1,0:T(8,128)(2,1)S(1)}, bf16[4,96,16,128]{3,2,1,0:T(8,128)(2,1)}, u32[]{:S(2)}, u32[]{:S(2)}) collective-permute-start(bf16[4,96,16,128]{3,2,1,0:T(8,128)(2,1)S(1)} %pad_maximum_fusion.1.refs_5_), channel_id=1, source_target_pairs={{0,16},{16,0},{2,18},{18,2},{1,17},{17,1},{3,19},{19,3},{4,20},{20... | collective-permute-start | bytes 4718600 | tf_op jit(solution)/shard_map/ppermute | solution.py:384
  61.6 0.1 slice.7
  61.8 2.7 %collective-permute-start.10 = (bf16[2,96,16,128]{3,2,1,0:T(8,128)(2,1)S(1)}, bf16[2,96,16,128]{3,2,1,0:T(8,128)(2,1)}, u32[]{:S(2)}, u32[]{:S(2)}) collective-permute-start(bf16[2,96,16,128]{3,2,1,0:T(8,128)(2,1)S(1)} %slice.7), channel_id=1, source_target_pairs={{0,3},{16,28},{2,0},{18,30},{1,2},{17,29},{3,1},{19,31},{4,7},{20,... | collective-permute-start | bytes 2359304 | tf_op jit(solution)/shard_map/ppermute | solution.py:384
  64.5 1.3 %dynamic-slice_bitcast_fusion.slots_ref = s32[24]{0:T(128)} fusion(s32[128,24]{1,0:T(8,128)} %constant.44.clone, s32[]{:T(128)S(6)} %select_n.4), kind=kLoop, calls=%fused_computation.2 | loop fusion | bytes 196 | tf_op jit(solution)/shard_map/jit(dynamic_index_in_dim)/squeeze | solution.py:383
  65.7 8.2 %collective-permute-done.10.refs_4_ = bf16[2,96,16,128]{3,2,1,0:T(8,128)(2,1)} collective-permute-done((bf16[2,96,16,128]{3,2,1,0:T(8,128)(2,1)S(1)}, bf16[2,96,16,128]{3,2,1,0:T(8,128)(2,1)}, u32[]{:S(2)}, u32[]{:S(2)}) %collective-permute-start.10) | collective-permute-done | bytes 786464 | tf_op jit(solution)/shard_map/ppermute | solution.py:384
  74.0 3.8 %collective-permute-done.9.refs_3_ = bf16[2,96,16,128]{3,2,1,0:T(8,128)(2,1)} collective-permute-done((bf16[2,96,16,128]{3,2,1,0:T(8,128)(2,1)S(1)}, bf16[2,96,16,128]{3,2,1,0:T(8,128)(2,1)}, u32[]{:S(2)}, u32[]{:S(2)}) %collective-permute-start.9) | collective-permute-done | bytes 786464 | tf_op jit(solution)/shard_map/ppermute | solution.py:384
  77.8 16.4 %stacks.1 = f32[401,64,128]{2,1,0:T(8,128)} custom-call(s32[24]{0:T(128)} %dynamic-slice_bitcast_fusion.slots_ref, bf16[4,96,16,128]{3,2,1,0:T(8,128)(2,1)} %copy-done, bf16[4,96,16,128]{3,2,1,0:T(8,128)(2,1)} %copy-done.3, bf16[4,96,16,128]{3,2,1,0:T(8,128)(2,1)} %copy-done.2, bf16[2,96,16,128]{3,2,1,0:T(8,128)(2,1)} %collective-permute-done.9.refs_3_, ...), custom_call_target="tpu_custom_call" | custom-call | flops 20000000000 | bytes 25165824 | tf_op jit(solution)/shard_map/stacks/pallas_call | solution.py:357
  (15 shorter events, 0.2 us)
Async XLA Ops:
  10.1 14.3 %collective-permute-start.3 = (bf16[96,16,128]{2,1,0:T(8,128)(2,1)}, bf16[96,16,128]{2,1,0:T(8,128)(2,1)S(1)}, u32[]{:S(2)}, u32[]{:S(2)}) collective-permute-start(bf16[96,16,128]{2,1,0:T(8,128)(2,1)} %whitened_spectra.1), channel_id=1, source_target_pairs={{0,0},{16,66},{2,32},{18,98},{1,64},{17,2},{3,96},{19,34},{4,48},{... | collective-permute-start | bytes 1179656 | tf_op jit(solution)/shard_map/ppermute | solution.py:384
  15.2 14.2 %collective-permute-start.2 = (bf16[96,16,128]{2,1,0:T(8,128)(2,1)}, bf16[96,16,128]{2,1,0:T(8,128)(2,1)S(1)}, u32[]{:S(2)}, u32[]{:S(2)}) collective-permute-start(bf16[96,16,128]{2,1,0:T(8,128)(2,1)} %whitened_spectra.1), channel_id=1, source_target_pairs={{0,8},{16,17},{2,10},{18,19},{1,9},{17,16},{3,11},{19,18},{4,12},{... | collective-permute-start | bytes 1179656 | tf_op jit(solution)/shard_map/ppermute | solution.py:384
  19.1 13.6 %collective-permute-start.1 = (bf16[96,16,128]{2,1,0:T(8,128)(2,1)}, bf16[96,16,128]{2,1,0:T(8,128)(2,1)S(1)}, u32[]{:S(2)}, u32[]{:S(2)}) collective-permute-start(bf16[96,16,128]{2,1,0:T(8,128)(2,1)} %whitened_spectra.1), channel_id=1, source_target_pairs={{0,12},{16,19},{2,14},{18,16},{1,13},{17,18},{3,15},{19,17},{4,0},... | collective-permute-start | bytes 1179656 | tf_op jit(solution)/shard_map/ppermute | solution.py:384
  19.1 14.4 %collective-permute-start = (bf16[96,16,128]{2,1,0:T(8,128)(2,1)}, bf16[96,16,128]{2,1,0:T(8,128)(2,1)S(1)}, u32[]{:S(2)}, u32[]{:S(2)}) collective-permute-start(bf16[96,16,128]{2,1,0:T(8,128)(2,1)} %whitened_spectra.1), channel_id=1, source_target_pairs={{0,4},{16,18},{2,6},{18,17},{1,5},{17,19},{3,7},{19,16},{4,8},{20,... | collective-permute-start | bytes 1179656 | tf_op jit(solution)/shard_map/ppermute | solution.py:384
  34.7 24.2 %copy-start = (bf16[4,96,16,128]{3,2,1,0:T(8,128)(2,1)}, bf16[4,96,16,128]{3,2,1,0:T(8,128)(2,1)S(1)}, u32[]{:S(2)}) copy-start(bf16[4,96,16,128]{3,2,1,0:T(8,128)(2,1)S(1)} %pad_maximum_fusion.refs_0_) | copy-start | bytes 4718596
  34.7 23.9 %collective-permute-start.5 = (bf16[4,96,16,128]{3,2,1,0:T(8,128)(2,1)S(1)}, bf16[4,96,16,128]{3,2,1,0:T(8,128)(2,1)S(1)}, u32[]{:S(2)}, u32[]{:S(2)}) collective-permute-start(bf16[4,96,16,128]{3,2,1,0:T(8,128)(2,1)S(1)} %pad_maximum_fusion.refs_0_), channel_id=1, source_target_pairs={{0,3},{16,28},{2,0},{18,30},{1,2},{17,29},{3,1},{19,31},{4,7},{20,... | collective-permute-start | bytes 4718600 | tf_op jit(solution)/shard_map/ppermute | solution.py:384
  36.8 21.9 %collective-permute-start.4 = (bf16[4,96,16,128]{3,2,1,0:T(8,128)(2,1)S(1)}, bf16[4,96,16,128]{3,2,1,0:T(8,128)(2,1)S(1)}, u32[]{:S(2)}, u32[]{:S(2)}) collective-permute-start(bf16[4,96,16,128]{3,2,1,0:T(8,128)(2,1)S(1)} %pad_maximum_fusion.refs_0_), channel_id=1, source_target_pairs={{0,2},{16,20},{2,1},{18,22},{1,3},{17,21},{3,0},{19,23},{4,6},{20,... | collective-permute-start | bytes 4718600 | tf_op jit(solution)/shard_map/ppermute | solution.py:384
  36.8 12.2 %collective-permute-start.8 = (bf16[96,16,128]{2,1,0:T(8,128)(2,1)S(1)}, bf16[96,16,128]{2,1,0:T(8,128)(2,1)S(1)}, u32[]{:S(2)}, u32[]{:S(2)}) collective-permute-start(bf16[96,16,128]{2,1,0:T(8,128)(2,1)S(1)} %collective-permute-done.3), channel_id=1, source_target_pairs={{0,64},{16,80},{2,66},{18,82},{1,65},{17,81},{3,67},{19,83},{4,68}... | collective-permute-start | bytes 1179656 | tf_op jit(solution)/shard_map/ppermute | solution.py:384
  39.7 18.7 %collective-permute-start.7 = (bf16[96,16,128]{2,1,0:T(8,128)(2,1)S(1)}, bf16[96,16,128]{2,1,0:T(8,128)(2,1)S(1)}, u32[]{:S(2)}, u32[]{:S(2)}) collective-permute-start(bf16[96,16,128]{2,1,0:T(8,128)(2,1)S(1)} %collective-permute-done.3), channel_id=1, source_target_pairs={{0,96},{16,112},{2,98},{18,114},{1,97},{17,113},{3,99},{19,115},{4... | collective-permute-start | bytes 1179656 | tf_op jit(solution)/shard_map/ppermute | solution.py:384
  40.5 18.2 %collective-permute-start.6 = (bf16[96,16,128]{2,1,0:T(8,128)(2,1)S(1)}, bf16[96,16,128]{2,1,0:T(8,128)(2,1)S(1)}, u32[]{:S(2)}, u32[]{:S(2)}) collective-permute-start(bf16[96,16,128]{2,1,0:T(8,128)(2,1)S(1)} %collective-permute-done.3), channel_id=1, source_target_pairs={{0,32},{16,48},{2,34},{18,50},{1,33},{17,49},{3,35},{19,51},{4,36}... | collective-permute-start | bytes 1179656 | tf_op jit(solution)/shard_map/ppermute | solution.py:384
  58.6 3.0 %copy-start.2 = (bf16[4,96,16,128]{3,2,1,0:T(8,128)(2,1)}, bf16[4,96,16,128]{3,2,1,0:T(8,128)(2,1)S(1)}, u32[]{:S(2)}) copy-start(bf16[4,96,16,128]{3,2,1,0:T(8,128)(2,1)S(1)} %collective-permute-done.5.refs_2_) | copy-start | bytes 4718596
  58.7 5.8 %copy-start.3 = (bf16[4,96,16,128]{3,2,1,0:T(8,128)(2,1)}, bf16[4,96,16,128]{3,2,1,0:T(8,128)(2,1)S(1)}, u32[]{:S(2)}) copy-start(bf16[4,96,16,128]{3,2,1,0:T(8,128)(2,1)S(1)} %collective-permute-done.4.refs_1_) | copy-start | bytes 4718596
  58.9 2.9 %copy-start.1 = (bf16[4,96,16,128]{3,2,1,0:T(8,128)(2,1)}, bf16[4,96,16,128]{3,2,1,0:T(8,128)(2,1)S(1)}, u32[]{:S(2)}) copy-start(bf16[4,96,16,128]{3,2,1,0:T(8,128)(2,1)S(1)} %pad_maximum_fusion.1.refs_5_) | copy-start | bytes 4718596
  58.9 18.9 %collective-permute-start.11 = (bf16[4,96,16,128]{3,2,1,0:T(8,128)(2,1)S(1)}, bf16[4,96,16,128]{3,2,1,0:T(8,128)(2,1)}, u32[]{:S(2)}, u32[]{:S(2)}) collective-permute-start(bf16[4,96,16,128]{3,2,1,0:T(8,128)(2,1)S(1)} %pad_maximum_fusion.1.refs_5_), channel_id=1, source_target_pairs={{0,16},{16,0},{2,18},{18,2},{1,17},{17,1},{3,19},{19,3},{4,20},{20... | collective-permute-start | bytes 4718600 | tf_op jit(solution)/shard_map/ppermute | solution.py:384
  61.8 12.2 %collective-permute-start.10 = (bf16[2,96,16,128]{3,2,1,0:T(8,128)(2,1)S(1)}, bf16[2,96,16,128]{3,2,1,0:T(8,128)(2,1)}, u32[]{:S(2)}, u32[]{:S(2)}) collective-permute-start(bf16[2,96,16,128]{3,2,1,0:T(8,128)(2,1)S(1)} %slice.7), channel_id=1, source_target_pairs={{0,3},{16,28},{2,0},{18,30},{1,2},{17,29},{3,1},{19,31},{4,7},{20,... | collective-permute-start | bytes 2359304 | tf_op jit(solution)/shard_map/ppermute | solution.py:384
  64.5 13.3 %collective-permute-start.9 = (bf16[2,96,16,128]{3,2,1,0:T(8,128)(2,1)S(1)}, bf16[2,96,16,128]{3,2,1,0:T(8,128)(2,1)}, u32[]{:S(2)}, u32[]{:S(2)}) collective-permute-start(bf16[2,96,16,128]{3,2,1,0:T(8,128)(2,1)S(1)} %slice.6), channel_id=1, source_target_pairs={{0,2},{16,20},{2,1},{18,22},{1,3},{17,21},{3,0},{19,23},{4,6},{20,... | collective-permute-start | bytes 2359304 | tf_op jit(solution)/shard_map/ppermute | solution.py:384

commit v3 on v2

--- a/solution.py
+++ b/solution.py
@@ -18,6 +18,7 @@
 SMOOTH = 5
 SEGS = 64
 PAIRS = NF // 2
+HALF = 1024
 CH = 16
 SEG_DEV = 32
 AXES = ("row", "col", "seg")
@@ -39,17 +40,16 @@
     return np.stack(parts)
 
 
-def forward_table():
-    times = np.arange(NT)
-    window_taper = 0.5 - 0.5 * np.cos((times + 0.5) * (2.0 * np.pi / NT))
-    rows = []
-    for reim in range(2):
-        for kpar in range(2):
-            freqs = F_LO + 2 * np.arange(PAIRS) + kpar
-            phase = np.mod(freqs[:, None] * times[None, :], NT) * (2.0 * np.pi / NT)
-            wave = np.cos(phase) if reim == 0 else -np.sin(phase)
-            rows.append(wave * window_taper[None, :])
-    return np.concatenate(rows, axis=0)
+def forward_tables():
+    times = np.arange(HALF) + 0.5
+    window_taper = (0.5 - 0.5 * np.cos(times * (2.0 * np.pi / NT))) * (np.arange(HALF) < NT // 2)
+    freqs = F_LO + np.concatenate([2 * np.arange(PAIRS), 2 * np.arange(PAIRS) + 1])
+    phase = np.mod(freqs[:, None] * times[None, :], NT) * (2.0 * np.pi / NT)
+    waves = [split_bf16(wave * window_taper, 3) for wave in (np.cos(phase), np.sin(phase))]
+    table = np.concatenate([wave.reshape(3 * NF, HALF) for wave in waves], axis=0)
+    angle = freqs[:, None] * (np.pi / NT)
+    turn = np.concatenate([np.cos(angle), np.sin(angle)], axis=1).astype(np.float32)
+    return table, turn
 
 
 def inverse_table():
@@ -72,20 +72,6 @@
     return near.astype(ml_dtypes.bfloat16), near.sum(axis=1, keepdims=True)
 
 
-def lane_tables():
-    by_channel = np.zeros((512, 512), np.float32)
-    by_group = np.zeros((512, 512), np.float32)
-    seg, ch = np.meshgrid(np.arange(SEG_DEV), np.arange(CH), indexing="ij")
-    by_channel[seg * CH + ch, ch * SEG_DEV + seg] = 1
-    grp, sub, seg = np.meshgrid(np.arange(4), np.arange(4), np.arange(32), indexing="ij")
-    by_group[grp * 128 + sub * 32 + seg, sub * 128 + grp * 32 + seg] = 1
-    rows = np.zeros((128, 128), np.float32)
-    ch, pair = np.meshgrid(np.arange(CH), np.arange(8), indexing="ij")
-    rows[pair * CH + ch, ch * 8 + pair] = 1
-    as16 = lambda t: t.astype(ml_dtypes.bfloat16)
-    return as16(by_channel), as16(by_group), as16(rows)
-
-
 def flat(x, y, z, core):
     return ((x * 2 + core) * 8 + (y * 2 + z % 2)) * 2 + z // 2
 
@@ -113,10 +99,24 @@
     )
 
 
+RING_PLACE = (
+    2, 1, 6, 3, 3, 7, 4, 0, 5, 6, 1, 4, 0, 5, 7, 2, 2, 0, 7, 3, 3, 7, 0, 4, 5, 6, 1, 5, 4, 1, 6, 2,
+    5, 7, 0, 4, 1, 5, 2, 6, 3, 0, 6, 2, 7, 3, 4, 1, 4, 7, 0, 4, 5, 0, 2, 6, 3, 1, 6, 2, 7, 3, 1, 5,
+    1, 2, 2, 6, 6, 3, 7, 4, 4, 7, 5, 0, 0, 5, 3, 1, 0, 2, 2, 7, 7, 3, 6, 4, 5, 6, 4, 0, 1, 5, 3, 1,
+    7, 4, 5, 0, 0, 5, 3, 1, 1, 2, 2, 7, 6, 3, 4, 6, 7, 5, 0, 4, 5, 0, 2, 6, 1, 3, 3, 7, 6, 2, 4, 1,
+)
+
+
+def ring_place(x, y, z, core):
+    return divmod(RING_PLACE[((x * 4 + y) * 4 + z) * 2 + core], 2)
+
+
 def to_readers():
-    return perm_of(
-        lambda x, y, z, core: ((x + y + z + 2 * core) % 4, x, 2 * (y // 2) + core, y % 2)
-    )
+    def move(x, y, z, core):
+        to_x, to_core = ring_place(x, y, z, core)
+        return to_x, x, 2 * (y // 2) + core, to_core
+
+    return perm_of(move)
 
 
 def along_x(n):
@@ -138,12 +138,14 @@
             pos1, pos2 = (first + offsets[k]) % 4, (second - n) % 4
             ys, zs = (pos1, pos2) if core == 0 else (pos2, pos1)
             row[at] = (2 * ys + zs % 2) * 2 + zs // 2
+        held = {
+            ring_place(y, ys, zs, z % 2): (zs // 2) * 4 + (ys % 2) * 2 + zs % 2
+            for ys in (2 * (z // 2), 2 * (z // 2) + 1)
+            for zs in range(4)
+        }
         for other in range(2):
             for k in range(4):
-                c2 = core ^ other
-                ys, xs = 2 * (z // 2) + c2, (x + offsets[k]) % 4
-                zs = (xs - y - ys - 2 * (z % 2)) % 4
-                row[16 + other * 4 + k] = (zs // 2) * 4 + c2 * 2 + zs % 2
+                row[16 + other * 4 + k] = held[(x + offsets[k]) % 4, core ^ other]
     return table
 
 
@@ -162,30 +164,49 @@
     return hi, mid, (rest - mid.astype(F32)).astype(BF16)
 
 
+def mirrored(traces):
+    rows = traces.shape[0]
+    last = NT % 128 - 1
+    lane = lax.broadcasted_iota(jnp.int32, (rows, 128), 1)
+    source = jnp.where(lane <= last, last - lane, last + 128 - lane)
+    tail = jnp.concatenate([traces[:, NT - last - 1:], traces[:, : 127 - last]], axis=1)
+    columns = [tail] + [
+        traces[:, 128 * n:128 * n + 128] for n in range(NT // 128 - 1, NT // 128 - 2 - HALF // 128, -1)
+    ]
+    turned = [jnp.take_along_axis(column, source, axis=1) for column in columns]
+    return jnp.concatenate(
+        [jnp.where(lane <= last, turned[n], turned[n + 1]) for n in range(HALF // 128)], axis=1
+    )
+
+
+def products(table, value):
+    hi, mid, lo = split3(value)
+    by_hi = dot_nt(table, hi)
+    by_mid = dot_nt(table[: 2 * NF], mid)
+    by_lo = dot_nt(table[:NF], lo)
+    small = by_hi[2 * NF:] + by_lo + by_mid[NF:]
+    return by_hi[:NF] + (by_hi[NF:2 * NF] + by_mid[:NF] + small)
+
+
+def ones_at(size, place):
+    row = lax.broadcasted_iota(jnp.int32, (size, size), 0)
+    col = lax.broadcasted_iota(jnp.int32, (size, size), 1)
+    return jnp.where(col == place(row), jnp.float32(1), jnp.float32(0)).astype(BF16)
+
+
 def spectra_kernel(
-    alive_ref, traces_ref, table_ref, near_ref, counts_ref, chan_ref, group_ref, rows_ref,
-    out_ref, total_ref,
+    alive_ref, traces_ref, table_ref, turn_ref, near_ref, counts_ref, out_ref, total_ref,
 ):
     step = pl.program_id(0)
-    lanes = SEG_DEV * CH
-    width = traces_ref.shape[2]
-    traces = traces_ref[...].reshape(lanes, width)
-    inside = lax.broadcasted_iota(jnp.int32, (1, width), 1) < NT - step * width
-    hi, mid, lo = split3(jnp.where(inside, traces, 0.0))
-    rows = 2 * NF
-    by_hi = dot_nt(table_ref[...], hi)
-    by_mid = dot_nt(table_ref[: 2 * rows], mid)
-    by_lo = dot_nt(table_ref[:rows], lo)
-    small = by_hi[2 * rows :] + by_lo + by_mid[rows:]
-    added = by_hi[:rows] + (by_hi[rows : 2 * rows] + by_mid[:rows] + small)
-
-    @pl.when(step == 0)
-    def _():
-        total_ref[...] = added
-
-    @pl.when(step > 0)
-    def _():
-        total_ref[...] += added
+    lanes = traces_ref.shape[0] * CH
+    traces = traces_ref[...].reshape(lanes, NT)
+    front, back = traces[:, :HALF], mirrored(traces)
+    even = products(table_ref[: 3 * NF], front + back)
+    odd = products(table_ref[3 * NF:], front - back)
+    cos, sin = turn_ref[:, 0:1], turn_ref[:, 1:2]
+    at = pl.ds(pl.multiple_of(step * lanes, 128), lanes)
+    total_ref[:NF, at] = even * cos + odd * sin
+    total_ref[NF:, at] = even * sin - odd * cos
 
     @pl.when(step == pl.num_programs(0) - 1)
     def _():
@@ -197,7 +218,7 @@
         water = jnp.sum(magnitude, axis=0, keepdims=True) * (1.0 / NF)
         weight = 1.0 / (smooth + 0.05 * water + 1e-6)
         white = jnp.concatenate([real * weight, imag * weight], axis=0).astype(BF16)
-        by_channel = dot_nn(white, chan_ref[...]).astype(BF16)
+        by_channel = dot_nn(white, ones_at(512, lambda n: (n % CH) * SEG_DEV + n // CH)).astype(BF16)
         alive = [alive_ref[c].astype(F32) for c in range(CH)]
         lhs = jnp.concatenate(
             [
@@ -209,7 +230,8 @@
             ],
             axis=0,
         )
-        grouped = dot_nn(lhs, group_ref[...])
+        by_pair = ones_at(128, lambda n: (n % CH) * 8 + n // CH)
+        grouped = dot_nn(lhs, ones_at(512, lambda n: (n // 32 % 4) * 128 + (n // 128) * 32 + n % 32))
         for half in range(PAIRS // 16):
             cols = []
             for part in range(2):
@@ -228,66 +250,67 @@
                     )
                 )
             block = jnp.concatenate(cols, axis=1).astype(BF16)
-            block = dot_nn(rows_ref[...], block).astype(BF16)
+            block = dot_nn(by_pair, block).astype(BF16)
             for part in range(2):
                 at = 16 * half + 8 * part
                 out_ref[at:at + 8] = block[:, 128 * part:128 * part + 128].reshape(8, CH, 128)
 
 
 def whitened(traces, alive):
-    width = 512
+    steps = 2
     near, counts = smoothing_tables()
-    by_channel, by_group, rows = lane_tables()
-    table = split_bf16(forward_table(), 3).reshape(6 * NF, NT)
-    table = np.concatenate([table, np.zeros((6 * NF, 4 * width - NT), table.dtype)], axis=1)
+    consts = forward_tables() + (near, counts)
     whole = lambda a: pl.BlockSpec(a.shape, lambda i: (0,) * a.ndim)
-    consts = (near, counts, by_channel, by_group, rows)
     return pl.pallas_call(
         spectra_kernel,
-        grid=(4,),
+        grid=(steps,),
         out_shape=jax.ShapeDtypeStruct((PAIRS, CH, 128), BF16),
         in_specs=[
             pl.BlockSpec(memory_space=pltpu.SMEM),
-            pl.BlockSpec((SEG_DEV, CH, width), lambda i: (0, 0, i)),
-            pl.BlockSpec((6 * NF, width), lambda i: (0, i)),
+            pl.BlockSpec((SEG_DEV // steps, CH, NT), lambda i: (i, 0, 0)),
         ]
         + [whole(a) for a in consts],
         out_specs=pl.BlockSpec((PAIRS, CH, 128), lambda i: (0, 0, 0)),
         scratch_shapes=[pltpu.VMEM((2 * NF, SEG_DEV * CH), F32)],
         compiler_params=pltpu.CompilerParams(vmem_limit_bytes=VMEM),
         name="whitened_spectra",
-    )(alive, traces, *(jnp.asarray(a) for a in (table,) + consts))
-
-
-CHUNKS = 4
+    )(alive, traces, *(jnp.asarray(a) for a in consts))
+
+
+CHUNKS = 3
+AHEAD = 2
 PER = PAIRS // CHUNKS
 J_STEP = 8
 
 
 def stack_kernel(slots_ref, *refs):
-    sources, table_ref, out_ref = refs[:7], refs[7], refs[8]
-    left, right = refs[9:11]
-    cross_refs, sems = refs[11:15], refs[15]
+    sources, table_ref, out_ref = refs[:10], refs[10], refs[11]
+    left, right, waves = refs[12:15]
+    cross_refs, sems, wave_sem = refs[15:19], refs[19], refs[20]
     step = pl.program_id(0)
 
     def copies(chunk):
         at = pl.ds(chunk * PER, PER)
         found = []
         for ref in sources:
-            for k in range(ref.shape[0]):
+            for k in range(ref.shape[0] if len(ref.shape) == 4 else 1):
                 to = left if len(found) < 16 else right
-                found.append((ref.at[k, at], to.at[slots_ref[len(found)], at]))
+                part = ref.at[k, at] if len(ref.shape) == 4 else ref.at[at]
+                found.append((part, to.at[slots_ref[len(found)], at]))
         return [
             pltpu.make_async_copy(src, dst, sems.at[chunk, n])
             for n, (src, dst) in enumerate(found)
         ]
 
+    table_copy = pltpu.make_async_copy(table_ref, waves, wave_sem)
+
     @pl.when(step == 0)
     def _():
         pending = [copies(chunk) for chunk in range(CHUNKS)]
-        for chunk in pending:
+        for chunk in pending[:AHEAD]:
             for copy in chunk:
                 copy.start()
+        table_copy.start()
         lane = lax.broadcasted_iota(jnp.int32, (CH, 128), 1)
         even = (lane // 32) % 2 == 0
         one, zero = jnp.float32(1), jnp.float32(0)
@@ -323,7 +346,11 @@
         for chunk in range(CHUNKS):
             for copy in pending[chunk]:
                 copy.wait()
+            for late in pending[chunk + AHEAD:chunk + AHEAD + 1]:
+                for copy in late:
+                    copy.start()
             lax.fori_loop(chunk * PER, (chunk + 1) * PER, cross, 0, unroll=UNROLL)
+        table_copy.wait()
 
     out_rows = out_ref.reshape(LAGS * J_STEP, 128)
     turned = 7 - lax.broadcasted_iota(jnp.int32, (LAG_ROWS // 8, 8, 128), 1)
@@ -337,7 +364,7 @@
                 x = [cross_refs[2 * kpar + reim][at, :].astype(BF16) for kpar in range(2)]
                 cols.append(jnp.concatenate(x * TERMS, axis=0))
             rows = slice(LAG_ROWS * reim, LAG_ROWS * (reim + 1))
-            halves.append(dot_nn(table_ref[rows, :], jnp.concatenate(cols, axis=1)))
+            halves.append(dot_nn(waves[rows, :], jnp.concatenate(cols, axis=1)))
         later, earlier = halves[0] + halves[1], halves[0] - halves[1]
         for e in range(2):
             lanes, j = slice(128 * e, 128 * e + 128), 2 * pair + e
@@ -349,7 +376,7 @@
             out_rows[pl.ds(MAXLAG * J_STEP + j, MAXLAG + 1, stride=J_STEP), :] = later[: MAXLAG + 1, lanes]
 
 
-UNROLL = 24
+UNROLL = 32
 
 
 def stacked(slots, sources, table):
@@ -359,14 +386,15 @@
         grid_spec=pltpu.PrefetchScalarGridSpec(
             num_scalar_prefetch=1,
             grid=(64 // J_STEP,),
-            in_specs=[any_spec] * len(sources) + [pl.BlockSpec(table.shape, lambda u, s: (0, 0))],
+            in_specs=[any_spec] * (len(sources) + 1),
             out_specs=pl.BlockSpec((LAGS, J_STEP, 128), lambda u, s: (0, u, 0)),
             scratch_shapes=[
                 pltpu.VMEM((16, PAIRS, CH, 128), BF16),
                 pltpu.VMEM((8, PAIRS, CH, 128), BF16),
+                pltpu.VMEM(table.shape, BF16),
             ]
             + [pltpu.VMEM((64 * XROWS, 128), F32)] * 4
-            + [pltpu.SemaphoreType.DMA((CHUNKS, 24))],
+            + [pltpu.SemaphoreType.DMA((CHUNKS, 24)), pltpu.SemaphoreType.DMA],
         ),
         out_shape=jax.ShapeDtypeStruct((LAGS, 64, 128), F32),
         compiler_params=pltpu.CompilerParams(vmem_limit_bytes=VMEM),
@@ -392,7 +420,7 @@
     seconds = jnp.stack(seconds)
     far_up, far_down = send(up[:2], along_second(1)), send(down[2:], along_second(-1))
     others = send(seconds, other_core())
-    sources = (mine, up, down, far_up, far_down, seconds, others)
+    sources = (*first, up, down, far_up, far_down, seconds, others)
     out = stacked(slots, sources, jnp.asarray(inverse_table()))
     return jnp.transpose(out, (2, 1, 0))
 

time: 94.5 us -> 91.2 us (0.965)
  Pallas kernels: 26.5 us -> 23.2 us
  starting transfers between devices: 23.3 us -> 20.7 us
  waiting for transfers between devices: 41.3 us -> 43.5 us
    ppermute x12, starting transfers between devices: 23.3 us -> 20.7 us  [body(): send = lambda a, perm: lax.ppermute(a, AXES, perm)]
    pallas_call x1, Pallas kernels: 10.1 us -> 7.93 us  [whitened(): pl.pallas_call(spectra_kernel, grid=(steps,), out_shape=jax.ShapeDtypeStr...]
    ppermute x12, waiting for transfers between devices: 41.3 us -> 43.5 us  [body(): send = lambda a, perm: lax.ppermute(a, AXES, perm)]
    pallas_call x1, Pallas kernels: 16.4 us -> 15.2 us  [stacked(): pl.pallas_call(stack_kernel, grid_spec=pltpu.PrefetchScalarGridSpec(num_s...]
where the time goes in v3:
time: 91.2 us; the launch traced here: 91 us
  waiting for transfers between devices  43.5 us (48%)
  Pallas kernels  23.2 us (25%)
  starting transfers between devices  20.7 us (23%)
  local copies, waits for them, and re-layouts  1.95 us (2%)
  other arithmetic  1.53 us (2%)
    ppermute x12, waiting for transfers between devices, body(): send = lambda a, perm: lax.ppermute(a, AXES, perm)  43.5 us
    ppermute x12, starting transfers between devices, body(): send = lambda a, perm: lax.ppermute(a, AXES, perm)  20.7 us
    pallas_call x1, Pallas kernels, stacked(): pl.pallas_call(stack_kernel, grid_spec=pltpu.PrefetchScalarGridSpec(num_s...  15.2 us
    pallas_call x1, Pallas kernels, whitened(): pl.pallas_call(spectra_kernel, grid=(steps,), out_shape=jax.ShapeDtypeStr...  7.93 us
  transfers between devices with their start and end apart: 12, of which 9 were waited for; matrix products, arithmetic and copies ran while one was open for 2% of the time, Pallas kernels for 0%

profile of v3, /device:TPU:4, one launch (start us, length us, event | category | flops | bytes accessed | tf_op | source)
XLA Modules:
  0.0 91.0 jit_solution(3585407141361320057)
XLA Ops:
  0.0 7.9 %whitened_spectra.1.refs_0_ = bf16[96,16,128]{2,1,0:T(8,128)(2,1)} custom-call(s32[16]{0:T(128)} %alive_ref.1, f32[32,16,2000]{2,1,0:T(8,128)} %traces_ref.1, bf16[1152,1024]{1,0:T(8,128)(2,1)} %constant.34.clone.table_ref, f32[192,2]{1,0:T(8,128)} %constant.35.clone.turn_ref, bf16[192,192]{1,0:T(8,128)(2,1)} %constant.36.clone.near_ref, ...), custom_call_target="tpu_custom_call" | custom-call | tf_op jit(solution)/shard_map/whitened_spectra/pallas_call | solution.py:264
  7.9 4.5 %collective-permute-start.3 = (bf16[96,16,128]{2,1,0:T(8,128)(2,1)}, bf16[96,16,128]{2,1,0:T(8,128)(2,1)S(1)}, u32[]{:S(2)}, u32[]{:S(2)}) collective-permute-start(bf16[96,16,128]{2,1,0:T(8,128)(2,1)} %whitened_spectra.1.refs_0_), channel_id=1, source_target_pairs={{0,32},{16,18},{2,96},{18,50},{1,48},{17,114},{3,64},{19,2},{4,80}... | collective-permute-start | bytes 1179656 | tf_op jit(solution)/shard_map/ppermute | solution.py:412
  12.4 4.5 %collective-permute-start.2 = (bf16[96,16,128]{2,1,0:T(8,128)(2,1)}, bf16[96,16,128]{2,1,0:T(8,128)(2,1)S(1)}, u32[]{:S(2)}, u32[]{:S(2)}) collective-permute-start(bf16[96,16,128]{2,1,0:T(8,128)(2,1)} %whitened_spectra.1.refs_0_), channel_id=1, source_target_pairs={{0,8},{16,17},{2,10},{18,19},{1,9},{17,16},{3,11},{19,18},{4,12},{... | collective-permute-start | bytes 1179656 | tf_op jit(solution)/shard_map/ppermute | solution.py:412
  16.9 2.0 %collective-permute-start = (bf16[96,16,128]{2,1,0:T(8,128)(2,1)}, bf16[96,16,128]{2,1,0:T(8,128)(2,1)S(1)}, u32[]{:S(2)}, u32[]{:S(2)}) collective-permute-start(bf16[96,16,128]{2,1,0:T(8,128)(2,1)} %whitened_spectra.1.refs_0_), channel_id=1, source_target_pairs={{0,4},{16,18},{2,6},{18,17},{1,5},{17,19},{3,7},{19,16},{4,8},{20,... | collective-permute-start | bytes 1179656 | tf_op jit(solution)/shard_map/ppermute | solution.py:412
  19.0 4.8 %collective-permute-done.3 = bf16[96,16,128]{2,1,0:T(8,128)(2,1)S(1)} collective-permute-done((bf16[96,16,128]{2,1,0:T(8,128)(2,1)}, bf16[96,16,128]{2,1,0:T(8,128)(2,1)S(1)}, u32[]{:S(2)}, u32[]{:S(2)}) %collective-permute-start.3) | collective-permute-done | bytes 393248 | tf_op jit(solution)/shard_map/ppermute | solution.py:412
  23.7 4.0 %collective-permute-done.2.refs_3_ = bf16[96,16,128]{2,1,0:T(8,128)(2,1)S(1)} collective-permute-done((bf16[96,16,128]{2,1,0:T(8,128)(2,1)}, bf16[96,16,128]{2,1,0:T(8,128)(2,1)S(1)}, u32[]{:S(2)}, u32[]{:S(2)}) %collective-permute-start.2) | collective-permute-done | bytes 393248 | tf_op jit(solution)/shard_map/ppermute | solution.py:412
  27.8 1.7 %collective-permute-done.1.refs_2_ = bf16[96,16,128]{2,1,0:T(8,128)(2,1)S(1)} collective-permute-done((bf16[96,16,128]{2,1,0:T(8,128)(2,1)}, bf16[96,16,128]{2,1,0:T(8,128)(2,1)S(1)}, u32[]{:S(2)}, u32[]{:S(2)}) %collective-permute-start.1) | collective-permute-done | bytes 393248 | tf_op jit(solution)/shard_map/ppermute | solution.py:412
  29.5 2.4 %collective-permute-done.refs_1_ = bf16[96,16,128]{2,1,0:T(8,128)(2,1)S(1)} collective-permute-done((bf16[96,16,128]{2,1,0:T(8,128)(2,1)}, bf16[96,16,128]{2,1,0:T(8,128)(2,1)S(1)}, u32[]{:S(2)}, u32[]{:S(2)}) %collective-permute-start) | collective-permute-done | bytes 393248 | tf_op jit(solution)/shard_map/ppermute | solution.py:412
  31.9 1.3 %pad_maximum_fusion = bf16[4,96,16,128]{3,2,1,0:T(8,128)(2,1)S(1)} fusion(bf16[1,96,16,128]{3,2,1,0:T(8,128)(2,1)S(1)} %bitcast.12, bf16[1,96,16,128]{3,2,1,0:T(8,128)(2,1)S(1)} %bitcast.13, bf16[1,96,16,128]{3,2,1,0:T(8,128)(2,1)S(1)} %bitcast.14, bf16[1,96,16,128]{3,2,1,0:T(8,128)(2,1)} %bitcast.11), kind=kLoop, calls=%fused_computation | loop fusion | flops 2359296 | bytes 3145728 | tf_op jit(solution)/shard_map/stack | solution.py:416
  33.3 1.8 %collective-permute-start.5 = (bf16[4,96,16,128]{3,2,1,0:T(8,128)(2,1)S(1)}, bf16[4,96,16,128]{3,2,1,0:T(8,128)(2,1)S(1)}, u32[]{:S(2)}, u32[]{:S(2)}) collective-permute-start(bf16[4,96,16,128]{3,2,1,0:T(8,128)(2,1)S(1)} %pad_maximum_fusion), channel_id=1, source_target_pairs={{0,3},{16,28},{2,0},{18,30},{1,2},{17,29},{3,1},{19,31},{4,7},{20,... | collective-permute-start | bytes 4718600 | tf_op jit(solution)/shard_map/ppermute | solution.py:412
  35.0 0.3 collective-permute-start.4
  35.4 3.5 %collective-permute-start.7 = (bf16[96,16,128]{2,1,0:T(8,128)(2,1)S(1)}, bf16[96,16,128]{2,1,0:T(8,128)(2,1)S(1)}, u32[]{:S(2)}, u32[]{:S(2)}) collective-permute-start(bf16[96,16,128]{2,1,0:T(8,128)(2,1)S(1)} %collective-permute-done.3), channel_id=1, source_target_pairs={{0,96},{16,112},{2,98},{18,114},{1,97},{17,113},{3,99},{19,115},{4... | collective-permute-start | bytes 1179656 | tf_op jit(solution)/shard_map/ppermute | solution.py:412
  38.9 8.4 %collective-permute-done.8 = bf16[96,16,128]{2,1,0:T(8,128)(2,1)S(1)} collective-permute-done((bf16[96,16,128]{2,1,0:T(8,128)(2,1)S(1)}, bf16[96,16,128]{2,1,0:T(8,128)(2,1)S(1)}, u32[]{:S(2)}, u32[]{:S(2)}) %collective-permute-start.8) | collective-permute-done | bytes 393248 | tf_op jit(solution)/shard_map/ppermute | solution.py:412
  47.3 7.9 %collective-permute-done.7 = bf16[96,16,128]{2,1,0:T(8,128)(2,1)S(1)} collective-permute-done((bf16[96,16,128]{2,1,0:T(8,128)(2,1)S(1)}, bf16[96,16,128]{2,1,0:T(8,128)(2,1)S(1)}, u32[]{:S(2)}, u32[]{:S(2)}) %collective-permute-start.7) | collective-permute-done | bytes 393248 | tf_op jit(solution)/shard_map/ppermute | solution.py:412
  55.3 2.0 %collective-permute-done.6 = bf16[96,16,128]{2,1,0:T(8,128)(2,1)S(1)} collective-permute-done((bf16[96,16,128]{2,1,0:T(8,128)(2,1)S(1)}, bf16[96,16,128]{2,1,0:T(8,128)(2,1)S(1)}, u32[]{:S(2)}, u32[]{:S(2)}) %collective-permute-start.6) | collective-permute-done | bytes 393248 | tf_op jit(solution)/shard_map/ppermute | solution.py:412
  57.3 0.2 pad_maximum_fusion.1.refs_8_
  57.5 1.1 %collective-permute-start.11 = (bf16[4,96,16,128]{3,2,1,0:T(8,128)(2,1)S(1)}, bf16[4,96,16,128]{3,2,1,0:T(8,128)(2,1)}, u32[]{:S(2)}, u32[]{:S(2)}) collective-permute-start(bf16[4,96,16,128]{3,2,1,0:T(8,128)(2,1)S(1)} %pad_maximum_fusion.1.refs_8_), channel_id=1, source_target_pairs={{0,16},{16,0},{2,18},{18,2},{1,17},{17,1},{3,19},{19,3},{4,20},{20... | collective-permute-start | bytes 4718600 | tf_op jit(solution)/shard_map/ppermute | solution.py:412
  58.8 0.1 copy-done.4
  59.1 0.4 copy-done
  59.4 2.9 %collective-permute-start.10 = (bf16[2,96,16,128]{3,2,1,0:T(8,128)(2,1)S(1)}, bf16[2,96,16,128]{3,2,1,0:T(8,128)(2,1)}, u32[]{:S(2)}, u32[]{:S(2)}) collective-permute-start(bf16[2,96,16,128]{3,2,1,0:T(8,128)(2,1)S(1)} %slice.7), channel_id=1, source_target_pairs={{0,3},{16,28},{2,0},{18,30},{1,2},{17,29},{3,1},{19,31},{4,7},{20,... | collective-permute-start | bytes 2359304 | tf_op jit(solution)/shard_map/ppermute | solution.py:412
  62.3 1.2 %dynamic-slice_bitcast_fusion.slots_ref = s32[24]{0:T(128)} fusion(s32[128,24]{1,0:T(8,128)} %constant.38.clone, s32[]{:T(128)S(6)} %select_n.4), kind=kLoop, calls=%fused_computation.2 | loop fusion | bytes 196 | tf_op jit(solution)/shard_map/jit(dynamic_index_in_dim)/squeeze | solution.py:411
  63.5 8.3 %collective-permute-done.10.refs_7_ = bf16[2,96,16,128]{3,2,1,0:T(8,128)(2,1)} collective-permute-done((bf16[2,96,16,128]{3,2,1,0:T(8,128)(2,1)S(1)}, bf16[2,96,16,128]{3,2,1,0:T(8,128)(2,1)}, u32[]{:S(2)}, u32[]{:S(2)}) %collective-permute-start.10) | collective-permute-done | bytes 786464 | tf_op jit(solution)/shard_map/ppermute | solution.py:412
  71.8 3.8 %collective-permute-done.9.refs_6_ = bf16[2,96,16,128]{3,2,1,0:T(8,128)(2,1)} collective-permute-done((bf16[2,96,16,128]{3,2,1,0:T(8,128)(2,1)S(1)}, bf16[2,96,16,128]{3,2,1,0:T(8,128)(2,1)}, u32[]{:S(2)}, u32[]{:S(2)}) %collective-permute-start.9) | collective-permute-done | bytes 786464 | tf_op jit(solution)/shard_map/ppermute | solution.py:412
  75.6 15.2 %stacks.1 = f32[401,64,128]{2,1,0:T(8,128)} custom-call(s32[24]{0:T(128)} %dynamic-slice_bitcast_fusion.slots_ref, bf16[96,16,128]{2,1,0:T(8,128)(2,1)} %whitened_spectra.1.refs_0_, bf16[96,16,128]{2,1,0:T(8,128)(2,1)} %copy-done.3, bf16[96,16,128]{2,1,0:T(8,128)(2,1)} %copy-done.2, bf16[96,16,128]{2,1,0:T(8,128)(2,1)} %copy-done.1, ...), custom_call_target="tpu_custom_call" | custom-call | flops 20000000000 | bytes 25165824 | tf_op jit(solution)/shard_map/stacks/pallas_call | solution.py:384
  (19 shorter events, 0.3 us)
Async XLA Ops:
  7.9 15.8 %collective-permute-start.3 = (bf16[96,16,128]{2,1,0:T(8,128)(2,1)}, bf16[96,16,128]{2,1,0:T(8,128)(2,1)S(1)}, u32[]{:S(2)}, u32[]{:S(2)}) collective-permute-start(bf16[96,16,128]{2,1,0:T(8,128)(2,1)} %whitened_spectra.1.refs_0_), channel_id=1, source_target_pairs={{0,32},{16,18},{2,96},{18,50},{1,48},{17,114},{3,64},{19,2},{4,80}... | collective-permute-start | bytes 1179656 | tf_op jit(solution)/shard_map/ppermute | solution.py:412
  12.4 15.4 %collective-permute-start.2 = (bf16[96,16,128]{2,1,0:T(8,128)(2,1)}, bf16[96,16,128]{2,1,0:T(8,128)(2,1)S(1)}, u32[]{:S(2)}, u32[]{:S(2)}) collective-permute-start(bf16[96,16,128]{2,1,0:T(8,128)(2,1)} %whitened_spectra.1.refs_0_), channel_id=1, source_target_pairs={{0,8},{16,17},{2,10},{18,19},{1,9},{17,16},{3,11},{19,18},{4,12},{... | collective-permute-start | bytes 1179656 | tf_op jit(solution)/shard_map/ppermute | solution.py:412
  16.9 12.6 %collective-permute-start.1 = (bf16[96,16,128]{2,1,0:T(8,128)(2,1)}, bf16[96,16,128]{2,1,0:T(8,128)(2,1)S(1)}, u32[]{:S(2)}, u32[]{:S(2)}) collective-permute-start(bf16[96,16,128]{2,1,0:T(8,128)(2,1)} %whitened_spectra.1.refs_0_), channel_id=1, source_target_pairs={{0,12},{16,19},{2,14},{18,16},{1,13},{17,18},{3,15},{19,17},{4,0},... | collective-permute-start | bytes 1179656 | tf_op jit(solution)/shard_map/ppermute | solution.py:412
  16.9 15.0 %collective-permute-start = (bf16[96,16,128]{2,1,0:T(8,128)(2,1)}, bf16[96,16,128]{2,1,0:T(8,128)(2,1)S(1)}, u32[]{:S(2)}, u32[]{:S(2)}) collective-permute-start(bf16[96,16,128]{2,1,0:T(8,128)(2,1)} %whitened_spectra.1.refs_0_), channel_id=1, source_target_pairs={{0,4},{16,18},{2,6},{18,17},{1,5},{17,19},{3,7},{19,16},{4,8},{20,... | collective-permute-start | bytes 1179656 | tf_op jit(solution)/shard_map/ppermute | solution.py:412
  27.8 5.4 %copy-start.1 = (bf16[96,16,128]{2,1,0:T(8,128)(2,1)}, bf16[96,16,128]{2,1,0:T(8,128)(2,1)S(1)}, u32[]{:S(2)}) copy-start(bf16[96,16,128]{2,1,0:T(8,128)(2,1)S(1)} %collective-permute-done.2.refs_3_) | copy-start | bytes 1179652
  29.5 3.8 %copy-start.2 = (bf16[96,16,128]{2,1,0:T(8,128)(2,1)}, bf16[96,16,128]{2,1,0:T(8,128)(2,1)S(1)}, u32[]{:S(2)}) copy-start(bf16[96,16,128]{2,1,0:T(8,128)(2,1)S(1)} %collective-permute-done.1.refs_2_) | copy-start | bytes 1179652
  31.9 1.4 %copy-start.3 = (bf16[96,16,128]{2,1,0:T(8,128)(2,1)}, bf16[96,16,128]{2,1,0:T(8,128)(2,1)S(1)}, u32[]{:S(2)}) copy-start(bf16[96,16,128]{2,1,0:T(8,128)(2,1)S(1)} %collective-permute-done.refs_1_) | copy-start | bytes 1179652
  33.3 24.0 %collective-permute-start.5 = (bf16[4,96,16,128]{3,2,1,0:T(8,128)(2,1)S(1)}, bf16[4,96,16,128]{3,2,1,0:T(8,128)(2,1)S(1)}, u32[]{:S(2)}, u32[]{:S(2)}) collective-permute-start(bf16[4,96,16,128]{3,2,1,0:T(8,128)(2,1)S(1)} %pad_maximum_fusion), channel_id=1, source_target_pairs={{0,3},{16,28},{2,0},{18,30},{1,2},{17,29},{3,1},{19,31},{4,7},{20,... | collective-permute-start | bytes 4718600 | tf_op jit(solution)/shard_map/ppermute | solution.py:412
  35.0 22.3 %collective-permute-start.4 = (bf16[4,96,16,128]{3,2,1,0:T(8,128)(2,1)S(1)}, bf16[4,96,16,128]{3,2,1,0:T(8,128)(2,1)S(1)}, u32[]{:S(2)}, u32[]{:S(2)}) collective-permute-start(bf16[4,96,16,128]{3,2,1,0:T(8,128)(2,1)S(1)} %pad_maximum_fusion), channel_id=1, source_target_pairs={{0,2},{16,20},{2,1},{18,22},{1,3},{17,21},{3,0},{19,23},{4,6},{20,... | collective-permute-start | bytes 4718600 | tf_op jit(solution)/shard_map/ppermute | solution.py:412
  35.4 12.0 %collective-permute-start.8 = (bf16[96,16,128]{2,1,0:T(8,128)(2,1)S(1)}, bf16[96,16,128]{2,1,0:T(8,128)(2,1)S(1)}, u32[]{:S(2)}, u32[]{:S(2)}) collective-permute-start(bf16[96,16,128]{2,1,0:T(8,128)(2,1)S(1)} %collective-permute-done.3), channel_id=1, source_target_pairs={{0,64},{16,80},{2,66},{18,82},{1,65},{17,81},{3,67},{19,83},{4,68}... | collective-permute-start | bytes 1179656 | tf_op jit(solution)/shard_map/ppermute | solution.py:412
  35.4 19.9 %collective-permute-start.7 = (bf16[96,16,128]{2,1,0:T(8,128)(2,1)S(1)}, bf16[96,16,128]{2,1,0:T(8,128)(2,1)S(1)}, u32[]{:S(2)}, u32[]{:S(2)}) collective-permute-start(bf16[96,16,128]{2,1,0:T(8,128)(2,1)S(1)} %collective-permute-done.3), channel_id=1, source_target_pairs={{0,96},{16,112},{2,98},{18,114},{1,97},{17,113},{3,99},{19,115},{4... | collective-permute-start | bytes 1179656 | tf_op jit(solution)/shard_map/ppermute | solution.py:412
  38.9 18.4 %collective-permute-start.6 = (bf16[96,16,128]{2,1,0:T(8,128)(2,1)S(1)}, bf16[96,16,128]{2,1,0:T(8,128)(2,1)S(1)}, u32[]{:S(2)}, u32[]{:S(2)}) collective-permute-start(bf16[96,16,128]{2,1,0:T(8,128)(2,1)S(1)} %collective-permute-done.3), channel_id=1, source_target_pairs={{0,32},{16,48},{2,34},{18,50},{1,33},{17,49},{3,35},{19,51},{4,36}... | collective-permute-start | bytes 1179656 | tf_op jit(solution)/shard_map/ppermute | solution.py:412
  57.3 1.6 %copy-start.4 = (bf16[4,96,16,128]{3,2,1,0:T(8,128)(2,1)}, bf16[4,96,16,128]{3,2,1,0:T(8,128)(2,1)S(1)}, u32[]{:S(2)}) copy-start(bf16[4,96,16,128]{3,2,1,0:T(8,128)(2,1)S(1)} %collective-permute-done.5.refs_5_) | copy-start | bytes 4718596
  57.3 1.4 %copy-start.5 = (bf16[4,96,16,128]{3,2,1,0:T(8,128)(2,1)}, bf16[4,96,16,128]{3,2,1,0:T(8,128)(2,1)S(1)}, u32[]{:S(2)}) copy-start(bf16[4,96,16,128]{3,2,1,0:T(8,128)(2,1)S(1)} %collective-permute-done.4.refs_4_) | copy-start | bytes 4718596
  57.5 1.9 %copy-start = (bf16[4,96,16,128]{3,2,1,0:T(8,128)(2,1)}, bf16[4,96,16,128]{3,2,1,0:T(8,128)(2,1)S(1)}, u32[]{:S(2)}) copy-start(bf16[4,96,16,128]{3,2,1,0:T(8,128)(2,1)S(1)} %pad_maximum_fusion.1.refs_8_) | copy-start | bytes 4718596
  57.5 18.1 %collective-permute-start.11 = (bf16[4,96,16,128]{3,2,1,0:T(8,128)(2,1)S(1)}, bf16[4,96,16,128]{3,2,1,0:T(8,128)(2,1)}, u32[]{:S(2)}, u32[]{:S(2)}) collective-permute-start(bf16[4,96,16,128]{3,2,1,0:T(8,128)(2,1)S(1)} %pad_maximum_fusion.1.refs_8_), channel_id=1, source_target_pairs={{0,16},{16,0},{2,18},{18,2},{1,17},{17,1},{3,19},{19,3},{4,20},{20... | collective-permute-start | bytes 4718600 | tf_op jit(solution)/shard_map/ppermute | solution.py:412
  59.4 12.4 %collective-permute-start.10 = (bf16[2,96,16,128]{3,2,1,0:T(8,128)(2,1)S(1)}, bf16[2,96,16,128]{3,2,1,0:T(8,128)(2,1)}, u32[]{:S(2)}, u32[]{:S(2)}) collective-permute-start(bf16[2,96,16,128]{3,2,1,0:T(8,128)(2,1)S(1)} %slice.7), channel_id=1, source_target_pairs={{0,3},{16,28},{2,0},{18,30},{1,2},{17,29},{3,1},{19,31},{4,7},{20,... | collective-permute-start | bytes 2359304 | tf_op jit(solution)/shard_map/ppermute | solution.py:412
  62.3 13.3 %collective-permute-start.9 = (bf16[2,96,16,128]{3,2,1,0:T(8,128)(2,1)S(1)}, bf16[2,96,16,128]{3,2,1,0:T(8,128)(2,1)}, u32[]{:S(2)}, u32[]{:S(2)}) collective-permute-start(bf16[2,96,16,128]{3,2,1,0:T(8,128)(2,1)S(1)} %slice.6), channel_id=1, source_target_pairs={{0,2},{16,20},{2,1},{18,22},{1,3},{17,21},{3,0},{19,23},{4,6},{20,... | collective-permute-start | bytes 2359304 | tf_op jit(solution)/shard_map/ppermute | solution.py:412

commit v4 on v3

--- a/solution.py
+++ b/solution.py
@@ -45,8 +45,8 @@
     window_taper = (0.5 - 0.5 * np.cos(times * (2.0 * np.pi / NT))) * (np.arange(HALF) < NT // 2)
     freqs = F_LO + np.concatenate([2 * np.arange(PAIRS), 2 * np.arange(PAIRS) + 1])
     phase = np.mod(freqs[:, None] * times[None, :], NT) * (2.0 * np.pi / NT)
-    waves = [split_bf16(wave * window_taper, 3) for wave in (np.cos(phase), np.sin(phase))]
-    table = np.concatenate([wave.reshape(3 * NF, HALF) for wave in waves], axis=0)
+    waves = [split_bf16(wave * window_taper, 2) for wave in (np.cos(phase), np.sin(phase))]
+    table = np.concatenate([wave.reshape(2 * NF, HALF) for wave in waves], axis=0)
     angle = freqs[:, None] * (np.pi / NT)
     turn = np.concatenate([np.cos(angle), np.sin(angle)], axis=1).astype(np.float32)
     return table, turn
@@ -180,16 +180,14 @@
 
 
 def products(table, value):
-    hi, mid, lo = split3(value)
+    hi = value.astype(BF16)
+    mid = (value - hi.astype(F32)).astype(BF16)
     by_hi = dot_nt(table, hi)
-    by_mid = dot_nt(table[: 2 * NF], mid)
-    by_lo = dot_nt(table[:NF], lo)
-    small = by_hi[2 * NF:] + by_lo + by_mid[NF:]
-    return by_hi[:NF] + (by_hi[NF:2 * NF] + by_mid[:NF] + small)
+    return by_hi[:NF] + (by_hi[NF:] + dot_nt(table[:NF], mid))
 
 
 def ones_at(size, place):
-    row = lax.broadcasted_iota(jnp.int32, (size, size), 0)
+    row = lax.broadcasted_iota(jnp.int32, (size, 1), 0)
     col = lax.broadcasted_iota(jnp.int32, (size, size), 1)
     return jnp.where(col == place(row), jnp.float32(1), jnp.float32(0)).astype(BF16)
 
@@ -201,8 +199,8 @@
     lanes = traces_ref.shape[0] * CH
     traces = traces_ref[...].reshape(lanes, NT)
     front, back = traces[:, :HALF], mirrored(traces)
-    even = products(table_ref[: 3 * NF], front + back)
-    odd = products(table_ref[3 * NF:], front - back)
+    even = products(table_ref[: 2 * NF], front + back)
+    odd = products(table_ref[2 * NF:], front - back)
     cos, sin = turn_ref[:, 0:1], turn_ref[:, 1:2]
     at = pl.ds(pl.multiple_of(step * lanes, 128), lanes)
     total_ref[:NF, at] = even * cos + odd * sin
@@ -218,7 +216,7 @@
         water = jnp.sum(magnitude, axis=0, keepdims=True) * (1.0 / NF)
         weight = 1.0 / (smooth + 0.05 * water + 1e-6)
         white = jnp.concatenate([real * weight, imag * weight], axis=0).astype(BF16)
-        by_channel = dot_nn(white, ones_at(512, lambda n: (n % CH) * SEG_DEV + n // CH)).astype(BF16)
+        by_channel = dot_nn(white, ones_at(512, lambda n: ((n & 15) << 5) | (n >> 4))).astype(BF16)
         alive = [alive_ref[c].astype(F32) for c in range(CH)]
         lhs = jnp.concatenate(
             [
@@ -230,8 +228,8 @@
             ],
             axis=0,
         )
-        by_pair = ones_at(128, lambda n: (n % CH) * 8 + n // CH)
-        grouped = dot_nn(lhs, ones_at(512, lambda n: (n // 32 % 4) * 128 + (n // 128) * 32 + n % 32))
+        by_pair = ones_at(128, lambda n: ((n & 15) << 3) | (n >> 4))
+        grouped = dot_nn(lhs, ones_at(512, lambda n: (((n >> 5) & 3) << 7) | ((n >> 7) << 5) | (n & 31)))
         for half in range(PAIRS // 16):
             cols = []
             for part in range(2):

time: 91.2 us -> 89.6 us (0.982)
  Pallas kernels: 23.2 us -> 21.7 us
    pallas_call x1, Pallas kernels: 7.93 us -> 6.5 us  [whitened(): pl.pallas_call(spectra_kernel, grid=(steps,), out_shape=jax.ShapeDtypeStr...]
where the time goes in v4:
time: 89.6 us; the launch traced here: 89.4 us
  waiting for transfers between devices  43.5 us (49%)
  Pallas kernels  21.7 us (24%)
  starting transfers between devices  20.7 us (23%)
  local copies, waits for them, and re-layouts  1.95 us (2%)
  other arithmetic  1.53 us (2%)
    ppermute x12, waiting for transfers between devices, body(): send = lambda a, perm: lax.ppermute(a, AXES, perm)  43.5 us
    ppermute x12, starting transfers between devices, body(): send = lambda a, perm: lax.ppermute(a, AXES, perm)  20.7 us
    pallas_call x1, Pallas kernels, stacked(): pl.pallas_call(stack_kernel, grid_spec=pltpu.PrefetchScalarGridSpec(num_s...  15.2 us
    pallas_call x1, Pallas kernels, whitened(): pl.pallas_call(spectra_kernel, grid=(steps,), out_shape=jax.ShapeDtypeStr...  6.5 us
  transfers between devices with their start and end apart: 12, of which 9 were waited for; matrix products, arithmetic and copies ran while one was open for 2% of the time, Pallas kernels for 0%

profile of v4, /device:TPU:4, one launch (start us, length us, event | category | flops | bytes accessed | tf_op | source)
XLA Modules:
  0.0 89.4 jit_solution(2524320378811433877)
XLA Ops:
  0.0 6.5 %whitened_spectra.1.refs_0_ = bf16[96,16,128]{2,1,0:T(8,128)(2,1)} custom-call(s32[16]{0:T(128)} %alive_ref.1, f32[32,16,2000]{2,1,0:T(8,128)} %traces_ref.1, bf16[768,1024]{1,0:T(8,128)(2,1)} %constant.34.clone.table_ref, f32[192,2]{1,0:T(8,128)} %constant.35.clone.turn_ref, bf16[192,192]{1,0:T(8,128)(2,1)} %constant.36.clone.near_ref, ...), custom_call_target="tpu_custom_call" | custom-call | tf_op jit(solution)/shard_map/whitened_spectra/pallas_call | solution.py:262
  6.5 4.5 %collective-permute-start.3 = (bf16[96,16,128]{2,1,0:T(8,128)(2,1)}, bf16[96,16,128]{2,1,0:T(8,128)(2,1)S(1)}, u32[]{:S(2)}, u32[]{:S(2)}) collective-permute-start(bf16[96,16,128]{2,1,0:T(8,128)(2,1)} %whitened_spectra.1.refs_0_), channel_id=1, source_target_pairs={{0,32},{16,18},{2,96},{18,50},{1,48},{17,114},{3,64},{19,2},{4,80}... | collective-permute-start | bytes 1179656 | tf_op jit(solution)/shard_map/ppermute | solution.py:410
  11.0 4.5 %collective-permute-start.2 = (bf16[96,16,128]{2,1,0:T(8,128)(2,1)}, bf16[96,16,128]{2,1,0:T(8,128)(2,1)S(1)}, u32[]{:S(2)}, u32[]{:S(2)}) collective-permute-start(bf16[96,16,128]{2,1,0:T(8,128)(2,1)} %whitened_spectra.1.refs_0_), channel_id=1, source_target_pairs={{0,8},{16,17},{2,10},{18,19},{1,9},{17,16},{3,11},{19,18},{4,12},{... | collective-permute-start | bytes 1179656 | tf_op jit(solution)/shard_map/ppermute | solution.py:410
  15.5 2.0 %collective-permute-start = (bf16[96,16,128]{2,1,0:T(8,128)(2,1)}, bf16[96,16,128]{2,1,0:T(8,128)(2,1)S(1)}, u32[]{:S(2)}, u32[]{:S(2)}) collective-permute-start(bf16[96,16,128]{2,1,0:T(8,128)(2,1)} %whitened_spectra.1.refs_0_), channel_id=1, source_target_pairs={{0,4},{16,18},{2,6},{18,17},{1,5},{17,19},{3,7},{19,16},{4,8},{20,... | collective-permute-start | bytes 1179656 | tf_op jit(solution)/shard_map/ppermute | solution.py:410
  17.5 4.8 %collective-permute-done.3 = bf16[96,16,128]{2,1,0:T(8,128)(2,1)S(1)} collective-permute-done((bf16[96,16,128]{2,1,0:T(8,128)(2,1)}, bf16[96,16,128]{2,1,0:T(8,128)(2,1)S(1)}, u32[]{:S(2)}, u32[]{:S(2)}) %collective-permute-start.3) | collective-permute-done | bytes 393248 | tf_op jit(solution)/shard_map/ppermute | solution.py:410
  22.3 4.1 %collective-permute-done.2.refs_3_ = bf16[96,16,128]{2,1,0:T(8,128)(2,1)S(1)} collective-permute-done((bf16[96,16,128]{2,1,0:T(8,128)(2,1)}, bf16[96,16,128]{2,1,0:T(8,128)(2,1)S(1)}, u32[]{:S(2)}, u32[]{:S(2)}) %collective-permute-start.2) | collective-permute-done | bytes 393248 | tf_op jit(solution)/shard_map/ppermute | solution.py:410
  26.4 1.7 %collective-permute-done.1.refs_2_ = bf16[96,16,128]{2,1,0:T(8,128)(2,1)S(1)} collective-permute-done((bf16[96,16,128]{2,1,0:T(8,128)(2,1)}, bf16[96,16,128]{2,1,0:T(8,128)(2,1)S(1)}, u32[]{:S(2)}, u32[]{:S(2)}) %collective-permute-start.1) | collective-permute-done | bytes 393248 | tf_op jit(solution)/shard_map/ppermute | solution.py:410
  28.1 2.4 %collective-permute-done.refs_1_ = bf16[96,16,128]{2,1,0:T(8,128)(2,1)S(1)} collective-permute-done((bf16[96,16,128]{2,1,0:T(8,128)(2,1)}, bf16[96,16,128]{2,1,0:T(8,128)(2,1)S(1)}, u32[]{:S(2)}, u32[]{:S(2)}) %collective-permute-start) | collective-permute-done | bytes 393248 | tf_op jit(solution)/shard_map/ppermute | solution.py:410
  30.5 1.3 %pad_maximum_fusion = bf16[4,96,16,128]{3,2,1,0:T(8,128)(2,1)S(1)} fusion(bf16[1,96,16,128]{3,2,1,0:T(8,128)(2,1)S(1)} %bitcast.12, bf16[1,96,16,128]{3,2,1,0:T(8,128)(2,1)S(1)} %bitcast.13, bf16[1,96,16,128]{3,2,1,0:T(8,128)(2,1)S(1)} %bitcast.14, bf16[1,96,16,128]{3,2,1,0:T(8,128)(2,1)} %bitcast.11), kind=kLoop, calls=%fused_computation | loop fusion | flops 2359296 | bytes 3145728 | tf_op jit(solution)/shard_map/stack | solution.py:414
  31.8 1.8 %collective-permute-start.5 = (bf16[4,96,16,128]{3,2,1,0:T(8,128)(2,1)S(1)}, bf16[4,96,16,128]{3,2,1,0:T(8,128)(2,1)S(1)}, u32[]{:S(2)}, u32[]{:S(2)}) collective-permute-start(bf16[4,96,16,128]{3,2,1,0:T(8,128)(2,1)S(1)} %pad_maximum_fusion), channel_id=1, source_target_pairs={{0,3},{16,28},{2,0},{18,30},{1,2},{17,29},{3,1},{19,31},{4,7},{20,... | collective-permute-start | bytes 4718600 | tf_op jit(solution)/shard_map/ppermute | solution.py:410
  33.6 0.3 collective-permute-start.4
  33.9 3.5 %collective-permute-start.7 = (bf16[96,16,128]{2,1,0:T(8,128)(2,1)S(1)}, bf16[96,16,128]{2,1,0:T(8,128)(2,1)S(1)}, u32[]{:S(2)}, u32[]{:S(2)}) collective-permute-start(bf16[96,16,128]{2,1,0:T(8,128)(2,1)S(1)} %collective-permute-done.3), channel_id=1, source_target_pairs={{0,96},{16,112},{2,98},{18,114},{1,97},{17,113},{3,99},{19,115},{4... | collective-permute-start | bytes 1179656 | tf_op jit(solution)/shard_map/ppermute | solution.py:410
  37.5 8.4 %collective-permute-done.8 = bf16[96,16,128]{2,1,0:T(8,128)(2,1)S(1)} collective-permute-done((bf16[96,16,128]{2,1,0:T(8,128)(2,1)S(1)}, bf16[96,16,128]{2,1,0:T(8,128)(2,1)S(1)}, u32[]{:S(2)}, u32[]{:S(2)}) %collective-permute-start.8) | collective-permute-done | bytes 393248 | tf_op jit(solution)/shard_map/ppermute | solution.py:410
  45.9 7.9 %collective-permute-done.7 = bf16[96,16,128]{2,1,0:T(8,128)(2,1)S(1)} collective-permute-done((bf16[96,16,128]{2,1,0:T(8,128)(2,1)S(1)}, bf16[96,16,128]{2,1,0:T(8,128)(2,1)S(1)}, u32[]{:S(2)}, u32[]{:S(2)}) %collective-permute-start.7) | collective-permute-done | bytes 393248 | tf_op jit(solution)/shard_map/ppermute | solution.py:410
  53.8 2.0 %collective-permute-done.6 = bf16[96,16,128]{2,1,0:T(8,128)(2,1)S(1)} collective-permute-done((bf16[96,16,128]{2,1,0:T(8,128)(2,1)S(1)}, bf16[96,16,128]{2,1,0:T(8,128)(2,1)S(1)}, u32[]{:S(2)}, u32[]{:S(2)}) %collective-permute-start.6) | collective-permute-done | bytes 393248 | tf_op jit(solution)/shard_map/ppermute | solution.py:410
  55.9 0.2 pad_maximum_fusion.1.refs_8_
  56.1 1.1 %collective-permute-start.11 = (bf16[4,96,16,128]{3,2,1,0:T(8,128)(2,1)S(1)}, bf16[4,96,16,128]{3,2,1,0:T(8,128)(2,1)}, u32[]{:S(2)}, u32[]{:S(2)}) collective-permute-start(bf16[4,96,16,128]{3,2,1,0:T(8,128)(2,1)S(1)} %pad_maximum_fusion.1.refs_8_), channel_id=1, source_target_pairs={{0,16},{16,0},{2,18},{18,2},{1,17},{17,1},{3,19},{19,3},{4,20},{20... | collective-permute-start | bytes 4718600 | tf_op jit(solution)/shard_map/ppermute | solution.py:410
  57.2 0.1 slice.6
  57.6 0.4 copy-done
  58.0 2.9 %collective-permute-start.10 = (bf16[2,96,16,128]{3,2,1,0:T(8,128)(2,1)S(1)}, bf16[2,96,16,128]{3,2,1,0:T(8,128)(2,1)}, u32[]{:S(2)}, u32[]{:S(2)}) collective-permute-start(bf16[2,96,16,128]{3,2,1,0:T(8,128)(2,1)S(1)} %slice.7), channel_id=1, source_target_pairs={{0,3},{16,28},{2,0},{18,30},{1,2},{17,29},{3,1},{19,31},{4,7},{20,... | collective-permute-start | bytes 2359304 | tf_op jit(solution)/shard_map/ppermute | solution.py:410
  60.9 1.2 %dynamic-slice_bitcast_fusion.slots_ref = s32[24]{0:T(128)} fusion(s32[128,24]{1,0:T(8,128)} %constant.38.clone, s32[]{:T(128)S(6)} %select_n.4), kind=kLoop, calls=%fused_computation.2 | loop fusion | bytes 196 | tf_op jit(solution)/shard_map/jit(dynamic_index_in_dim)/squeeze | solution.py:409
  62.1 8.3 %collective-permute-done.10.refs_7_ = bf16[2,96,16,128]{3,2,1,0:T(8,128)(2,1)} collective-permute-done((bf16[2,96,16,128]{3,2,1,0:T(8,128)(2,1)S(1)}, bf16[2,96,16,128]{3,2,1,0:T(8,128)(2,1)}, u32[]{:S(2)}, u32[]{:S(2)}) %collective-permute-start.10) | collective-permute-done | bytes 786464 | tf_op jit(solution)/shard_map/ppermute | solution.py:410
  70.4 3.8 %collective-permute-done.9.refs_6_ = bf16[2,96,16,128]{3,2,1,0:T(8,128)(2,1)} collective-permute-done((bf16[2,96,16,128]{3,2,1,0:T(8,128)(2,1)S(1)}, bf16[2,96,16,128]{3,2,1,0:T(8,128)(2,1)}, u32[]{:S(2)}, u32[]{:S(2)}) %collective-permute-start.9) | collective-permute-done | bytes 786464 | tf_op jit(solution)/shard_map/ppermute | solution.py:410
  74.2 15.2 %stacks.1 = f32[401,64,128]{2,1,0:T(8,128)} custom-call(s32[24]{0:T(128)} %dynamic-slice_bitcast_fusion.slots_ref, bf16[96,16,128]{2,1,0:T(8,128)(2,1)} %whitened_spectra.1.refs_0_, bf16[96,16,128]{2,1,0:T(8,128)(2,1)} %copy-done.3, bf16[96,16,128]{2,1,0:T(8,128)(2,1)} %copy-done.2, bf16[96,16,128]{2,1,0:T(8,128)(2,1)} %copy-done.1, ...), custom_call_target="tpu_custom_call" | custom-call | flops 20000000000 | bytes 25165824 | tf_op jit(solution)/shard_map/stacks/pallas_call | solution.py:382
  (19 shorter events, 0.3 us)
Async XLA Ops:
  6.5 15.8 %collective-permute-start.3 = (bf16[96,16,128]{2,1,0:T(8,128)(2,1)}, bf16[96,16,128]{2,1,0:T(8,128)(2,1)S(1)}, u32[]{:S(2)}, u32[]{:S(2)}) collective-permute-start(bf16[96,16,128]{2,1,0:T(8,128)(2,1)} %whitened_spectra.1.refs_0_), channel_id=1, source_target_pairs={{0,32},{16,18},{2,96},{18,50},{1,48},{17,114},{3,64},{19,2},{4,80}... | collective-permute-start | bytes 1179656 | tf_op jit(solution)/shard_map/ppermute | solution.py:410
  11.0 15.4 %collective-permute-start.2 = (bf16[96,16,128]{2,1,0:T(8,128)(2,1)}, bf16[96,16,128]{2,1,0:T(8,128)(2,1)S(1)}, u32[]{:S(2)}, u32[]{:S(2)}) collective-permute-start(bf16[96,16,128]{2,1,0:T(8,128)(2,1)} %whitened_spectra.1.refs_0_), channel_id=1, source_target_pairs={{0,8},{16,17},{2,10},{18,19},{1,9},{17,16},{3,11},{19,18},{4,12},{... | collective-permute-start | bytes 1179656 | tf_op jit(solution)/shard_map/ppermute | solution.py:410
  15.5 12.6 %collective-permute-start.1 = (bf16[96,16,128]{2,1,0:T(8,128)(2,1)}, bf16[96,16,128]{2,1,0:T(8,128)(2,1)S(1)}, u32[]{:S(2)}, u32[]{:S(2)}) collective-permute-start(bf16[96,16,128]{2,1,0:T(8,128)(2,1)} %whitened_spectra.1.refs_0_), channel_id=1, source_target_pairs={{0,12},{16,19},{2,14},{18,16},{1,13},{17,18},{3,15},{19,17},{4,0},... | collective-permute-start | bytes 1179656 | tf_op jit(solution)/shard_map/ppermute | solution.py:410
  15.5 15.0 %collective-permute-start = (bf16[96,16,128]{2,1,0:T(8,128)(2,1)}, bf16[96,16,128]{2,1,0:T(8,128)(2,1)S(1)}, u32[]{:S(2)}, u32[]{:S(2)}) collective-permute-start(bf16[96,16,128]{2,1,0:T(8,128)(2,1)} %whitened_spectra.1.refs_0_), channel_id=1, source_target_pairs={{0,4},{16,18},{2,6},{18,17},{1,5},{17,19},{3,7},{19,16},{4,8},{20,... | collective-permute-start | bytes 1179656 | tf_op jit(solution)/shard_map/ppermute | solution.py:410
  26.4 5.4 %copy-start.1 = (bf16[96,16,128]{2,1,0:T(8,128)(2,1)}, bf16[96,16,128]{2,1,0:T(8,128)(2,1)S(1)}, u32[]{:S(2)}) copy-start(bf16[96,16,128]{2,1,0:T(8,128)(2,1)S(1)} %collective-permute-done.2.refs_3_) | copy-start | bytes 1179652
  28.1 3.8 %copy-start.2 = (bf16[96,16,128]{2,1,0:T(8,128)(2,1)}, bf16[96,16,128]{2,1,0:T(8,128)(2,1)S(1)}, u32[]{:S(2)}) copy-start(bf16[96,16,128]{2,1,0:T(8,128)(2,1)S(1)} %collective-permute-done.1.refs_2_) | copy-start | bytes 1179652
  30.5 1.4 %copy-start.3 = (bf16[96,16,128]{2,1,0:T(8,128)(2,1)}, bf16[96,16,128]{2,1,0:T(8,128)(2,1)S(1)}, u32[]{:S(2)}) copy-start(bf16[96,16,128]{2,1,0:T(8,128)(2,1)S(1)} %collective-permute-done.refs_1_) | copy-start | bytes 1179652
  31.8 24.0 %collective-permute-start.5 = (bf16[4,96,16,128]{3,2,1,0:T(8,128)(2,1)S(1)}, bf16[4,96,16,128]{3,2,1,0:T(8,128)(2,1)S(1)}, u32[]{:S(2)}, u32[]{:S(2)}) collective-permute-start(bf16[4,96,16,128]{3,2,1,0:T(8,128)(2,1)S(1)} %pad_maximum_fusion), channel_id=1, source_target_pairs={{0,3},{16,28},{2,0},{18,30},{1,2},{17,29},{3,1},{19,31},{4,7},{20,... | collective-permute-start | bytes 4718600 | tf_op jit(solution)/shard_map/ppermute | solution.py:410
  33.6 22.3 %collective-permute-start.4 = (bf16[4,96,16,128]{3,2,1,0:T(8,128)(2,1)S(1)}, bf16[4,96,16,128]{3,2,1,0:T(8,128)(2,1)S(1)}, u32[]{:S(2)}, u32[]{:S(2)}) collective-permute-start(bf16[4,96,16,128]{3,2,1,0:T(8,128)(2,1)S(1)} %pad_maximum_fusion), channel_id=1, source_target_pairs={{0,2},{16,20},{2,1},{18,22},{1,3},{17,21},{3,0},{19,23},{4,6},{20,... | collective-permute-start | bytes 4718600 | tf_op jit(solution)/shard_map/ppermute | solution.py:410
  33.9 12.0 %collective-permute-start.8 = (bf16[96,16,128]{2,1,0:T(8,128)(2,1)S(1)}, bf16[96,16,128]{2,1,0:T(8,128)(2,1)S(1)}, u32[]{:S(2)}, u32[]{:S(2)}) collective-permute-start(bf16[96,16,128]{2,1,0:T(8,128)(2,1)S(1)} %collective-permute-done.3), channel_id=1, source_target_pairs={{0,64},{16,80},{2,66},{18,82},{1,65},{17,81},{3,67},{19,83},{4,68}... | collective-permute-start | bytes 1179656 | tf_op jit(solution)/shard_map/ppermute | solution.py:410
  33.9 19.9 %collective-permute-start.7 = (bf16[96,16,128]{2,1,0:T(8,128)(2,1)S(1)}, bf16[96,16,128]{2,1,0:T(8,128)(2,1)S(1)}, u32[]{:S(2)}, u32[]{:S(2)}) collective-permute-start(bf16[96,16,128]{2,1,0:T(8,128)(2,1)S(1)} %collective-permute-done.3), channel_id=1, source_target_pairs={{0,96},{16,112},{2,98},{18,114},{1,97},{17,113},{3,99},{19,115},{4... | collective-permute-start | bytes 1179656 | tf_op jit(solution)/shard_map/ppermute | solution.py:410
  37.5 18.4 %collective-permute-start.6 = (bf16[96,16,128]{2,1,0:T(8,128)(2,1)S(1)}, bf16[96,16,128]{2,1,0:T(8,128)(2,1)S(1)}, u32[]{:S(2)}, u32[]{:S(2)}) collective-permute-start(bf16[96,16,128]{2,1,0:T(8,128)(2,1)S(1)} %collective-permute-done.3), channel_id=1, source_target_pairs={{0,32},{16,48},{2,34},{18,50},{1,33},{17,49},{3,35},{19,51},{4,36}... | collective-permute-start | bytes 1179656 | tf_op jit(solution)/shard_map/ppermute | solution.py:410
  55.9 1.6 %copy-start.4 = (bf16[4,96,16,128]{3,2,1,0:T(8,128)(2,1)}, bf16[4,96,16,128]{3,2,1,0:T(8,128)(2,1)S(1)}, u32[]{:S(2)}) copy-start(bf16[4,96,16,128]{3,2,1,0:T(8,128)(2,1)S(1)} %collective-permute-done.5.refs_5_) | copy-start | bytes 4718596
  55.9 1.4 %copy-start.5 = (bf16[4,96,16,128]{3,2,1,0:T(8,128)(2,1)}, bf16[4,96,16,128]{3,2,1,0:T(8,128)(2,1)S(1)}, u32[]{:S(2)}) copy-start(bf16[4,96,16,128]{3,2,1,0:T(8,128)(2,1)S(1)} %collective-permute-done.4.refs_4_) | copy-start | bytes 4718596
  56.1 1.9 %copy-start = (bf16[4,96,16,128]{3,2,1,0:T(8,128)(2,1)}, bf16[4,96,16,128]{3,2,1,0:T(8,128)(2,1)S(1)}, u32[]{:S(2)}) copy-start(bf16[4,96,16,128]{3,2,1,0:T(8,128)(2,1)S(1)} %pad_maximum_fusion.1.refs_8_) | copy-start | bytes 4718596
  56.1 18.1 %collective-permute-start.11 = (bf16[4,96,16,128]{3,2,1,0:T(8,128)(2,1)S(1)}, bf16[4,96,16,128]{3,2,1,0:T(8,128)(2,1)}, u32[]{:S(2)}, u32[]{:S(2)}) collective-permute-start(bf16[4,96,16,128]{3,2,1,0:T(8,128)(2,1)S(1)} %pad_maximum_fusion.1.refs_8_), channel_id=1, source_target_pairs={{0,16},{16,0},{2,18},{18,2},{1,17},{17,1},{3,19},{19,3},{4,20},{20... | collective-permute-start | bytes 4718600 | tf_op jit(solution)/shard_map/ppermute | solution.py:410
  58.0 12.4 %collective-permute-start.10 = (bf16[2,96,16,128]{3,2,1,0:T(8,128)(2,1)S(1)}, bf16[2,96,16,128]{3,2,1,0:T(8,128)(2,1)}, u32[]{:S(2)}, u32[]{:S(2)}) collective-permute-start(bf16[2,96,16,128]{3,2,1,0:T(8,128)(2,1)S(1)} %slice.7), channel_id=1, source_target_pairs={{0,3},{16,28},{2,0},{18,30},{1,2},{17,29},{3,1},{19,31},{4,7},{20,... | collective-permute-start | bytes 2359304 | tf_op jit(solution)/shard_map/ppermute | solution.py:410
  60.9 13.3 %collective-permute-start.9 = (bf16[2,96,16,128]{3,2,1,0:T(8,128)(2,1)S(1)}, bf16[2,96,16,128]{3,2,1,0:T(8,128)(2,1)}, u32[]{:S(2)}, u32[]{:S(2)}) collective-permute-start(bf16[2,96,16,128]{3,2,1,0:T(8,128)(2,1)S(1)} %slice.6), channel_id=1, source_target_pairs={{0,2},{16,20},{2,1},{18,22},{1,3},{17,21},{3,0},{19,23},{4,6},{20,... | collective-permute-start | bytes 2359304 | tf_op jit(solution)/shard_map/ppermute | solution.py:410

commit v5 on v4

--- a/solution.py
+++ b/solution.py
@@ -193,7 +193,7 @@
 
 
 def spectra_kernel(
-    alive_ref, traces_ref, table_ref, turn_ref, near_ref, counts_ref, out_ref, total_ref,
+    alive_ref, traces_ref, table_ref, turn_ref, near_ref, counts_ref, out_ref, four_ref, total_ref,
 ):
     step = pl.program_id(0)
     lanes = traces_ref.shape[0] * CH
@@ -251,7 +251,9 @@
             block = dot_nn(by_pair, block).astype(BF16)
             for part in range(2):
                 at = 16 * half + 8 * part
-                out_ref[at:at + 8] = block[:, 128 * part:128 * part + 128].reshape(8, CH, 128)
+                shard = block[:, 128 * part:128 * part + 128].reshape(8, CH, 128)
+                out_ref[at:at + 8] = shard
+                four_ref[0, at:at + 8] = shard
 
 
 def whitened(traces, alive):
@@ -262,13 +264,19 @@
     return pl.pallas_call(
         spectra_kernel,
         grid=(steps,),
-        out_shape=jax.ShapeDtypeStruct((PAIRS, CH, 128), BF16),
+        out_shape=[
+            jax.ShapeDtypeStruct((PAIRS, CH, 128), BF16),
+            jax.ShapeDtypeStruct((4, PAIRS, CH, 128), BF16),
+        ],
         in_specs=[
             pl.BlockSpec(memory_space=pltpu.SMEM),
             pl.BlockSpec((SEG_DEV // steps, CH, NT), lambda i: (i, 0, 0)),
         ]
         + [whole(a) for a in consts],
-        out_specs=pl.BlockSpec((PAIRS, CH, 128), lambda i: (0, 0, 0)),
+        out_specs=[
+            pl.BlockSpec((PAIRS, CH, 128), lambda i: (0, 0, 0)),
+            pl.BlockSpec((1, PAIRS, CH, 128), lambda i: (0, 0, 0, 0)),
+        ],
         scratch_shapes=[pltpu.VMEM((2 * NF, SEG_DEV * CH), F32)],
         compiler_params=pltpu.CompilerParams(vmem_limit_bytes=VMEM),
         name="whitened_spectra",
@@ -282,19 +290,18 @@
 
 
 def stack_kernel(slots_ref, *refs):
-    sources, table_ref, out_ref = refs[:10], refs[10], refs[11]
-    left, right, waves = refs[12:15]
-    cross_refs, sems, wave_sem = refs[15:19], refs[19], refs[20]
+    sources, table_ref, out_ref = refs[:-11], refs[-11], refs[-10]
+    left, right, waves = refs[-9:-6]
+    cross_refs, sems, wave_sem = refs[-6:-2], refs[-2], refs[-1]
     step = pl.program_id(0)
 
     def copies(chunk):
         at = pl.ds(chunk * PER, PER)
         found = []
         for ref in sources:
-            for k in range(ref.shape[0] if len(ref.shape) == 4 else 1):
+            for k in range(ref.shape[0]):
                 to = left if len(found) < 16 else right
-                part = ref.at[k, at] if len(ref.shape) == 4 else ref.at[at]
-                found.append((part, to.at[slots_ref[len(found)], at]))
+                found.append((ref.at[k, at], to.at[slots_ref[len(found)], at]))
         return [
             pltpu.make_async_copy(src, dst, sems.at[chunk, n])
             for n, (src, dst) in enumerate(found)
@@ -404,21 +411,21 @@
 
 
 def body(traces, channel_alive):
-    own = whitened(traces, channel_alive)
+    own, mine = whitened(traces, channel_alive)
     device = (lax.axis_index("row") * 8 + lax.axis_index("col")) * 2 + lax.axis_index("seg")
     slots = lax.dynamic_index_in_dim(jnp.asarray(slot_table()), device, 0, keepdims=False)
     send = lambda a, perm: lax.ppermute(a, AXES, perm)
-    first = [own] + [send(own, along_first(n)) for n in (1, -1, 2)]
     second = send(own, to_readers())
-    *first, second = lax.optimization_barrier((*first, second))
-    mine = jnp.stack(first)
+    for k, n in enumerate((1, -1, 2)):
+        mine = lax.dynamic_update_slice(mine, send(own, along_first(n))[None], (k + 1, 0, 0, 0))
+    mine, second = lax.optimization_barrier((mine, second))
     up, down = send(mine, along_second(1)), send(mine, along_second(-1))
     seconds = [second] + [send(second, along_x(n)) for n in (1, -1, 2)]
     up, down, *seconds = lax.optimization_barrier((up, down, *seconds))
     seconds = jnp.stack(seconds)
     far_up, far_down = send(up[:2], along_second(1)), send(down[2:], along_second(-1))
     others = send(seconds, other_core())
-    sources = (*first, up, down, far_up, far_down, seconds, others)
+    sources = (mine, up, down, far_up, far_down, seconds, others)
     out = stacked(slots, sources, jnp.asarray(inverse_table()))
     return jnp.transpose(out, (2, 1, 0))
 

time: 89.6 us -> 87.6 us (0.978)
  waiting for transfers between devices: 43.5 us -> 39.3 us
  local copies, waits for them, and re-layouts: 1.95 us -> 5.37 us
  other arithmetic: 1.53 us -> 0.2 us
    ppermute x12, waiting for transfers between devices: 43.5 us -> 39.3 us  [body(): send = lambda a, perm: lax.ppermute(a, AXES, perm)]
    dynamic_update_slice x0 -> x3, local copies, waits for them, and re-layouts: none -> 2.31 us  [body(): lax.dynamic_update_slice(mine, send(own, along_first(n))[None], (k + 1, 0...]
    another operation x1 -> x0, other arithmetic: 1.33 us -> none  [body(): mine = jnp.stack(first)]
    unnamed x12 -> x6, local copies, waits for them, and re-layouts: 0.51 us -> 1.5 us
  transfers between devices with their start and end apart: 12 -> 12, of which waited for: 9 -> 6; matrix products, arithmetic and copies ran while one was open for 2% -> 4% of each run, Pallas kernels for 0% -> 0%
where the time goes in v5:
time: 87.6 us; the launch traced here: 87.4 us
  waiting for transfers between devices  39.3 us (45%)
  Pallas kernels  21.8 us (25%)
  starting transfers between devices  20.6 us (24%)
  local copies, waits for them, and re-layouts  5.37 us (6%)
    ppermute x12, waiting for transfers between devices, body(): send = lambda a, perm: lax.ppermute(a, AXES, perm)  39.3 us
    ppermute x12, starting transfers between devices, body(): send = lambda a, perm: lax.ppermute(a, AXES, perm)  20.6 us
    pallas_call x1, Pallas kernels, stacked(): pl.pallas_call(stack_kernel, grid_spec=pltpu.PrefetchScalarGridSpec(num_s...  15.2 us
    pallas_call x1, Pallas kernels, whitened(): pl.pallas_call(spectra_kernel, grid=(steps,), out_shape=[jax.ShapeDtypeSt...  6.6 us
    dynamic_update_slice x3, local copies, waits for them, and re-layouts, body(): lax.dynamic_update_slice(mine, send(own, along_first(n))[None], (k + 1, 0...  2.31 us
  transfers between devices with their start and end apart: 12, of which 6 were waited for; matrix products, arithmetic and copies ran while one was open for 4% of the time, Pallas kernels for 0%

profile of v5, /device:TPU:4, one launch (start us, length us, event | category | flops | bytes accessed | tf_op | source)
XLA Modules:
  0.0 87.4 jit_solution(12256776318964493039)
XLA Ops:
  0.0 6.6 %whitened_spectra.1 = (bf16[96,16,128]{2,1,0:T(8,128)(2,1)}, bf16[4,96,16,128]{3,2,1,0:T(8,128)(2,1)}) custom-call(s32[16]{0:T(128)} %alive_ref.1, f32[32,16,2000]{2,1,0:T(8,128)} %traces_ref.1, bf16[768,1024]{1,0:T(8,128)(2,1)} %constant.39.clone.table_ref, f32[192,2]{1,0:T(8,128)} %constant.40.clone.turn_ref, bf16[192,192]{1,0:T(8,128)(2,1)} %constant.41.clone.near_ref, ...), custom_call_target="tpu_custom_call" | custom-call | tf_op jit(solution)/shard_map/whitened_spectra/pallas_call | solution.py:264
  6.6 1.6 %collective-permute-start = (bf16[96,16,128]{2,1,0:T(8,128)(2,1)}, bf16[96,16,128]{2,1,0:T(8,128)(2,1)S(1)}, u32[]{:S(2)}, u32[]{:S(2)}) collective-permute-start(bf16[96,16,128]{2,1,0:T(8,128)(2,1)} %get-tuple-element.16), channel_id=1, source_target_pairs={{0,4},{16,18},{2,6},{18,17},{1,5},{17,19},{3,7},{19,16},{4,8},{20,... | collective-permute-start | bytes 1179656 | tf_op jit(solution)/shard_map/ppermute | solution.py:417
  8.2 1.7 %collective-permute-start.1 = (bf16[96,16,128]{2,1,0:T(8,128)(2,1)}, bf16[96,16,128]{2,1,0:T(8,128)(2,1)S(1)}, u32[]{:S(2)}, u32[]{:S(2)}) collective-permute-start(bf16[96,16,128]{2,1,0:T(8,128)(2,1)} %get-tuple-element.16), channel_id=1, source_target_pairs={{0,12},{16,19},{2,14},{18,16},{1,13},{17,18},{3,15},{19,17},{4,0},... | collective-permute-start | bytes 1179656 | tf_op jit(solution)/shard_map/ppermute | solution.py:417
  9.8 5.0 %collective-permute-start.3 = (bf16[96,16,128]{2,1,0:T(8,128)(2,1)}, bf16[96,16,128]{2,1,0:T(8,128)(2,1)S(1)}, u32[]{:S(2)}, u32[]{:S(2)}) collective-permute-start(bf16[96,16,128]{2,1,0:T(8,128)(2,1)} %get-tuple-element.16), channel_id=1, source_target_pairs={{0,32},{16,18},{2,96},{18,50},{1,48},{17,114},{3,64},{19,2},{4,80}... | collective-permute-start | bytes 1179656 | tf_op jit(solution)/shard_map/ppermute | solution.py:417
  14.8 2.8 %collective-permute-start.2 = (bf16[96,16,128]{2,1,0:T(8,128)(2,1)}, bf16[96,16,128]{2,1,0:T(8,128)(2,1)S(1)}, u32[]{:S(2)}, u32[]{:S(2)}) collective-permute-start(bf16[96,16,128]{2,1,0:T(8,128)(2,1)} %get-tuple-element.16), channel_id=1, source_target_pairs={{0,8},{16,17},{2,10},{18,19},{1,9},{17,16},{3,11},{19,18},{4,12},{... | collective-permute-start | bytes 1179656 | tf_op jit(solution)/shard_map/ppermute | solution.py:417
  17.6 0.8 bitcast_dynamic-update-slice_fusion.2
  18.4 0.8 bitcast_dynamic-update-slice_fusion.1
  19.2 9.3 %collective-permute-done.2 = bf16[96,16,128]{2,1,0:T(8,128)(2,1)S(1)} collective-permute-done((bf16[96,16,128]{2,1,0:T(8,128)(2,1)}, bf16[96,16,128]{2,1,0:T(8,128)(2,1)S(1)}, u32[]{:S(2)}, u32[]{:S(2)}) %collective-permute-start.2) | collective-permute-done | bytes 393248 | tf_op jit(solution)/shard_map/ppermute | solution.py:417
  28.5 0.8 bitcast_dynamic-update-slice_fusion.refs_0_
  29.3 2.8 %collective-permute-start.5 = (bf16[4,96,16,128]{3,2,1,0:T(8,128)(2,1)}, bf16[4,96,16,128]{3,2,1,0:T(8,128)(2,1)S(1)}, u32[]{:S(2)}, u32[]{:S(2)}) collective-permute-start(bf16[4,96,16,128]{3,2,1,0:T(8,128)(2,1)} %bitcast_dynamic-update-slice_fusion.refs_0_), channel_id=1, source_target_pairs={{0,3},{16,28},{2,0},{18,30},{1,2},{17,29},{3,1},{19,31},{4,7},{20,... | collective-permute-start | bytes 4718600 | tf_op jit(solution)/shard_map/ppermute | solution.py:417
  32.1 4.0 %collective-permute-start.7 = (bf16[96,16,128]{2,1,0:T(8,128)(2,1)S(1)}, bf16[96,16,128]{2,1,0:T(8,128)(2,1)S(1)}, u32[]{:S(2)}, u32[]{:S(2)}) collective-permute-start(bf16[96,16,128]{2,1,0:T(8,128)(2,1)S(1)} %collective-permute-done.3), channel_id=1, source_target_pairs={{0,96},{16,112},{2,98},{18,114},{1,97},{17,113},{3,99},{19,115},{4... | collective-permute-start | bytes 1179656 | tf_op jit(solution)/shard_map/ppermute | solution.py:417
  36.1 9.4 %collective-permute-done.8 = bf16[96,16,128]{2,1,0:T(8,128)(2,1)S(1)} collective-permute-done((bf16[96,16,128]{2,1,0:T(8,128)(2,1)S(1)}, bf16[96,16,128]{2,1,0:T(8,128)(2,1)S(1)}, u32[]{:S(2)}, u32[]{:S(2)}) %collective-permute-start.8) | collective-permute-done | bytes 393248 | tf_op jit(solution)/shard_map/ppermute | solution.py:417
  45.5 6.7 %collective-permute-done.7 = bf16[96,16,128]{2,1,0:T(8,128)(2,1)S(1)} collective-permute-done((bf16[96,16,128]{2,1,0:T(8,128)(2,1)S(1)}, bf16[96,16,128]{2,1,0:T(8,128)(2,1)S(1)}, u32[]{:S(2)}, u32[]{:S(2)}) %collective-permute-start.7) | collective-permute-done | bytes 393248 | tf_op jit(solution)/shard_map/ppermute | solution.py:417
  52.1 1.9 %collective-permute-done.6 = bf16[96,16,128]{2,1,0:T(8,128)(2,1)S(1)} collective-permute-done((bf16[96,16,128]{2,1,0:T(8,128)(2,1)S(1)}, bf16[96,16,128]{2,1,0:T(8,128)(2,1)S(1)}, u32[]{:S(2)}, u32[]{:S(2)}) %collective-permute-start.6) | collective-permute-done | bytes 393248 | tf_op jit(solution)/shard_map/ppermute | solution.py:417
  54.0 0.2 pad_maximum_fusion.refs_5_
  54.3 0.8 copy-done.2
  55.2 0.1 slice.6
  55.3 0.3 copy-done.1
  55.8 0.3 copy-done
  56.1 2.7 %collective-permute-start.10 = (bf16[2,96,16,128]{3,2,1,0:T(8,128)(2,1)S(1)}, bf16[2,96,16,128]{3,2,1,0:T(8,128)(2,1)}, u32[]{:S(2)}, u32[]{:S(2)}) collective-permute-start(bf16[2,96,16,128]{3,2,1,0:T(8,128)(2,1)S(1)} %slice.7), channel_id=1, source_target_pairs={{0,3},{16,28},{2,0},{18,30},{1,2},{17,29},{3,1},{19,31},{4,7},{20,... | collective-permute-start | bytes 2359304 | tf_op jit(solution)/shard_map/ppermute | solution.py:417
  58.8 1.3 %fusion.slots_ref = s32[24]{0:T(128)} fusion(s32[128,24]{1,0:T(8,128)} %constant.43.clone, s32[]{:T(128)S(6)} %select_n.4), kind=kLoop, calls=%fused_computation.5 | loop fusion | bytes 196 | tf_op jit(solution)/shard_map/jit(dynamic_index_in_dim)/squeeze | solution.py:416
  60.1 8.2 %collective-permute-done.10.refs_4_ = bf16[2,96,16,128]{3,2,1,0:T(8,128)(2,1)} collective-permute-done((bf16[2,96,16,128]{3,2,1,0:T(8,128)(2,1)S(1)}, bf16[2,96,16,128]{3,2,1,0:T(8,128)(2,1)}, u32[]{:S(2)}, u32[]{:S(2)}) %collective-permute-start.10) | collective-permute-done | bytes 786464 | tf_op jit(solution)/shard_map/ppermute | solution.py:417
  68.3 3.8 %collective-permute-done.9.refs_3_ = bf16[2,96,16,128]{3,2,1,0:T(8,128)(2,1)} collective-permute-done((bf16[2,96,16,128]{3,2,1,0:T(8,128)(2,1)S(1)}, bf16[2,96,16,128]{3,2,1,0:T(8,128)(2,1)}, u32[]{:S(2)}, u32[]{:S(2)}) %collective-permute-start.9) | collective-permute-done | bytes 786464 | tf_op jit(solution)/shard_map/ppermute | solution.py:417
  72.1 15.2 %stacks.1 = f32[401,64,128]{2,1,0:T(8,128)} custom-call(s32[24]{0:T(128)} %fusion.slots_ref, bf16[4,96,16,128]{3,2,1,0:T(8,128)(2,1)} %bitcast_dynamic-update-slice_fusion.refs_0_, bf16[4,96,16,128]{3,2,1,0:T(8,128)(2,1)} %copy-done.2, bf16[4,96,16,128]{3,2,1,0:T(8,128)(2,1)} %copy-done.1, bf16[2,96,16,128]{3,2,1,0:T(8,128)(2,1)} %collective-permute-done.9.refs_3_, ...), custom_call_target="tpu_custom_call" | custom-call | flops 20000000000 | bytes 25165824 | tf_op jit(solution)/shard_map/stacks/pallas_call | solution.py:389
  (15 shorter events, 0.3 us)
Async XLA Ops:
  6.6 11.0 %collective-permute-start = (bf16[96,16,128]{2,1,0:T(8,128)(2,1)}, bf16[96,16,128]{2,1,0:T(8,128)(2,1)S(1)}, u32[]{:S(2)}, u32[]{:S(2)}) collective-permute-start(bf16[96,16,128]{2,1,0:T(8,128)(2,1)} %get-tuple-element.16), channel_id=1, source_target_pairs={{0,4},{16,18},{2,6},{18,17},{1,5},{17,19},{3,7},{19,16},{4,8},{20,... | collective-permute-start | bytes 1179656 | tf_op jit(solution)/shard_map/ppermute | solution.py:417
  8.2 10.2 %collective-permute-start.1 = (bf16[96,16,128]{2,1,0:T(8,128)(2,1)}, bf16[96,16,128]{2,1,0:T(8,128)(2,1)S(1)}, u32[]{:S(2)}, u32[]{:S(2)}) collective-permute-start(bf16[96,16,128]{2,1,0:T(8,128)(2,1)} %get-tuple-element.16), channel_id=1, source_target_pairs={{0,12},{16,19},{2,14},{18,16},{1,13},{17,18},{3,15},{19,17},{4,0},... | collective-permute-start | bytes 1179656 | tf_op jit(solution)/shard_map/ppermute | solution.py:417
  9.8 19.4 %collective-permute-start.3 = (bf16[96,16,128]{2,1,0:T(8,128)(2,1)}, bf16[96,16,128]{2,1,0:T(8,128)(2,1)S(1)}, u32[]{:S(2)}, u32[]{:S(2)}) collective-permute-start(bf16[96,16,128]{2,1,0:T(8,128)(2,1)} %get-tuple-element.16), channel_id=1, source_target_pairs={{0,32},{16,18},{2,96},{18,50},{1,48},{17,114},{3,64},{19,2},{4,80}... | collective-permute-start | bytes 1179656 | tf_op jit(solution)/shard_map/ppermute | solution.py:417
  14.8 13.7 %collective-permute-start.2 = (bf16[96,16,128]{2,1,0:T(8,128)(2,1)}, bf16[96,16,128]{2,1,0:T(8,128)(2,1)S(1)}, u32[]{:S(2)}, u32[]{:S(2)}) collective-permute-start(bf16[96,16,128]{2,1,0:T(8,128)(2,1)} %get-tuple-element.16), channel_id=1, source_target_pairs={{0,8},{16,17},{2,10},{18,19},{1,9},{17,16},{3,11},{19,18},{4,12},{... | collective-permute-start | bytes 1179656 | tf_op jit(solution)/shard_map/ppermute | solution.py:417
  29.3 24.7 %collective-permute-start.5 = (bf16[4,96,16,128]{3,2,1,0:T(8,128)(2,1)}, bf16[4,96,16,128]{3,2,1,0:T(8,128)(2,1)S(1)}, u32[]{:S(2)}, u32[]{:S(2)}) collective-permute-start(bf16[4,96,16,128]{3,2,1,0:T(8,128)(2,1)} %bitcast_dynamic-update-slice_fusion.refs_0_), channel_id=1, source_target_pairs={{0,3},{16,28},{2,0},{18,30},{1,2},{17,29},{3,1},{19,31},{4,7},{20,... | collective-permute-start | bytes 4718600 | tf_op jit(solution)/shard_map/ppermute | solution.py:417
  32.1 21.9 %collective-permute-start.4 = (bf16[4,96,16,128]{3,2,1,0:T(8,128)(2,1)}, bf16[4,96,16,128]{3,2,1,0:T(8,128)(2,1)S(1)}, u32[]{:S(2)}, u32[]{:S(2)}) collective-permute-start(bf16[4,96,16,128]{3,2,1,0:T(8,128)(2,1)} %bitcast_dynamic-update-slice_fusion.refs_0_), channel_id=1, source_target_pairs={{0,2},{16,20},{2,1},{18,22},{1,3},{17,21},{3,0},{19,23},{4,6},{20,... | collective-permute-start | bytes 4718600 | tf_op jit(solution)/shard_map/ppermute | solution.py:417
  32.1 13.4 %collective-permute-start.8 = (bf16[96,16,128]{2,1,0:T(8,128)(2,1)S(1)}, bf16[96,16,128]{2,1,0:T(8,128)(2,1)S(1)}, u32[]{:S(2)}, u32[]{:S(2)}) collective-permute-start(bf16[96,16,128]{2,1,0:T(8,128)(2,1)S(1)} %collective-permute-done.3), channel_id=1, source_target_pairs={{0,64},{16,80},{2,66},{18,82},{1,65},{17,81},{3,67},{19,83},{4,68}... | collective-permute-start | bytes 1179656 | tf_op jit(solution)/shard_map/ppermute | solution.py:417
  32.1 20.0 %collective-permute-start.7 = (bf16[96,16,128]{2,1,0:T(8,128)(2,1)S(1)}, bf16[96,16,128]{2,1,0:T(8,128)(2,1)S(1)}, u32[]{:S(2)}, u32[]{:S(2)}) collective-permute-start(bf16[96,16,128]{2,1,0:T(8,128)(2,1)S(1)} %collective-permute-done.3), channel_id=1, source_target_pairs={{0,96},{16,112},{2,98},{18,114},{1,97},{17,113},{3,99},{19,115},{4... | collective-permute-start | bytes 1179656 | tf_op jit(solution)/shard_map/ppermute | solution.py:417
  36.1 17.9 %collective-permute-start.6 = (bf16[96,16,128]{2,1,0:T(8,128)(2,1)S(1)}, bf16[96,16,128]{2,1,0:T(8,128)(2,1)S(1)}, u32[]{:S(2)}, u32[]{:S(2)}) collective-permute-start(bf16[96,16,128]{2,1,0:T(8,128)(2,1)S(1)} %collective-permute-done.3), channel_id=1, source_target_pairs={{0,32},{16,48},{2,34},{18,50},{1,33},{17,49},{3,35},{19,51},{4,36}... | collective-permute-start | bytes 1179656 | tf_op jit(solution)/shard_map/ppermute | solution.py:417
  54.0 1.7 %copy-start.1 = (bf16[4,96,16,128]{3,2,1,0:T(8,128)(2,1)}, bf16[4,96,16,128]{3,2,1,0:T(8,128)(2,1)S(1)}, u32[]{:S(2)}) copy-start(bf16[4,96,16,128]{3,2,1,0:T(8,128)(2,1)S(1)} %collective-permute-done.5.refs_2_) | copy-start | bytes 4718596
  54.0 1.2 %copy-start.2 = (bf16[4,96,16,128]{3,2,1,0:T(8,128)(2,1)}, bf16[4,96,16,128]{3,2,1,0:T(8,128)(2,1)S(1)}, u32[]{:S(2)}) copy-start(bf16[4,96,16,128]{3,2,1,0:T(8,128)(2,1)S(1)} %collective-permute-done.4.refs_1_) | copy-start | bytes 4718596
  54.2 1.9 %copy-start = (bf16[4,96,16,128]{3,2,1,0:T(8,128)(2,1)}, bf16[4,96,16,128]{3,2,1,0:T(8,128)(2,1)S(1)}, u32[]{:S(2)}) copy-start(bf16[4,96,16,128]{3,2,1,0:T(8,128)(2,1)S(1)} %pad_maximum_fusion.refs_5_) | copy-start | bytes 4718596
  54.2 17.9 %collective-permute-start.11 = (bf16[4,96,16,128]{3,2,1,0:T(8,128)(2,1)S(1)}, bf16[4,96,16,128]{3,2,1,0:T(8,128)(2,1)}, u32[]{:S(2)}, u32[]{:S(2)}) collective-permute-start(bf16[4,96,16,128]{3,2,1,0:T(8,128)(2,1)S(1)} %pad_maximum_fusion.refs_5_), channel_id=1, source_target_pairs={{0,16},{16,0},{2,18},{18,2},{1,17},{17,1},{3,19},{19,3},{4,20},{20... | collective-permute-start | bytes 4718600 | tf_op jit(solution)/shard_map/ppermute | solution.py:417
  56.1 12.2 %collective-permute-start.10 = (bf16[2,96,16,128]{3,2,1,0:T(8,128)(2,1)S(1)}, bf16[2,96,16,128]{3,2,1,0:T(8,128)(2,1)}, u32[]{:S(2)}, u32[]{:S(2)}) collective-permute-start(bf16[2,96,16,128]{3,2,1,0:T(8,128)(2,1)S(1)} %slice.7), channel_id=1, source_target_pairs={{0,3},{16,28},{2,0},{18,30},{1,2},{17,29},{3,1},{19,31},{4,7},{20,... | collective-permute-start | bytes 2359304 | tf_op jit(solution)/shard_map/ppermute | solution.py:417
  58.8 13.3 %collective-permute-start.9 = (bf16[2,96,16,128]{3,2,1,0:T(8,128)(2,1)S(1)}, bf16[2,96,16,128]{3,2,1,0:T(8,128)(2,1)}, u32[]{:S(2)}, u32[]{:S(2)}) collective-permute-start(bf16[2,96,16,128]{3,2,1,0:T(8,128)(2,1)S(1)} %slice.6), channel_id=1, source_target_pairs={{0,2},{16,20},{2,1},{18,22},{1,3},{17,21},{3,0},{19,23},{4,6},{20,... | collective-permute-start | bytes 2359304 | tf_op jit(solution)/shard_map/ppermute | solution.py:417

commit v6 on v5

--- a/solution.py
+++ b/solution.py
@@ -421,9 +421,10 @@
     mine, second = lax.optimization_barrier((mine, second))
     up, down = send(mine, along_second(1)), send(mine, along_second(-1))
     seconds = [second] + [send(second, along_x(n)) for n in (1, -1, 2)]
-    up, down, *seconds = lax.optimization_barrier((up, down, *seconds))
+    up, down = lax.optimization_barrier((up, down))
+    far_up, far_down = send(up[:2], along_second(1)), send(down[2:], along_second(-1))
+    *seconds, up = lax.optimization_barrier((*seconds, up))
     seconds = jnp.stack(seconds)
-    far_up, far_down = send(up[:2], along_second(1)), send(down[2:], along_second(-1))
     others = send(seconds, other_core())
     sources = (mine, up, down, far_up, far_down, seconds, others)
     out = stacked(slots, sources, jnp.asarray(inverse_table()))

time: 87.6 us -> 87.6 us (level)
  no operation moved by 1% of the time
where the time goes in v6:
time: 87.6 us; the launch traced here: 86.6 us
  waiting for transfers between devices  39.3 us (45%)
  Pallas kernels  21.9 us (25%)
  starting transfers between devices  20.4 us (23%)
  local copies, waits for them, and re-layouts  4.83 us (6%)
    ppermute x12, waiting for transfers between devices, body(): send = lambda a, perm: lax.ppermute(a, AXES, perm)  39.3 us
    ppermute x12, starting transfers between devices, body(): send = lambda a, perm: lax.ppermute(a, AXES, perm)  20.4 us
    pallas_call x1, Pallas kernels, stacked(): pl.pallas_call(stack_kernel, grid_spec=pltpu.PrefetchScalarGridSpec(num_s...  15.2 us
    pallas_call x1, Pallas kernels, whitened(): pl.pallas_call(spectra_kernel, grid=(steps,), out_shape=[jax.ShapeDtypeSt...  6.6 us
    dynamic_update_slice x3, local copies, waits for them, and re-layouts, body(): lax.dynamic_update_slice(mine, send(own, along_first(n))[None], (k + 1, 0...  2.31 us
  transfers between devices with their start and end apart: 12, of which 6 were waited for; matrix products, arithmetic and copies ran while one was open for 4% of the time, Pallas kernels for 0%

profile of v6, /device:TPU:4, one launch (start us, length us, event | category | flops | bytes accessed | tf_op | source)
XLA Modules:
  0.0 86.6 jit_solution(1192365371616949553)
XLA Ops:
  0.0 6.6 %whitened_spectra.1 = (bf16[96,16,128]{2,1,0:T(8,128)(2,1)}, bf16[4,96,16,128]{3,2,1,0:T(8,128)(2,1)}) custom-call(s32[16]{0:T(128)} %alive_ref.1, f32[32,16,2000]{2,1,0:T(8,128)} %traces_ref.1, bf16[768,1024]{1,0:T(8,128)(2,1)} %constant.39.clone.table_ref, f32[192,2]{1,0:T(8,128)} %constant.40.clone.turn_ref, bf16[192,192]{1,0:T(8,128)(2,1)} %constant.41.clone.near_ref, ...), custom_call_target="tpu_custom_call" | custom-call | tf_op jit(solution)/shard_map/whitened_spectra/pallas_call | solution.py:264
  6.6 1.6 %collective-permute-start = (bf16[96,16,128]{2,1,0:T(8,128)(2,1)}, bf16[96,16,128]{2,1,0:T(8,128)(2,1)S(1)}, u32[]{:S(2)}, u32[]{:S(2)}) collective-permute-start(bf16[96,16,128]{2,1,0:T(8,128)(2,1)} %get-tuple-element.17), channel_id=1, source_target_pairs={{0,4},{16,18},{2,6},{18,17},{1,5},{17,19},{3,7},{19,16},{4,8},{20,... | collective-permute-start | bytes 1179656 | tf_op jit(solution)/shard_map/ppermute | solution.py:417
  8.2 1.7 %collective-permute-start.1 = (bf16[96,16,128]{2,1,0:T(8,128)(2,1)}, bf16[96,16,128]{2,1,0:T(8,128)(2,1)S(1)}, u32[]{:S(2)}, u32[]{:S(2)}) collective-permute-start(bf16[96,16,128]{2,1,0:T(8,128)(2,1)} %get-tuple-element.17), channel_id=1, source_target_pairs={{0,12},{16,19},{2,14},{18,16},{1,13},{17,18},{3,15},{19,17},{4,0},... | collective-permute-start | bytes 1179656 | tf_op jit(solution)/shard_map/ppermute | solution.py:417
  9.8 5.0 %collective-permute-start.3 = (bf16[96,16,128]{2,1,0:T(8,128)(2,1)}, bf16[96,16,128]{2,1,0:T(8,128)(2,1)S(1)}, u32[]{:S(2)}, u32[]{:S(2)}) collective-permute-start(bf16[96,16,128]{2,1,0:T(8,128)(2,1)} %get-tuple-element.17), channel_id=1, source_target_pairs={{0,32},{16,18},{2,96},{18,50},{1,48},{17,114},{3,64},{19,2},{4,80}... | collective-permute-start | bytes 1179656 | tf_op jit(solution)/shard_map/ppermute | solution.py:417
  14.8 2.8 %collective-permute-start.2 = (bf16[96,16,128]{2,1,0:T(8,128)(2,1)}, bf16[96,16,128]{2,1,0:T(8,128)(2,1)S(1)}, u32[]{:S(2)}, u32[]{:S(2)}) collective-permute-start(bf16[96,16,128]{2,1,0:T(8,128)(2,1)} %get-tuple-element.17), channel_id=1, source_target_pairs={{0,8},{16,17},{2,10},{18,19},{1,9},{17,16},{3,11},{19,18},{4,12},{... | collective-permute-start | bytes 1179656 | tf_op jit(solution)/shard_map/ppermute | solution.py:417
  17.6 0.8 bitcast_dynamic-update-slice_fusion.2
  18.4 0.8 bitcast_dynamic-update-slice_fusion.1
  19.2 9.3 %collective-permute-done.2 = bf16[96,16,128]{2,1,0:T(8,128)(2,1)S(1)} collective-permute-done((bf16[96,16,128]{2,1,0:T(8,128)(2,1)}, bf16[96,16,128]{2,1,0:T(8,128)(2,1)S(1)}, u32[]{:S(2)}, u32[]{:S(2)}) %collective-permute-start.2) | collective-permute-done | bytes 393248 | tf_op jit(solution)/shard_map/ppermute | solution.py:417
  28.5 0.8 bitcast_dynamic-update-slice_fusion.refs_0_
  29.3 2.8 %collective-permute-start.8 = (bf16[4,96,16,128]{3,2,1,0:T(8,128)(2,1)}, bf16[4,96,16,128]{3,2,1,0:T(8,128)(2,1)S(1)}, u32[]{:S(2)}, u32[]{:S(2)}) collective-permute-start(bf16[4,96,16,128]{3,2,1,0:T(8,128)(2,1)} %bitcast_dynamic-update-slice_fusion.refs_0_), channel_id=1, source_target_pairs={{0,3},{16,28},{2,0},{18,30},{1,2},{17,29},{3,1},{19,31},{4,7},{20,... | collective-permute-start | bytes 4718600 | tf_op jit(solution)/shard_map/ppermute | solution.py:417
  32.1 4.0 %collective-permute-start.5 = (bf16[96,16,128]{2,1,0:T(8,128)(2,1)S(1)}, bf16[96,16,128]{2,1,0:T(8,128)(2,1)S(1)}, u32[]{:S(2)}, u32[]{:S(2)}) collective-permute-start(bf16[96,16,128]{2,1,0:T(8,128)(2,1)S(1)} %collective-permute-done.3), channel_id=1, source_target_pairs={{0,96},{16,112},{2,98},{18,114},{1,97},{17,113},{3,99},{19,115},{4... | collective-permute-start | bytes 1179656 | tf_op jit(solution)/shard_map/ppermute | solution.py:417
  36.1 14.3 %collective-permute-done.8.refs_2_ = bf16[4,96,16,128]{3,2,1,0:T(8,128)(2,1)S(1)} collective-permute-done((bf16[4,96,16,128]{3,2,1,0:T(8,128)(2,1)}, bf16[4,96,16,128]{3,2,1,0:T(8,128)(2,1)S(1)}, u32[]{:S(2)}, u32[]{:S(2)}) %collective-permute-start.8) | collective-permute-done | bytes 1572896 | tf_op jit(solution)/shard_map/ppermute | solution.py:417
  50.3 3.6 %collective-permute-done.7.refs_1_ = bf16[4,96,16,128]{3,2,1,0:T(8,128)(2,1)S(1)} collective-permute-done((bf16[4,96,16,128]{3,2,1,0:T(8,128)(2,1)}, bf16[4,96,16,128]{3,2,1,0:T(8,128)(2,1)S(1)}, u32[]{:S(2)}, u32[]{:S(2)}) %collective-permute-start.7) | collective-permute-done | bytes 1572896 | tf_op jit(solution)/shard_map/ppermute | solution.py:417
  54.0 0.2 pad_maximum_fusion.refs_5_
  54.2 0.1 collective-permute-start.11
  54.3 0.7 copy-done.2
  55.1 0.1 slice.6
  55.2 0.1 slice.7
  55.4 0.2 copy-done
  55.6 2.5 %collective-permute-start.10 = (bf16[2,96,16,128]{3,2,1,0:T(8,128)(2,1)S(1)}, bf16[2,96,16,128]{3,2,1,0:T(8,128)(2,1)}, u32[]{:S(2)}, u32[]{:S(2)}) collective-permute-start(bf16[2,96,16,128]{3,2,1,0:T(8,128)(2,1)S(1)} %slice.7), channel_id=1, source_target_pairs={{0,3},{16,28},{2,0},{18,30},{1,2},{17,29},{3,1},{19,31},{4,7},{20,... | collective-permute-start | bytes 2359304 | tf_op jit(solution)/shard_map/ppermute | solution.py:417
  58.0 1.3 %fusion.slots_ref = s32[24]{0:T(128)} fusion(s32[128,24]{1,0:T(8,128)} %constant.43.clone, s32[]{:T(128)S(6)} %select_n.4), kind=kLoop, calls=%fused_computation.5 | loop fusion | bytes 196 | tf_op jit(solution)/shard_map/jit(dynamic_index_in_dim)/squeeze | solution.py:416
  59.3 8.3 %collective-permute-done.10.refs_4_ = bf16[2,96,16,128]{3,2,1,0:T(8,128)(2,1)} collective-permute-done((bf16[2,96,16,128]{3,2,1,0:T(8,128)(2,1)S(1)}, bf16[2,96,16,128]{3,2,1,0:T(8,128)(2,1)}, u32[]{:S(2)}, u32[]{:S(2)}) %collective-permute-start.10) | collective-permute-done | bytes 786464 | tf_op jit(solution)/shard_map/ppermute | solution.py:417
  67.7 3.7 %collective-permute-done.9.refs_3_ = bf16[2,96,16,128]{3,2,1,0:T(8,128)(2,1)} collective-permute-done((bf16[2,96,16,128]{3,2,1,0:T(8,128)(2,1)S(1)}, bf16[2,96,16,128]{3,2,1,0:T(8,128)(2,1)}, u32[]{:S(2)}, u32[]{:S(2)}) %collective-permute-start.9) | collective-permute-done | bytes 786464 | tf_op jit(solution)/shard_map/ppermute | solution.py:417
  71.3 15.2 %stacks.1 = f32[401,64,128]{2,1,0:T(8,128)} custom-call(s32[24]{0:T(128)} %fusion.slots_ref, bf16[4,96,16,128]{3,2,1,0:T(8,128)(2,1)} %bitcast_dynamic-update-slice_fusion.refs_0_, bf16[4,96,16,128]{3,2,1,0:T(8,128)(2,1)} %copy-done.2, bf16[4,96,16,128]{3,2,1,0:T(8,128)(2,1)} %copy-done.1, bf16[2,96,16,128]{3,2,1,0:T(8,128)(2,1)} %collective-permute-done.9.refs_3_, ...), custom_call_target="tpu_custom_call" | custom-call | flops 20000000000 | bytes 25165824 | tf_op jit(solution)/shard_map/stacks/pallas_call | solution.py:389
  (15 shorter events, 0.1 us)
Async XLA Ops:
  6.6 11.0 %collective-permute-start = (bf16[96,16,128]{2,1,0:T(8,128)(2,1)}, bf16[96,16,128]{2,1,0:T(8,128)(2,1)S(1)}, u32[]{:S(2)}, u32[]{:S(2)}) collective-permute-start(bf16[96,16,128]{2,1,0:T(8,128)(2,1)} %get-tuple-element.17), channel_id=1, source_target_pairs={{0,4},{16,18},{2,6},{18,17},{1,5},{17,19},{3,7},{19,16},{4,8},{20,... | collective-permute-start | bytes 1179656 | tf_op jit(solution)/shard_map/ppermute | solution.py:417
  8.2 10.2 %collective-permute-start.1 = (bf16[96,16,128]{2,1,0:T(8,128)(2,1)}, bf16[96,16,128]{2,1,0:T(8,128)(2,1)S(1)}, u32[]{:S(2)}, u32[]{:S(2)}) collective-permute-start(bf16[96,16,128]{2,1,0:T(8,128)(2,1)} %get-tuple-element.17), channel_id=1, source_target_pairs={{0,12},{16,19},{2,14},{18,16},{1,13},{17,18},{3,15},{19,17},{4,0},... | collective-permute-start | bytes 1179656 | tf_op jit(solution)/shard_map/ppermute | solution.py:417
  9.8 19.4 %collective-permute-start.3 = (bf16[96,16,128]{2,1,0:T(8,128)(2,1)}, bf16[96,16,128]{2,1,0:T(8,128)(2,1)S(1)}, u32[]{:S(2)}, u32[]{:S(2)}) collective-permute-start(bf16[96,16,128]{2,1,0:T(8,128)(2,1)} %get-tuple-element.17), channel_id=1, source_target_pairs={{0,32},{16,18},{2,96},{18,50},{1,48},{17,114},{3,64},{19,2},{4,80}... | collective-permute-start | bytes 1179656 | tf_op jit(solution)/shard_map/ppermute | solution.py:417
  14.8 13.7 %collective-permute-start.2 = (bf16[96,16,128]{2,1,0:T(8,128)(2,1)}, bf16[96,16,128]{2,1,0:T(8,128)(2,1)S(1)}, u32[]{:S(2)}, u32[]{:S(2)}) collective-permute-start(bf16[96,16,128]{2,1,0:T(8,128)(2,1)} %get-tuple-element.17), channel_id=1, source_target_pairs={{0,8},{16,17},{2,10},{18,19},{1,9},{17,16},{3,11},{19,18},{4,12},{... | collective-permute-start | bytes 1179656 | tf_op jit(solution)/shard_map/ppermute | solution.py:417
  29.3 21.0 %collective-permute-start.8 = (bf16[4,96,16,128]{3,2,1,0:T(8,128)(2,1)}, bf16[4,96,16,128]{3,2,1,0:T(8,128)(2,1)S(1)}, u32[]{:S(2)}, u32[]{:S(2)}) collective-permute-start(bf16[4,96,16,128]{3,2,1,0:T(8,128)(2,1)} %bitcast_dynamic-update-slice_fusion.refs_0_), channel_id=1, source_target_pairs={{0,3},{16,28},{2,0},{18,30},{1,2},{17,29},{3,1},{19,31},{4,7},{20,... | collective-permute-start | bytes 4718600 | tf_op jit(solution)/shard_map/ppermute | solution.py:417
  32.1 21.8 %collective-permute-start.7 = (bf16[4,96,16,128]{3,2,1,0:T(8,128)(2,1)}, bf16[4,96,16,128]{3,2,1,0:T(8,128)(2,1)S(1)}, u32[]{:S(2)}, u32[]{:S(2)}) collective-permute-start(bf16[4,96,16,128]{3,2,1,0:T(8,128)(2,1)} %bitcast_dynamic-update-slice_fusion.refs_0_), channel_id=1, source_target_pairs={{0,2},{16,20},{2,1},{18,22},{1,3},{17,21},{3,0},{19,23},{4,6},{20,... | collective-permute-start | bytes 4718600 | tf_op jit(solution)/shard_map/ppermute | solution.py:417
  32.1 21.8 %collective-permute-start.6 = (bf16[96,16,128]{2,1,0:T(8,128)(2,1)S(1)}, bf16[96,16,128]{2,1,0:T(8,128)(2,1)S(1)}, u32[]{:S(2)}, u32[]{:S(2)}) collective-permute-start(bf16[96,16,128]{2,1,0:T(8,128)(2,1)S(1)} %collective-permute-done.3), channel_id=1, source_target_pairs={{0,64},{16,80},{2,66},{18,82},{1,65},{17,81},{3,67},{19,83},{4,68}... | collective-permute-start | bytes 1179656 | tf_op jit(solution)/shard_map/ppermute | solution.py:417
  32.1 21.8 %collective-permute-start.5 = (bf16[96,16,128]{2,1,0:T(8,128)(2,1)S(1)}, bf16[96,16,128]{2,1,0:T(8,128)(2,1)S(1)}, u32[]{:S(2)}, u32[]{:S(2)}) collective-permute-start(bf16[96,16,128]{2,1,0:T(8,128)(2,1)S(1)} %collective-permute-done.3), channel_id=1, source_target_pairs={{0,96},{16,112},{2,98},{18,114},{1,97},{17,113},{3,99},{19,115},{4... | collective-permute-start | bytes 1179656 | tf_op jit(solution)/shard_map/ppermute | solution.py:417
  36.1 17.9 %collective-permute-start.4 = (bf16[96,16,128]{2,1,0:T(8,128)(2,1)S(1)}, bf16[96,16,128]{2,1,0:T(8,128)(2,1)S(1)}, u32[]{:S(2)}, u32[]{:S(2)}) collective-permute-start(bf16[96,16,128]{2,1,0:T(8,128)(2,1)S(1)} %collective-permute-done.3), channel_id=1, source_target_pairs={{0,32},{16,48},{2,34},{18,50},{1,33},{17,49},{3,35},{19,51},{4,36}... | collective-permute-start | bytes 1179656 | tf_op jit(solution)/shard_map/ppermute | solution.py:417
  50.3 4.9 %copy-start.1 = (bf16[4,96,16,128]{3,2,1,0:T(8,128)(2,1)}, bf16[4,96,16,128]{3,2,1,0:T(8,128)(2,1)S(1)}, u32[]{:S(2)}) copy-start(bf16[4,96,16,128]{3,2,1,0:T(8,128)(2,1)S(1)} %collective-permute-done.8.refs_2_) | copy-start | bytes 4718596
  53.9 1.2 %copy-start.2 = (bf16[4,96,16,128]{3,2,1,0:T(8,128)(2,1)}, bf16[4,96,16,128]{3,2,1,0:T(8,128)(2,1)S(1)}, u32[]{:S(2)}) copy-start(bf16[4,96,16,128]{3,2,1,0:T(8,128)(2,1)S(1)} %collective-permute-done.7.refs_1_) | copy-start | bytes 4718596
  54.2 1.4 %copy-start = (bf16[4,96,16,128]{3,2,1,0:T(8,128)(2,1)}, bf16[4,96,16,128]{3,2,1,0:T(8,128)(2,1)S(1)}, u32[]{:S(2)}) copy-start(bf16[4,96,16,128]{3,2,1,0:T(8,128)(2,1)S(1)} %pad_maximum_fusion.refs_5_) | copy-start | bytes 4718596
  54.2 17.1 %collective-permute-start.11 = (bf16[4,96,16,128]{3,2,1,0:T(8,128)(2,1)S(1)}, bf16[4,96,16,128]{3,2,1,0:T(8,128)(2,1)}, u32[]{:S(2)}, u32[]{:S(2)}) collective-permute-start(bf16[4,96,16,128]{3,2,1,0:T(8,128)(2,1)S(1)} %pad_maximum_fusion.refs_5_), channel_id=1, source_target_pairs={{0,16},{16,0},{2,18},{18,2},{1,17},{17,1},{3,19},{19,3},{4,20},{20... | collective-permute-start | bytes 4718600 | tf_op jit(solution)/shard_map/ppermute | solution.py:417
  55.6 12.1 %collective-permute-start.10 = (bf16[2,96,16,128]{3,2,1,0:T(8,128)(2,1)S(1)}, bf16[2,96,16,128]{3,2,1,0:T(8,128)(2,1)}, u32[]{:S(2)}, u32[]{:S(2)}) collective-permute-start(bf16[2,96,16,128]{3,2,1,0:T(8,128)(2,1)S(1)} %slice.7), channel_id=1, source_target_pairs={{0,3},{16,28},{2,0},{18,30},{1,2},{17,29},{3,1},{19,31},{4,7},{20,... | collective-permute-start | bytes 2359304 | tf_op jit(solution)/shard_map/ppermute | solution.py:417
  58.0 13.3 %collective-permute-start.9 = (bf16[2,96,16,128]{3,2,1,0:T(8,128)(2,1)S(1)}, bf16[2,96,16,128]{3,2,1,0:T(8,128)(2,1)}, u32[]{:S(2)}, u32[]{:S(2)}) collective-permute-start(bf16[2,96,16,128]{3,2,1,0:T(8,128)(2,1)S(1)} %slice.6), channel_id=1, source_target_pairs={{0,2},{16,20},{2,1},{18,22},{1,3},{17,21},{3,0},{19,23},{4,6},{20,... | collective-permute-start | bytes 2359304 | tf_op jit(solution)/shard_map/ppermute | solution.py:417
